TPU v7x, 256 devices: a whole 4x4x8 slice. The times are simulated.
256 devices in a mesh: dp: 16 (over y_lo, x, core), ref: 16 (over z, y_hi).
Axes of the slice: x: 4, y: 4 (y_hi: 2, y_lo: 2; y = y_hi * 2 + y_lo), z: 8, core: 2. Of those that a mesh axis runs over, the one named last changes fastest.
Arguments:
- images: bfloat16 [12288, 16384], P(('dp', 'ref'))
- ctf: bfloat16 [12288, 8192], P(('dp', 'ref'))
- refs: bfloat16 [192, 16384], P('ref')
- shifts: int32 [9, 2], replicated, may hold values from -3 to 3
- lists: int32 [12288, 12], P(('dp', 'ref')), may hold values from 0 to 191, as said below
- counts: int32 [12288], P(('dp', 'ref')), may hold values from 1 to 12
Outputs:
- sums: float32 [192, 16384], P('ref', 'dp')
- totals: float32 [192], P('ref')
- log_evidence: float32 [12288], P(('dp', 'ref'))
Inputs may be any that keep to these rules, and one draw needn't show every extreme that they name: Row p of lists holds 12 distinct orientation indices, clustered near one orientation; only its first counts[p] entries are used.
All inputs are finite; a program needn't handle non-finite values.
Results may differ from a plain program's by a relative error of at most 0.0045.
Values may be sent and summed in bfloat16 or wider, within the bound.
No kernel may reach another device: no remote copies, remote signals or barrier semaphores. Data moves between devices by JAX's collectives and lax.ppermute only.
A program may use at most 128 MiB of HBM per device.

v0:
```python
import math

import jax
import jax.numpy as jnp
from jax import lax
from jax.experimental import pallas as pl
from jax.experimental.pallas import tpu as pltpu
from jax.sharding import Mesh, PartitionSpec as P

GRID = 128
BLOCK = 1024
SIDE = BLOCK // 2
LANES = 128
GROUPS = SIDE // LANES
HALF = 48
CHUNK = 256
STACKED = (0, 4, 2, 6, 1, 5, 3, 7)
CHIPS = ("z", "y_hi", "y_lo", "x")
EVERYONE = ("y_lo", "x", "core", "z", "y_hi")
SMEM = pl.BlockSpec(memory_space=pltpu.SMEM)
VMEM = pl.BlockSpec(memory_space=pltpu.VMEM)
ANY = pl.BlockSpec(memory_space=pl.ANY)


def over_z(value, bits):
    return lax.ppermute(value, "z", [(i, i ^ bits) for i in range(8)])


def over(value, bits, core_on_x):
    pairs = []
    for y_lo in range(2):
        for x in range(4):
            for core in range(2):
                for y_hi in range(2):
                    here = ((y_lo * 4 + x) * 2 + core) * 2 + y_hi
                    if core == core_on_x:
                        there = ((y_lo * 4 + (x ^ bits)) * 2 + core) * 2 + y_hi
                    else:
                        there = (((y_lo ^ (bits & 1)) * 4 + x) * 2 + core) * 2 + (y_hi ^ (bits >> 1))
                    pairs.append((here, there))
    return lax.ppermute(value, ("y_lo", "x", "core", "y_hi"), pairs)


def pack_kernel(column_ref, core_ref, refs_ref, out_ref):
    for p in range(2):
        start = pl.multiple_of((2 * column_ref[0] + p) * BLOCK + core_ref[0] * SIDE, SIDE)
        block = refs_ref[:, pl.ds(start, SIDE)].astype(jnp.float32)
        tiles = [block[0:8, g * LANES : (g + 1) * LANES] for g in range(GROUPS)]
        tiles += [block[8:12, g * LANES : (g + 1) * LANES] for g in range(GROUPS)]
        out_ref[0, p] = jnp.concatenate(tiles, axis=0).astype(jnp.bfloat16)


def stack_kernel(*args):
    out_ref = args[-1]
    row = 0
    for ref in args[:-1]:
        count = ref.shape[0]
        out_ref[row : row + count] = ref[...]
        row += count


def join_kernel(own_ref, one_ref, two_ref, three_ref, rot_ref, low_ref, high_ref):
    low_ref[0] = own_ref[...]
    low_ref[1] = one_ref[...]
    high_ref[0] = two_ref[...]
    high_ref[1] = three_ref[...]


def weighted_kernel(core_ref, x_ref, images_ref, ctf_ref, packed_ref, own_ref, other_ref):
    core, x = core_ref[0], x_ref[0]
    for out_ref, side in ((own_ref, core), (other_ref, 1 - core)):
        for xr in range(4):
            for p in range(2):
                column = pl.multiple_of((2 * (x ^ xr) + p) * BLOCK + side * SIDE, SIDE)
                gain = ctf_ref[:, pl.ds(column, SIDE)].astype(jnp.float32)
                for part in range(2):
                    start = pl.multiple_of(part * 8 * BLOCK + column, SIDE)
                    values = images_ref[:, pl.ds(start, SIDE)].astype(jnp.float32)
                    out_ref[part, xr, :, p * SIDE : (p + 1) * SIDE] = (gain * values).astype(
                        jnp.bfloat16
                    )


def rotate_chunk(core, x, shifts_ref, own_ref, recv_ref, xr, start, tables, put):
    rows = own_ref.shape[2]
    trans = shifts_ref.shape[0]
    half = GRID // 2
    cos_ref, sin_ref = tables
    lanes = pl.ds(start, CHUNK)
    pixel = (2 * (x ^ xr) + start // SIDE) * BLOCK + core * SIDE + start % SIDE
    pixel = pixel + lax.broadcasted_iota(jnp.int32, (trans, CHUNK), 1)
    freq_y = (((pixel >> 6) + half) & (GRID - 1)) - half
    turns = (pixel & (half - 1)) * shifts_ref[:, 0:1] + freq_y * shifts_ref[:, 1:2]
    angle = (turns & (GRID - 1)).astype(jnp.float32) * jnp.float32(2.0 * math.pi / GRID)
    cos_ref[...] = jnp.cos(angle)
    sin_ref[...] = jnp.sin(angle)
    for h, half_ref in enumerate((own_ref, recv_ref)):
        re = half_ref[0, xr, :, lanes].astype(jnp.float32)
        im = half_ref[1, xr, :, lanes].astype(jnp.float32)
        for t in range(trans):
            cosine, sine = cos_ref[t : t + 1, :], sin_ref[t : t + 1, :]
            base = (h * trans + t) * rows
            put(0, base, rows, (re * cosine + im * sine).astype(jnp.bfloat16))
            put(1, base, rows, (im * cosine - re * sine).astype(jnp.bfloat16))


def rotate_kernel(
    core_ref, x_ref, part_ref, shifts_ref, own_ref, recv_ref, rot_ref, cos_ref, sin_ref
):
    first = part_ref[0]
    steps = BLOCK // CHUNK

    def step(index, carry):
        xr = index // steps
        start = pl.multiple_of((index % steps) * CHUNK, CHUNK)

        def put(part, base, rows, value):
            rot_ref[part ^ first, xr, base : base + rows, pl.ds(start, CHUNK)] = value

        rotate_chunk(
            core_ref[0], x_ref[0], shifts_ref, own_ref, recv_ref, xr, start, (cos_ref, sin_ref), put
        )
        return carry

    lax.fori_loop(0, 4 * steps, step, 0)


def low_rows():
    return lax.broadcasted_iota(jnp.int32, (8, LANES), 0) < 4


def spread(own, other, wide_ref, row, column):
    low = low_rows()
    for g in range(GROUPS):
        lanes = slice(column + g * LANES, column + (g + 1) * LANES)
        wide_ref[row : row + 8, lanes] = own[8 * g : 8 * g + 8]
        wide_ref[row + 8 : row + 16, lanes] = other[8 * g : 8 * g + 8]
    for j in range(GROUPS // 2):
        at = 8 * (GROUPS + j)
        a, b = own[at : at + 8], other[at : at + 8]
        start = column + 2 * j * LANES
        wide_ref[row + 16 : row + 24, start : start + LANES] = jnp.where(low, a, pltpu.roll(b, 4, 0))
        start = start + LANES
        wide_ref[row + 16 : row + 24, start : start + LANES] = jnp.where(low, pltpu.roll(a, 4, 0), b)


def forward_kernel(*args):
    core_ref, blocks, (rot_ref, out_ref, wide_ref) = args[0], args[1:9], args[9:]
    first = core_ref[0] == 0

    def block(n, m, k):
        return blocks[2 * n + m // 2][m % 2, STACKED[k]].astype(jnp.float32)

    for b in range(2):
        for xr in range(4):
            wide = wide_ref.at[xr % 2]
            for k in range(8):
                pair = []
                for a in range(2):
                    y = 2 * a + b
                    value = block(xr, y, k)
                    if y != xr:
                        value = jnp.where(first, value, block(y, xr, k))
                    pair.append(value)
                for p in range(2):
                    spread(pair[0][p], pair[1][p], wide, 24 * k, p * SIDE)
            product = lax.dot_general(
                rot_ref[b, xr],
                wide[...].astype(jnp.bfloat16),
                (((1,), (1,)), ((), ())),
                preferred_element_type=jnp.float32,
            )
            count = product.shape[1]
            if b == 0 and xr == 0:
                out_ref[:, :count] = product
                out_ref[:, count:] = jnp.zeros(
                    (product.shape[0], out_ref.shape[1] - count), jnp.float32
                )
            else:
                out_ref[:, :count] += product


def orientation(position, z, y_hi):
    k = jnp.zeros_like(position)
    for step in range(1, 8):
        k = k + (position >= 24 * step).astype(jnp.int32)
    place = position - 24 * k
    tail = (place >= 16).astype(jnp.int32)
    late = place - 16 * tail
    a = jnp.where(tail == 1, (late >= 4).astype(jnp.int32), (late >= 8).astype(jnp.int32))
    row = jnp.where(tail == 1, 8 + late - 4 * a, late - 8 * a)
    return ((z ^ k) * 2 + (y_hi ^ a)) * 12 + row


def softmax(scale, z, y_hi, mine_ref, theirs_ref, lists_ref, weights_ref, evidence_ref):
    particles, slots = lists_ref.shape[1:]
    refs_all = weights_ref.shape[1]
    trans = mine_ref.shape[0] // (2 * particles)
    shares = []
    index = orientation(lax.broadcasted_iota(jnp.int32, (8, refs_all), 1), z, y_hi)
    index = jnp.concatenate([index] * (particles // 8), axis=0)
    for h in range(2):
        listed = index == lists_ref[h, :, 0:1]
        for slot in range(1, slots):
            listed = listed | (index == lists_ref[h, :, slot : slot + 1])
        scores = []
        for t in range(trans):
            a = (h * trans + t) * particles
            b = ((1 - h) * trans + t) * particles
            value = mine_ref[a : a + particles, :refs_all] + theirs_ref[b : b + particles, :refs_all]
            scores.append(jnp.where(listed, value * scale, -jnp.inf))
        top = scores[0]
        for value in scores[1:]:
            top = jnp.maximum(top, value)
        top = jnp.max(top, axis=1, keepdims=True)
        exps = [jnp.exp(value - top) for value in scores]
        norm = exps[0]
        for value in exps[1:]:
            norm = norm + value
        summed = jnp.sum(norm, axis=1, keepdims=True)
        inverse = 1.0 / summed
        for t in range(trans):
            a = (h * trans + t) * particles
            weights_ref[a : a + particles] = exps[t] * inverse
        if h == 0:
            evidence_ref[...] = top + jnp.log(summed)
        shares.append(jnp.sum(norm * inverse, axis=0, keepdims=True))
    weights_ref[2 * trans * particles :] = jnp.broadcast_to(shares[0] + shares[1], (8, refs_all))


def backward_kernel(scale, *args):
    core_ref, x_ref, y_lo_ref, z_ref, y_hi_ref, mine_ref, theirs_ref, lists_ref = args[:8]
    shifts_ref, own_ref, recv_ref = args[8:11]
    stays, far_low, far_high, one_low, one_high, three_low, three_high = args[11:18]
    evidence_ref, totals_ref, weights_ref, rot_ref, sums_ref, cos_ref, sin_ref = args[18:]
    core, x, y_lo, z, y_hi = core_ref[0], x_ref[0], y_lo_ref[0], z_ref[0], y_hi_ref[0]
    softmax(scale, z, y_hi, mine_ref, theirs_ref, lists_ref, weights_ref, evidence_ref)
    flipped = weights_ref[...].T
    refs_all, rows = flipped.shape[0], flipped.shape[1] - 8
    index = orientation(lax.broadcasted_iota(jnp.int32, (refs_all, 1), 0), z, y_hi)
    column = lax.broadcasted_iota(jnp.int32, (refs_all, refs_all), 1)
    totals = jnp.where(index == column, flipped[:, rows : rows + 1], 0.0)
    totals = jnp.sum(totals, axis=0, keepdims=True)
    totals_ref[...] = jnp.zeros(totals_ref.shape, jnp.float32)
    totals_ref[0:1, :] = totals[:, :LANES]
    totals_ref[1:2, : refs_all - LANES] = totals[:, LANES:]
    weights = flipped[:, :rows].astype(jnp.bfloat16)
    low = low_rows()

    def step(at, carry):
        xr, p = at // 2, at % 2
        for c in range(SIDE // CHUNK):
            start = pl.multiple_of(p * SIDE + c * CHUNK, CHUNK)

            def put(part, base, rows, value):
                rot_ref[c, part, base : base + rows, :] = value

            tables = cos_ref.at[c], sin_ref.at[c]
            rotate_chunk(core, x, shifts_ref, own_ref, recv_ref, xr, start, tables, put)
            for part in range(2):
                product = lax.dot_general(
                    weights,
                    rot_ref[c, part],
                    (((1,), (0,)), ((), ())),
                    preferred_element_type=jnp.float32,
                )
                for a in range(2):
                    y = 2 * a + (part ^ y_lo)
                    i, j = jnp.where(core == 0, xr, y), jnp.where(core == 0, y, xr)
                    for k in range(8):
                        row = 24 * k
                        ref = sums_ref.at[i, j, k, p]
                        for g in range(2):
                            to = 8 * (2 * c + g)
                            ref[to : to + 8] = product[
                                row + 8 * a : row + 8 * a + 8, g * LANES : (g + 1) * LANES
                            ]
                        one = product[row + 16 : row + 24, :LANES]
                        two = product[row + 16 : row + 24, LANES:]
                        if a == 0:
                            tail = jnp.where(low, one, pltpu.roll(two, 4, 0))
                        else:
                            tail = jnp.where(low, pltpu.roll(one, 4, 0), two)
                        to = 8 * (GROUPS + c)
                        ref[to : to + 8] = tail
        return carry

    lax.fori_loop(0, 8, step, 0)
    for place in range(4):
        stays[place] = sums_ref[0, place]
        for distance, low_ref, high_ref in (
            (2, far_low, far_high),
            (1, one_low, one_high),
            (3, three_low, three_high),
        ):
            low_ref[place] = sums_ref[distance, place, 0:4].astype(low_ref.dtype)
            high_ref[place] = sums_ref[distance, place, 4:8].astype(high_ref.dtype)


def add_kernel(one_ref, one_more_ref, three_ref, three_more_ref, one_out, three_out):
    one_out[...] = (one_ref[...] + one_more_ref[...].astype(jnp.float32)).astype(jnp.bfloat16)
    three_out[...] = (three_ref[...] + three_more_ref[...].astype(jnp.float32)).astype(jnp.bfloat16)


def middle_kernel(stays, one_low, one_high, three_low, three_high, *outs):
    for n, out_ref in enumerate(outs):
        for ks, one, three in ((0, one_low, three_low), (4, one_high, three_high)):
            total = stays[n, ks : ks + 4] + one[n].astype(jnp.float32)
            total = total + three[n].astype(jnp.float32)
            out_ref[ks : ks + 4] = total.astype(out_ref.dtype)


def late_kernel(stays, one, two, three, even_ref, odd_ref):
    for k in range(8):
        total = stays[k] + one[k].astype(jnp.float32)
        total = total + (two[k].astype(jnp.float32) + three[k].astype(jnp.float32))
        if k % 2 == 0:
            even_ref[k // 2] = total
        else:
            odd_ref[k // 2] = total.astype(odd_ref.dtype)


def halve_kernel(stays, came, even_ref, odd_ref):
    for k in range(stays.shape[0]):
        total = stays[k] + came[k].astype(jnp.float32)
        if k % 2 == 0:
            even_ref[k // 2] = total
        else:
            odd_ref[k // 2] = total


def deal_kernel(core_ref, stays, came, mine_ref, give_ref):
    first = core_ref[0] == 0
    low, high = stays[0, 0] + came[0, 0], stays[0, 1] + came[0, 1]
    mine_ref[...] = jnp.where(first, low, high)
    give_ref[...] = jnp.where(first, high, low)


def last_kernel(core_ref, mine_ref, came_ref, out_ref):
    first = core_ref[0] == 0
    low = jnp.where(first, mine_ref[...], came_ref[...])
    high = jnp.where(first, came_ref[...], mine_ref[...])
    for side, block in enumerate((low, high)):
        for g in range(GROUPS):
            start = side * SIDE + g * LANES
            out_ref[0:8, start : start + LANES] = block[8 * g : 8 * g + 8]
            at = 8 * GROUPS + 4 * g
            out_ref[8:12, start : start + LANES] = block[at : at + 4]


def totals_kernel(ref_ref, all_ref, out_ref):
    total = jnp.sum(all_ref[...], axis=0)
    row = jnp.concatenate([total[0:1], total[1:2]], axis=1)
    row = jnp.broadcast_to(row, (8, 2 * LANES))
    row = pltpu.roll(row, (2 * LANES - 12 * ref_ref[0]) % (2 * LANES), 1)
    out_ref[...] = row[0:1, :LANES]


def call(name, kernel, ins, outs, specs=None, scratch=(), mebibytes=16, micros=1):
    single = not isinstance(outs, (list, tuple))
    return pl.pallas_call(
        kernel,
        out_shape=outs,
        in_specs=specs or [VMEM] * len(ins),
        out_specs=VMEM if single else [VMEM] * len(outs),
        scratch_shapes=list(scratch),
        compiler_params=pltpu.CompilerParams(vmem_limit_bytes=mebibytes * 1024 * 1024),
        cost_estimate=pl.CostEstimate(
            flops=micros * 1000000, bytes_accessed=micros * 3000000, transcendentals=0
        ),
        name=name,
    )(*ins)


def shape(*dims, dtype=jnp.bfloat16):
    return jax.ShapeDtypeStruct(dims, dtype)


def scalar(value):
    return jnp.full((1,), value, jnp.int32)


def local(images, ctf, refs, shifts, lists, counts):
    f32, bf16 = jnp.float32, jnp.bfloat16
    parts, rdev, trans = images.shape[0], refs.shape[0], shifts.shape[0]
    refs_all = rdev * 16
    rows = 2 * trans * parts
    swap = [(0, 1), (1, 0)]
    core, x, y_lo = lax.axis_index("core"), lax.axis_index("x"), lax.axis_index("y_lo")
    z, y_hi = scalar(lax.axis_index("z")), scalar(lax.axis_index("y_hi"))
    ref = scalar(lax.axis_index(("z", "y_hi")))
    column = scalar(y_lo * 4 + x)
    core, x, y_lo = scalar(core), scalar(x), scalar(y_lo)

    mine = call(
        "pack", pack_kernel, [column, core, refs], shape(1, 2, HALF, LANES), [SMEM, SMEM, VMEM]
    )
    half = shape(2, 4, parts, BLOCK)
    own, other = call(
        "weighted",
        weighted_kernel,
        [core, x, images, ctf, mine],
        [half, half],
        [SMEM, SMEM, VMEM, VMEM, ANY],
    )
    recv = lax.ppermute(other, "core", swap)
    slot = jnp.arange(lists.shape[1], dtype=jnp.int32)[None, :]
    used = jnp.where(slot < counts[:, None], lists, -1)
    used_pair = jnp.stack([used, lax.ppermute(used, "core", swap)])
    tables = [pltpu.VMEM((trans, CHUNK), f32)] * 2
    rot = call(
        "rotate",
        rotate_kernel,
        [core, x, y_lo, shifts, own, recv],
        shape(2, 4, rows, BLOCK),
        [SMEM] * 3 + [VMEM] * 3,
        tables,
        8,
        6,
    )

    blocks = mine
    for bits in (4, 2, 1):
        came = over_z(blocks, bits)
        blocks = call(
            "stack", stack_kernel, [blocks, came], shape(2 * blocks.shape[0], 2, HALF, LANES)
        )
    fours = [blocks] + [over(blocks, m, 1) for m in (1, 2, 3)]
    low, high = call(
        "join", join_kernel, fours + [rot], [shape(2, 8, 2, HALF, LANES)] * 2, [VMEM] * 4 + [ANY]
    )
    one_low, three_high = over(low, 1, 0), over(high, 3, 0)
    one_high, three_low = over(high, 1, 0), over(low, 3, 0)
    two_low, two_high = over(one_low, 3, 0), over(three_high, 1, 0)
    lanes = -(-refs_all // LANES) * LANES
    scores = call(
        "forward",
        forward_kernel,
        [core, low, high, one_low, one_high, two_low, two_high, three_low, three_high, rot],
        shape(rows, lanes, dtype=f32),
        [SMEM] + [VMEM] * 9,
        [pltpu.VMEM((2, refs_all, BLOCK), f32)],
        16,
        4,
    )
    theirs = lax.ppermute(scores, "core", swap)

    scale = (2 * ctf.shape[1]) ** -0.5
    part16, part32 = shape(4, 4, 2, HALF, LANES), shape(4, 4, 2, HALF, LANES, dtype=f32)
    stays, far_low, far_high, one_low, one_high, three_low, three_high, evidence, totals = call(
        "backward",
        lambda *args: backward_kernel(scale, *args),
        [core, x, y_lo, z, y_hi, scores, theirs, used_pair, shifts, own, recv],
        [shape(4, 8, 2, HALF, LANES, dtype=f32), part16, part16, part16, part32, part32, part16]
        + [shape(parts, 1, dtype=f32), shape(8, LANES, dtype=f32)],
        [SMEM] * 5 + [VMEM] * 6,
        [
            pltpu.VMEM((rows + 8, refs_all), f32),
            pltpu.VMEM((2, 2, rows, CHUNK), bf16),
            pltpu.VMEM((4, 4, 8, 2, HALF, LANES), f32),
            pltpu.VMEM((2, trans, CHUNK), f32),
            pltpu.VMEM((2, trans, CHUNK), f32),
        ],
        24,
        10,
    )
    all_totals = lax.all_gather(totals, CHIPS, axis=0, tiled=False)
    far_one, far_three = over(far_low, 1, 0), over(far_high, 3, 0)
    one_low, three_high = over(one_low, 1, 0), over(three_high, 3, 0)
    one_high, three_low = call(
        "add", add_kernel, [one_high, far_three, three_low, far_one], [part16, part16]
    )
    one_high, three_low = over(one_high, 1, 0), over(three_low, 3, 0)
    eight16, eight32 = shape(8, 2, HALF, LANES), shape(8, 2, HALF, LANES, dtype=f32)
    middle = call(
        "middle",
        middle_kernel,
        [stays, one_low, one_high, three_low, three_high],
        [eight32, eight16, eight16, eight16],
    )
    came = [over(middle[m], m, 1) for m in (1, 2, 3)]
    even, odd = call(
        "late",
        late_kernel,
        [middle[0]] + came,
        [shape(4, 2, HALF, LANES, dtype=f32), shape(4, 2, HALF, LANES)],
    )
    came = over_z(odd, 1)
    two32 = shape(2, 2, HALF, LANES, dtype=f32)
    even, odd = call("halve", halve_kernel, [even, came], [two32, two32])
    came = over_z(odd, 2)
    one32 = shape(1, 2, HALF, LANES, dtype=f32)
    even, odd = call("halve", halve_kernel, [even, came], [one32, one32])
    came = over_z(odd, 4)
    block = shape(HALF, LANES, dtype=f32)
    mine, give = call("deal", deal_kernel, [core, even, came], [block, block], [SMEM, VMEM, VMEM])
    came = lax.ppermute(give, "core", swap)
    result = call(
        "last",
        last_kernel,
        [core, mine, came],
        shape(rdev, BLOCK, dtype=f32),
        [SMEM, VMEM, VMEM],
    )
    my_totals = call(
        "totals", totals_kernel, [ref, all_totals], shape(1, LANES, dtype=f32), [SMEM, VMEM]
    )
    return (result, my_totals[0, :rdev], evidence[:, 0])


def solution(mesh):
    fine = Mesh(mesh.devices.reshape(2, 4, 2, 8, 2), EVERYONE)
    placed = (
        P(EVERYONE, None),
        P(EVERYONE, None),
        P(("z", "y_hi"), None),
        P(),
        P(EVERYONE, None),
        P(EVERYONE),
    )
    return jax.shard_map(
        local,
        mesh=fine,
        in_specs=placed,
        out_specs=(P(("z", "y_hi"), ("y_lo", "x", "core")), P(("z", "y_hi")), P(EVERYONE)),
        check_vma=False,
    )
```

profile of v0, /device:TPU:1, one launch (start us, length us, event | category | flops | bytes accessed | tf_op | source)
XLA Modules:
  0.0 468.1 jit_solution(12704260701591997863)
XLA Ops:
  0.7 1.0 copy-done.2
  1.7 1.4 copy-done
  3.1 1.1 copy-done.1
  4.3 0.3 weighted.1
  4.6 3.3 collective-permute-start.6
  7.9 5.2 %collective-permute-start = (bf16[1,2,48,128]{3,2,1,0:T(8,128)(2,1)S(1)}, bf16[1,2,48,128]{3,2,1,0:T(8,128)(2,1)S(1)}, u32[]{:S(2)}, u32[]{:S(2)}) collective-permute-start(bf16[1,2,48,128]{3,2,1,0:T(8,128)(2,1)S(1)} %pack.1.args_0_.packed_ref), channel_id=1, source_target_pairs={{0,8},{2,10},{4,12},{6,14},{8,0},{10,2},{12,4},{14,6},{1,9},{3,11}... | collective-permute-start | bytes 73736 | tf_op jit(solution)/shard_map/ppermute | solution.py:26
  13.1 1.4 collective-permute-done.args_1_
  14.5 1.3 collective-permute-start.1
  15.8 3.1 collective-permute-done.1.args_1_
  18.9 0.2 collective-permute-start.2
  19.1 3.4 collective-permute-done.2.args_1_
  22.4 1.2 collective-permute-start.3
  23.6 2.5 collective-permute-start.4
  26.1 0.3 collective-permute-start.5
  26.4 0.1 copy.19.shifts_ref.args_8_
  26.5 5.7 %rotate.1.rot_ref.args_9_ = bf16[2,4,864,1024]{3,2,1,0:T(8,128)(2,1)S(1)} custom-call(s32[1]{0:T(128)} %bitcast.core_ref.args_0_, s32[1]{0:T(128)} %bitcast.1.x_ref.args_1_, s32[1]{0:T(128)} %bitcast.2.part_ref.args_2_, s32[9,2]{1,0:T(8,128)S(1)} %copy.19.shifts_ref.args_8_, bf16[2,4,48,1024]{3,2,1,0:T(8,128)(2,1)S(1)} %get-tuple-element.30.own_ref.args_9_, ...), custom_call_target="tpu_custom_call" | custom-call | flops 6000000 | bytes 18000000 | tf_op jit(solution)/shard_map/rotate/pallas_call | solution.py:361
  32.2 1.5 collective-permute-done.5.three_ref
  33.7 2.8 collective-permute-start.10
  36.5 0.5 collective-permute-start.12
  37.0 1.0 collective-permute-start.8
  38.0 3.7 collective-permute-done.10.args_8_
  41.7 1.8 collective-permute-done.7.args_3_
  43.4 1.2 collective-permute-start.9
  44.7 1.5 collective-permute-done.12.args_7_
  46.2 1.5 collective-permute-done.8.args_4_
  47.7 4.2 collective-permute-done.11.args_6_
  51.9 4.2 forward.1.args_5_
  56.1 7.4 %collective-permute-start.13 = (f32[864,256]{1,0:T(8,128)S(1)}, f32[864,256]{1,0:T(8,128)S(1)}, u32[]{:S(2)}, u32[]{:S(2)}) collective-permute-start(f32[864,256]{1,0:T(8,128)S(1)} %forward.1.args_5_), channel_id=1, source_target_pairs={{0,16},{16,0},{1,17},{17,1},{2,18},{18,2},{3,19},{19,3},{4,20},{20... | collective-permute-start | bytes 2654216 | tf_op jit(solution)/shard_map/ppermute | solution.py:446
  63.5 0.1 copy.20
  63.6 0.1 fusion
  63.7 0.1 fusion.1
  63.8 1.8 collective-permute-done.14
  65.6 9.0 %backward.1 = (f32[4,8,2,48,128]{4,3,2,1,0:T(8,128)S(1)}, bf16[4,4,2,48,128]{4,3,2,1,0:T(8,128)(2,1)S(1)}, bf16[4,4,2,48,128]{4,3,2,1,0:T(8,128)(2,1)S(1)}, bf16...) custom-call(s32[1]{0:T(128)} %bitcast.core_ref.args_0_, ...), custom_call_target="tpu_custom_call" | custom-call | flops 10000000 | bytes 30000000 | tf_op jit(solution)/shard_map/backward/pallas_call | solution.py:361
  74.6 0.1 collective-permute-start.16
  74.7 0.1 collective-permute-start.17
  74.8 1.5 collective-permute-start.15
  76.3 2.6 collective-permute-start.20
  78.9 4.0 collective-permute-done.16.one_more_ref
  82.9 0.2 add.12
  83.1 0.1 collective-permute-start.18
  83.2 1.5 collective-permute-start.19
  84.7 1.2 collective-permute-done.15.one_low
  86.0 1.1 collective-permute-done.20.three_high
  87.1 3.1 collective-permute-done.18.one_high
  90.2 1.2 collective-permute-done.19.three_low
  91.4 0.3 middle.1
  91.6 0.1 collective-permute-start.21
  91.7 2.4 collective-permute-start.22
  94.2 1.4 collective-permute-start.23
  95.6 0.7 collective-permute-done.21.one
  96.3 3.4 collective-permute-done.22.two
  99.6 2.1 collective-permute-done.23.three
  101.7 0.1 late.1
  101.8 0.3 collective-permute-start.24
  102.2 3.2 collective-permute-done.24.came
  105.4 2.2 collective-permute-start.25
  107.6 2.2 collective-permute-done.25.came
  109.9 6.2 %collective-permute-start.26 = (f32[1,2,48,128]{3,2,1,0:T(8,128)S(1)}, f32[1,2,48,128]{3,2,1,0:T(8,128)S(1)}, u32[]{:S(2)}, u32[]{:S(2)}) collective-permute-start(f32[1,2,48,128]{3,2,1,0:T(8,128)S(1)} %get-tuple-element.52), channel_id=1, source_target_pairs={{0,8},{2,10},{4,12},{6,14},{8,0},{10,2},{12,4},{14,6},{1,9},{3,11}... | collective-permute-start | bytes 147464 | tf_op jit(solution)/shard_map/ppermute | solution.py:26
  116.1 288.2 %all-gather = f32[1024,128]{1,0:T(8,128)S(1)} all-gather(f32[8,128]{1,0:T(8,128)S(1)} %get-tuple-element.55), channel_id=2, replica_groups=mesh['y_lo'=2,'x'=4,'core'=2,'z'=8,'y_hi'=2] {'z','y_hi','y_lo','x'}, dimensions={0}, use_global_device_ids=true | all-gather | bytes 528384 | tf_op jit(solution)/shard_map/all_gather | solution.py:467
  404.3 0.2 totals.1
  404.5 61.7 %collective-permute-start.27 = (f32[48,128]{1,0:T(8,128)S(1)}, f32[48,128]{1,0:T(8,128)S(1)}, u32[]{:S(2)}, u32[]{:S(2)}) collective-permute-start(f32[48,128]{1,0:T(8,128)S(1)} %get-tuple-element.54), channel_id=1, source_target_pairs={{0,16},{16,0},{1,17},{17,1},{2,18},{18,2},{3,19},{19,3},{4,20},{20... | collective-permute-start | bytes 73736 | tf_op jit(solution)/shard_map/ppermute | solution.py:497
  466.3 0.5 slice_bitcast_fusion
  466.8 0.6 reduce
  467.4 0.6 last.1
  (29 shorter events, 0.2 us)
Async XLA Ops:
  0.6 1.0 copy-start.2
  1.7 24.7 %copy-start.5 = (s32[9,2]{0,1:T(2,128)S(1)}, s32[9,2]{0,1:T(2,128)}, u32[]{:S(2)}) copy-start(s32[9,2]{0,1:T(2,128)} %param.9) | copy-start | bytes 220
  1.7 1.4 copy-start
  3.1 1.1 copy-start.1
  4.6 21.9 %collective-permute-start.6 = (bf16[2,4,48,1024]{3,2,1,0:T(8,128)(2,1)S(1)}, bf16[2,4,48,1024]{3,2,1,0:T(8,128)(2,1)S(1)}, u32[]{:S(2)}, u32[]{:S(2)}) collective-permute-start(bf16[2,4,48,1024]{3,2,1,0:T(8,128)(2,1)S(1)} %get-tuple-element.31), channel_id=1, source_target_pairs={{0,16},{16,0},{1,17},{17,1},{2,18},{18,2},{3,19},{19,3},{4,20},{20... | collective-permute-start | bytes 2359304 | tf_op jit(solution)/shard_map/ppermute | solution.py:406
  7.9 6.6 %collective-permute-start = (bf16[1,2,48,128]{3,2,1,0:T(8,128)(2,1)S(1)}, bf16[1,2,48,128]{3,2,1,0:T(8,128)(2,1)S(1)}, u32[]{:S(2)}, u32[]{:S(2)}) collective-permute-start(bf16[1,2,48,128]{3,2,1,0:T(8,128)(2,1)S(1)} %pack.1.args_0_.packed_ref), channel_id=1, source_target_pairs={{0,8},{2,10},{4,12},{6,14},{8,0},{10,2},{12,4},{14,6},{1,9},{3,11}... | collective-permute-start | bytes 73736 | tf_op jit(solution)/shard_map/ppermute | solution.py:26
  14.5 4.4 collective-permute-start.1
  18.9 3.6 collective-permute-start.2
  22.4 9.7 %collective-permute-start.3 = (bf16[8,2,48,128]{3,2,1,0:T(8,128)(2,1)S(1)}, bf16[8,2,48,128]{3,2,1,0:T(8,128)(2,1)S(1)}, u32[]{:S(2)}, u32[]{:S(2)}) collective-permute-start(bf16[8,2,48,128]{3,2,1,0:T(8,128)(2,1)S(1)} %stack.17.own_ref), channel_id=1, source_target_pairs={{0,128},{1,129},{16,48},{17,49},{32,160},{33,161},{48,16},{49,17},... | collective-permute-start | bytes 589832 | tf_op jit(solution)/shard_map/ppermute | solution.py:41
  23.6 8.5 %collective-permute-start.4 = (bf16[8,2,48,128]{3,2,1,0:T(8,128)(2,1)S(1)}, bf16[8,2,48,128]{3,2,1,0:T(8,128)(2,1)S(1)}, u32[]{:S(2)}, u32[]{:S(2)}) collective-permute-start(bf16[8,2,48,128]{3,2,1,0:T(8,128)(2,1)S(1)} %stack.17.own_ref), channel_id=1, source_target_pairs={{0,1},{1,0},{16,80},{17,81},{32,33},{33,32},{48,112},{49,113},{64,... | collective-permute-start | bytes 589832 | tf_op jit(solution)/shard_map/ppermute | solution.py:41
  26.1 7.6 %collective-permute-start.5 = (bf16[8,2,48,128]{3,2,1,0:T(8,128)(2,1)S(1)}, bf16[8,2,48,128]{3,2,1,0:T(8,128)(2,1)S(1)}, u32[]{:S(2)}, u32[]{:S(2)}) collective-permute-start(bf16[8,2,48,128]{3,2,1,0:T(8,128)(2,1)S(1)} %stack.17.own_ref), channel_id=1, source_target_pairs={{0,129},{1,128},{16,112},{17,113},{32,161},{33,160},{48,80},{49,81... | collective-permute-start | bytes 589832 | tf_op jit(solution)/shard_map/ppermute | solution.py:41
  33.7 8.0 %collective-permute-start.10 = (bf16[2,8,2,48,128]{4,3,2,1,0:T(8,128)(2,1)S(1)}, bf16[2,8,2,48,128]{4,3,2,1,0:T(8,128)(2,1)S(1)}, u32[]{:S(2)}, u32[]{:S(2)}) collective-permute-start(bf16[2,8,2,48,128]{4,3,2,1,0:T(8,128)(2,1)S(1)} %get-tuple-element.33.args_2_), channel_id=1, source_target_pairs={{0,96},{1,97},{16,145},{17,144},{32,64},{33,65},{48,177},{49,176},... | collective-permute-start | bytes 1179656 | tf_op jit(solution)/shard_map/ppermute | solution.py:41
  36.5 27.0 %copy-start.3 = (s32[48,12]{0,1:T(8,128)S(1)}, s32[48,12]{0,1:T(8,128)}, u32[]{:S(2)}) copy-start(s32[48,12]{0,1:T(8,128)} %param.10) | copy-start | bytes 6916
  36.5 27.1 %copy-start.4 = (s32[48]{0:T(128)S(1)}, s32[48]{0:T(128)}, u32[]{:S(2)}) copy-start(s32[48]{0:T(128)} %param.11) | copy-start | bytes 580
  36.5 6.9 %collective-permute-start.7 = (bf16[2,8,2,48,128]{4,3,2,1,0:T(8,128)(2,1)S(1)}, bf16[2,8,2,48,128]{4,3,2,1,0:T(8,128)(2,1)S(1)}, u32[]{:S(2)}, u32[]{:S(2)}) collective-permute-start(bf16[2,8,2,48,128]{4,3,2,1,0:T(8,128)(2,1)S(1)} %get-tuple-element.32.args_1_), channel_id=1, source_target_pairs={{0,32},{1,33},{16,144},{17,145},{32,0},{33,1},{48,176},{49,177},{6... | collective-permute-start | bytes 1179656 | tf_op jit(solution)/shard_map/ppermute | solution.py:41
  36.5 9.7 %collective-permute-start.12 = (bf16[2,8,2,48,128]{4,3,2,1,0:T(8,128)(2,1)S(1)}, bf16[2,8,2,48,128]{4,3,2,1,0:T(8,128)(2,1)S(1)}, u32[]{:S(2)}, u32[]{:S(2)}) collective-permute-start(bf16[2,8,2,48,128]{4,3,2,1,0:T(8,128)(2,1)S(1)} %get-tuple-element.32.args_1_), channel_id=1, source_target_pairs={{0,96},{1,97},{16,145},{17,144},{32,64},{33,65},{48,177},{49,176},... | collective-permute-start | bytes 1179656 | tf_op jit(solution)/shard_map/ppermute | solution.py:41
  37.0 10.7 %collective-permute-start.8 = (bf16[2,8,2,48,128]{4,3,2,1,0:T(8,128)(2,1)S(1)}, bf16[2,8,2,48,128]{4,3,2,1,0:T(8,128)(2,1)S(1)}, u32[]{:S(2)}, u32[]{:S(2)}) collective-permute-start(bf16[2,8,2,48,128]{4,3,2,1,0:T(8,128)(2,1)S(1)} %get-tuple-element.33.args_2_), channel_id=1, source_target_pairs={{0,32},{1,33},{16,144},{17,145},{32,0},{33,1},{48,176},{49,177},{6... | collective-permute-start | bytes 1179656 | tf_op jit(solution)/shard_map/ppermute | solution.py:41
  41.7 10.2 %collective-permute-start.11 = (bf16[2,8,2,48,128]{4,3,2,1,0:T(8,128)(2,1)S(1)}, bf16[2,8,2,48,128]{4,3,2,1,0:T(8,128)(2,1)S(1)}, u32[]{:S(2)}, u32[]{:S(2)}) collective-permute-start(bf16[2,8,2,48,128]{4,3,2,1,0:T(8,128)(2,1)S(1)} %collective-permute-done.10.args_8_), channel_id=1, source_target_pairs={{0,32},{1,33},{16,144},{17,145},{32,0},{33,1},{48,176},{49,177},{6... | collective-permute-start | bytes 1179656 | tf_op jit(solution)/shard_map/ppermute | solution.py:41
  43.4 8.4 %collective-permute-start.9 = (bf16[2,8,2,48,128]{4,3,2,1,0:T(8,128)(2,1)S(1)}, bf16[2,8,2,48,128]{4,3,2,1,0:T(8,128)(2,1)S(1)}, u32[]{:S(2)}, u32[]{:S(2)}) collective-permute-start(bf16[2,8,2,48,128]{4,3,2,1,0:T(8,128)(2,1)S(1)} %collective-permute-done.7.args_3_), channel_id=1, source_target_pairs={{0,96},{1,97},{16,145},{17,144},{32,64},{33,65},{48,177},{49,176},... | collective-permute-start | bytes 1179656 | tf_op jit(solution)/shard_map/ppermute | solution.py:41
  56.1 9.5 %collective-permute-start.13 = (f32[864,256]{1,0:T(8,128)S(1)}, f32[864,256]{1,0:T(8,128)S(1)}, u32[]{:S(2)}, u32[]{:S(2)}) collective-permute-start(f32[864,256]{1,0:T(8,128)S(1)} %forward.1.args_5_), channel_id=1, source_target_pairs={{0,16},{16,0},{1,17},{17,1},{2,18},{18,2},{3,19},{19,3},{4,20},{20... | collective-permute-start | bytes 2654216 | tf_op jit(solution)/shard_map/ppermute | solution.py:446
  63.7 1.9 collective-permute-start.14
  74.6 8.2 %collective-permute-start.16 = (bf16[4,4,2,48,128]{4,3,2,1,0:T(8,128)(2,1)S(1)}, bf16[4,4,2,48,128]{4,3,2,1,0:T(8,128)(2,1)S(1)}, u32[]{:S(2)}, u32[]{:S(2)}) collective-permute-start(bf16[4,4,2,48,128]{4,3,2,1,0:T(8,128)(2,1)S(1)} %get-tuple-element.37), channel_id=1, source_target_pairs={{0,96},{1,97},{16,145},{17,144},{32,64},{33,65},{48,177},{49,176},... | collective-permute-start | bytes 1179656 | tf_op jit(solution)/shard_map/ppermute | solution.py:41
  74.7 8.1 %collective-permute-start.17 = (bf16[4,4,2,48,128]{4,3,2,1,0:T(8,128)(2,1)S(1)}, bf16[4,4,2,48,128]{4,3,2,1,0:T(8,128)(2,1)S(1)}, u32[]{:S(2)}, u32[]{:S(2)}) collective-permute-start(bf16[4,4,2,48,128]{4,3,2,1,0:T(8,128)(2,1)S(1)} %get-tuple-element.39), channel_id=1, source_target_pairs={{0,32},{1,33},{16,144},{17,145},{32,0},{33,1},{48,176},{49,177},{6... | collective-permute-start | bytes 1179656 | tf_op jit(solution)/shard_map/ppermute | solution.py:41
  74.8 11.1 %collective-permute-start.15 = (bf16[4,4,2,48,128]{4,3,2,1,0:T(8,128)(2,1)S(1)}, bf16[4,4,2,48,128]{4,3,2,1,0:T(8,128)(2,1)S(1)}, u32[]{:S(2)}, u32[]{:S(2)}) collective-permute-start(bf16[4,4,2,48,128]{4,3,2,1,0:T(8,128)(2,1)S(1)} %get-tuple-element.35), channel_id=1, source_target_pairs={{0,32},{1,33},{16,144},{17,145},{32,0},{33,1},{48,176},{49,177},{6... | collective-permute-start | bytes 1179656 | tf_op jit(solution)/shard_map/ppermute | solution.py:41
  76.3 10.8 %collective-permute-start.20 = (bf16[4,4,2,48,128]{4,3,2,1,0:T(8,128)(2,1)S(1)}, bf16[4,4,2,48,128]{4,3,2,1,0:T(8,128)(2,1)S(1)}, u32[]{:S(2)}, u32[]{:S(2)}) collective-permute-start(bf16[4,4,2,48,128]{4,3,2,1,0:T(8,128)(2,1)S(1)} %get-tuple-element.42), channel_id=1, source_target_pairs={{0,96},{1,97},{16,145},{17,144},{32,64},{33,65},{48,177},{49,176},... | collective-permute-start | bytes 1179656 | tf_op jit(solution)/shard_map/ppermute | solution.py:41
  83.1 7.1 %collective-permute-start.18 = (bf16[4,4,2,48,128]{4,3,2,1,0:T(8,128)(2,1)S(1)}, bf16[4,4,2,48,128]{4,3,2,1,0:T(8,128)(2,1)S(1)}, u32[]{:S(2)}, u32[]{:S(2)}) collective-permute-start(bf16[4,4,2,48,128]{4,3,2,1,0:T(8,128)(2,1)S(1)} %get-tuple-element.40), channel_id=1, source_target_pairs={{0,32},{1,33},{16,144},{17,145},{32,0},{33,1},{48,176},{49,177},{6... | collective-permute-start | bytes 1179656 | tf_op jit(solution)/shard_map/ppermute | solution.py:41
  83.2 8.2 %collective-permute-start.19 = (bf16[4,4,2,48,128]{4,3,2,1,0:T(8,128)(2,1)S(1)}, bf16[4,4,2,48,128]{4,3,2,1,0:T(8,128)(2,1)S(1)}, u32[]{:S(2)}, u32[]{:S(2)}) collective-permute-start(bf16[4,4,2,48,128]{4,3,2,1,0:T(8,128)(2,1)S(1)} %get-tuple-element.41), channel_id=1, source_target_pairs={{0,96},{1,97},{16,145},{17,144},{32,64},{33,65},{48,177},{49,176},... | collective-permute-start | bytes 1179656 | tf_op jit(solution)/shard_map/ppermute | solution.py:41
  91.6 4.6 collective-permute-start.21
  91.7 7.9 %collective-permute-start.22 = (bf16[8,2,48,128]{3,2,1,0:T(8,128)(2,1)S(1)}, bf16[8,2,48,128]{3,2,1,0:T(8,128)(2,1)S(1)}, u32[]{:S(2)}, u32[]{:S(2)}) collective-permute-start(bf16[8,2,48,128]{3,2,1,0:T(8,128)(2,1)S(1)} %get-tuple-element.45), channel_id=1, source_target_pairs={{0,1},{1,0},{16,80},{17,81},{32,33},{33,32},{48,112},{49,113},{64,... | collective-permute-start | bytes 589832 | tf_op jit(solution)/shard_map/ppermute | solution.py:41
  94.2 7.6 %collective-permute-start.23 = (bf16[8,2,48,128]{3,2,1,0:T(8,128)(2,1)S(1)}, bf16[8,2,48,128]{3,2,1,0:T(8,128)(2,1)S(1)}, u32[]{:S(2)}, u32[]{:S(2)}) collective-permute-start(bf16[8,2,48,128]{3,2,1,0:T(8,128)(2,1)S(1)} %get-tuple-element.46), channel_id=1, source_target_pairs={{0,129},{1,128},{16,112},{17,113},{32,161},{33,160},{48,80},{49,81... | collective-permute-start | bytes 589832 | tf_op jit(solution)/shard_map/ppermute | solution.py:41
  101.8 3.6 collective-permute-start.24
  105.4 4.5 collective-permute-start.25
  109.9 294.6 %collective-permute-start.26 = (f32[1,2,48,128]{3,2,1,0:T(8,128)S(1)}, f32[1,2,48,128]{3,2,1,0:T(8,128)S(1)}, u32[]{:S(2)}, u32[]{:S(2)}) collective-permute-start(f32[1,2,48,128]{3,2,1,0:T(8,128)S(1)} %get-tuple-element.52), channel_id=1, source_target_pairs={{0,8},{2,10},{4,12},{6,14},{8,0},{10,2},{12,4},{14,6},{1,9},{3,11}... | collective-permute-start | bytes 147464 | tf_op jit(solution)/shard_map/ppermute | solution.py:26
  404.5 62.9 %collective-permute-start.27 = (f32[48,128]{1,0:T(8,128)S(1)}, f32[48,128]{1,0:T(8,128)S(1)}, u32[]{:S(2)}, u32[]{:S(2)}) collective-permute-start(f32[48,128]{1,0:T(8,128)S(1)} %get-tuple-element.54), channel_id=1, source_target_pairs={{0,16},{16,0},{1,17},{17,1},{2,18},{18,2},{3,19},{19,3},{4,20},{20... | collective-permute-start | bytes 73736 | tf_op jit(solution)/shard_map/ppermute | solution.py:497
where the time goes:
time: 468 us
  blocking collectives  288 us (62%)
  starting transfers between devices  107 us (23%)
  waiting for transfers between devices  46.1 us (10%)
  Pallas kernels  20.7 us (4%)
    all_gather x1, blocking collectives, local(): all_totals = lax.all_gather(totals, CHIPS, axis=0, tiled=False)  288 us
    ppermute x1, starting transfers between devices, local(): came = lax.ppermute(give, 'core', swap)  61.7 us
    ppermute x18, waiting for transfers between devices, over(): return lax.ppermute(value, ('y_lo', 'x', 'core', 'y_hi'), pairs)  30.9 us
    pallas_call x17, Pallas kernels, call(): pl.pallas_call(kernel, out_shape=outs, in_specs=specs or [VMEM] * len(ins...  20.7 us
    ppermute x18, starting transfers between devices, over(): return lax.ppermute(value, ('y_lo', 'x', 'core', 'y_hi'), pairs)  19.2 us
    ppermute x6, starting transfers between devices, over_z(): return lax.ppermute(value, 'z', [(i, i ^ bits) for i in range(8)])  15.4 us
    ppermute x6, waiting for transfers between devices, over_z(): return lax.ppermute(value, 'z', [(i, i ^ bits) for i in range(8)])  13.3 us
  transfers between devices with their start and end apart: 28, of which 20 were waited for; matrix products, arithmetic and copies ran while one was open for 0% of the time, Pallas kernels for 1%

commit v1 on v0

--- a/solution.py
+++ b/solution.py
@@ -1,3 +1,4 @@
+import functools
 import math
 
 import jax
@@ -15,7 +16,6 @@
 HALF = 48
 CHUNK = 256
 STACKED = (0, 4, 2, 6, 1, 5, 3, 7)
-CHIPS = ("z", "y_hi", "y_lo", "x")
 EVERYONE = ("y_lo", "x", "core", "z", "y_hi")
 SMEM = pl.BlockSpec(memory_space=pltpu.SMEM)
 VMEM = pl.BlockSpec(memory_space=pltpu.VMEM)
@@ -50,13 +50,11 @@
         out_ref[0, p] = jnp.concatenate(tiles, axis=0).astype(jnp.bfloat16)
 
 
-def stack_kernel(*args):
-    out_ref = args[-1]
-    row = 0
-    for ref in args[:-1]:
-        count = ref.shape[0]
-        out_ref[row : row + count] = ref[...]
-        row += count
+def stack_kernel(own_ref, came_ref, *rest):
+    out_ref = rest[-1]
+    count = own_ref.shape[0]
+    out_ref[:count] = own_ref[...]
+    out_ref[count:] = came_ref[...]
 
 
 def join_kernel(own_ref, one_ref, two_ref, three_ref, rot_ref, low_ref, high_ref):
@@ -105,7 +103,7 @@
 
 
 def rotate_kernel(
-    core_ref, x_ref, part_ref, shifts_ref, own_ref, recv_ref, rot_ref, cos_ref, sin_ref
+    first_xr, core_ref, x_ref, part_ref, shifts_ref, own_ref, recv_ref, rot_ref, cos_ref, sin_ref
 ):
     first = part_ref[0]
     steps = BLOCK // CHUNK
@@ -114,15 +112,30 @@
         xr = index // steps
         start = pl.multiple_of((index % steps) * CHUNK, CHUNK)
 
-        def put(part, base, rows, value):
-            rot_ref[part ^ first, xr, base : base + rows, pl.ds(start, CHUNK)] = value
-
-        rotate_chunk(
-            core_ref[0], x_ref[0], shifts_ref, own_ref, recv_ref, xr, start, (cos_ref, sin_ref), put
-        )
+        def put(part, base, rows, value, place=xr):
+            rot_ref[part ^ first, place, base : base + rows, pl.ds(start, CHUNK)] = value
+
+        tables = cos_ref, sin_ref
+        xr = first_xr + xr
+        rotate_chunk(core_ref[0], x_ref[0], shifts_ref, own_ref, recv_ref, xr, start, tables, put)
         return carry
 
-    lax.fori_loop(0, 4 * steps, step, 0)
+    lax.fori_loop(0, rot_ref.shape[1] * steps, step, 0)
+
+
+def three_parts(value):
+    terms = []
+    for _ in range(3):
+        term = value.astype(jnp.bfloat16)
+        terms.append(term.astype(jnp.float32))
+        value = value - terms[-1]
+    terms.append(jnp.zeros((HALF - 24, LANES), jnp.float32))
+    return jnp.concatenate(terms, axis=0).astype(jnp.bfloat16)
+
+
+def whole(block):
+    block = block.astype(jnp.float32)
+    return (block[0:8] + block[8:16]) + block[16:24]
 
 
 def low_rows():
@@ -145,7 +158,7 @@
 
 
 def forward_kernel(*args):
-    core_ref, blocks, (rot_ref, out_ref, wide_ref) = args[0], args[1:9], args[9:]
+    core_ref, blocks, rots, (out_ref, wide_ref) = args[0], args[1:9], args[9:11], args[11:]
     first = core_ref[0] == 0
 
     def block(n, m, k):
@@ -165,7 +178,7 @@
                 for p in range(2):
                     spread(pair[0][p], pair[1][p], wide, 24 * k, p * SIDE)
             product = lax.dot_general(
-                rot_ref[b, xr],
+                rots[xr // 2][b, xr % 2],
                 wide[...].astype(jnp.bfloat16),
                 (((1,), (1,)), ((), ())),
                 preferred_element_type=jnp.float32,
@@ -244,6 +257,10 @@
     totals_ref[...] = jnp.zeros(totals_ref.shape, jnp.float32)
     totals_ref[0:1, :] = totals[:, :LANES]
     totals_ref[1:2, : refs_all - LANES] = totals[:, LANES:]
+    parts = three_parts(totals_ref[...])
+    totals_ref[...] = whole(parts)
+    far_low[32] = parts
+    far_high[32] = parts
     weights = flipped[:, :rows].astype(jnp.bfloat16)
     low = low_rows()
 
@@ -293,67 +310,102 @@
             (1, one_low, one_high),
             (3, three_low, three_high),
         ):
-            low_ref[place] = sums_ref[distance, place, 0:4].astype(low_ref.dtype)
-            high_ref[place] = sums_ref[distance, place, 4:8].astype(high_ref.dtype)
-
-
-def add_kernel(one_ref, one_more_ref, three_ref, three_more_ref, one_out, three_out):
-    one_out[...] = (one_ref[...] + one_more_ref[...].astype(jnp.float32)).astype(jnp.bfloat16)
-    three_out[...] = (three_ref[...] + three_more_ref[...].astype(jnp.float32)).astype(jnp.bfloat16)
-
-
-def middle_kernel(stays, one_low, one_high, three_low, three_high, *outs):
-    for n, out_ref in enumerate(outs):
+            for k in range(4):
+                for p in range(2):
+                    at = 8 * place + 2 * k + p
+                    low_ref[at] = sums_ref[distance, place, k, p].astype(low_ref.dtype)
+                    high_ref[at] = sums_ref[distance, place, 4 + k, p].astype(high_ref.dtype)
+
+
+def add_kernel(
+    totals_ref, one_ref, far_three, three_ref, far_one, one_out, three_out, both_ref, third_ref
+):
+    one_out[0:32] = (one_ref[...] + far_three[0:32].astype(jnp.float32)).astype(jnp.bfloat16)
+    one_out[32] = far_three[32]
+    three_out[...] = (three_ref[...] + far_one[0:32].astype(jnp.float32)).astype(jnp.bfloat16)
+    both_ref[...] = totals_ref[...] + whole(far_one[32])
+    third_ref[...] = whole(far_three[32])
+
+
+def middle_kernel(both_ref, third_ref, stays, one_low, one_high, three_low, three_high, *outs):
+    totals_ref = outs[-1]
+    totals = both_ref[...] + (whole(one_high[32]) + third_ref[...])
+    parts = three_parts(totals)
+    totals_ref[...] = whole(parts)
+    for n, out_ref in enumerate(outs[:-1]):
+        if n:
+            out_ref[16] = parts
         for ks, one, three in ((0, one_low, three_low), (4, one_high, three_high)):
-            total = stays[n, ks : ks + 4] + one[n].astype(jnp.float32)
-            total = total + three[n].astype(jnp.float32)
-            out_ref[ks : ks + 4] = total.astype(out_ref.dtype)
-
-
-def late_kernel(stays, one, two, three, even_ref, odd_ref):
+            for k in range(4):
+                for p in range(2):
+                    at = 8 * n + 2 * k + p
+                    total = stays[n, ks + k, p] + one[at].astype(jnp.float32)
+                    total = total + three[at].astype(jnp.float32)
+                    out_ref[2 * (ks + k) + p] = total.astype(out_ref.dtype)
+
+
+def late_kernel(totals_ref, stays, one, two, three, even_ref, odd_ref, sum_ref):
+    totals = totals_ref[...] + whole(one[16])
+    totals = totals + (whole(two[16]) + whole(three[16]))
+    parts = three_parts(totals)
+    sum_ref[...] = whole(parts)
+    odd_ref[8] = parts
     for k in range(8):
-        total = stays[k] + one[k].astype(jnp.float32)
-        total = total + (two[k].astype(jnp.float32) + three[k].astype(jnp.float32))
-        if k % 2 == 0:
-            even_ref[k // 2] = total
-        else:
-            odd_ref[k // 2] = total.astype(odd_ref.dtype)
-
-
-def halve_kernel(stays, came, even_ref, odd_ref):
-    for k in range(stays.shape[0]):
-        total = stays[k] + came[k].astype(jnp.float32)
-        if k % 2 == 0:
-            even_ref[k // 2] = total
-        else:
-            odd_ref[k // 2] = total
-
-
-def deal_kernel(core_ref, stays, came, mine_ref, give_ref):
+        for p in range(2):
+            at = 2 * k + p
+            total = stays[at] + one[at].astype(jnp.float32)
+            total = total + (two[at].astype(jnp.float32) + three[at].astype(jnp.float32))
+            if k % 2 == 0:
+                even_ref[2 * (k // 2) + p] = total
+            else:
+                odd_ref[2 * (k // 2) + p] = total.astype(odd_ref.dtype)
+
+
+def halve_kernel(totals_ref, stays, came, even_ref, odd_ref, sum_ref):
+    count = stays.shape[0] // 2
+    last = came[2 * count]
+    if last.dtype == jnp.bfloat16:
+        totals = totals_ref[...] + whole(last)
+    else:
+        totals = totals_ref[...] + last[0:8]
+    sum_ref[...] = totals
+    odd_ref[count] = jnp.zeros((HALF, LANES), jnp.float32)
+    odd_ref[count, 0:8] = totals
+    for k in range(count):
+        for p in range(2):
+            total = stays[2 * k + p] + came[2 * k + p].astype(jnp.float32)
+            if k % 2 == 0:
+                even_ref[2 * (k // 2) + p] = total
+            else:
+                odd_ref[2 * (k // 2) + p] = total
+
+
+def deal_kernel(core_ref, totals_ref, stays, came, mine_ref, give_ref):
     first = core_ref[0] == 0
-    low, high = stays[0, 0] + came[0, 0], stays[0, 1] + came[0, 1]
-    mine_ref[...] = jnp.where(first, low, high)
-    give_ref[...] = jnp.where(first, high, low)
-
-
-def last_kernel(core_ref, mine_ref, came_ref, out_ref):
+    low, high = stays[0] + came[0], stays[1] + came[1]
+    totals = totals_ref[...] + came[2, 0:8]
+    mine_ref[0] = jnp.where(first, low, high)
+    give_ref[0] = jnp.where(first, high, low)
+    for ref in (mine_ref, give_ref):
+        ref[1] = jnp.zeros((HALF, LANES), jnp.float32)
+        ref[1, 0:8] = totals
+
+
+def last_kernel(core_ref, ref_ref, mine_ref, came_ref, out_ref, totals_ref):
     first = core_ref[0] == 0
-    low = jnp.where(first, mine_ref[...], came_ref[...])
-    high = jnp.where(first, came_ref[...], mine_ref[...])
+    low = jnp.where(first, mine_ref[0], came_ref[0])
+    high = jnp.where(first, came_ref[0], mine_ref[0])
+    total = jnp.where(first, mine_ref[1, 0:8], came_ref[1, 0:8])
+    row = jnp.concatenate([total[0:1], total[1:2]], axis=1)
+    row = jnp.broadcast_to(row, (8, 2 * LANES))
+    row = pltpu.roll(row, (2 * LANES - 12 * ref_ref[0]) % (2 * LANES), 1)
+    totals_ref[...] = row[0:1, :LANES]
     for side, block in enumerate((low, high)):
         for g in range(GROUPS):
             start = side * SIDE + g * LANES
             out_ref[0:8, start : start + LANES] = block[8 * g : 8 * g + 8]
             at = 8 * GROUPS + 4 * g
             out_ref[8:12, start : start + LANES] = block[at : at + 4]
-
-
-def totals_kernel(ref_ref, all_ref, out_ref):
-    total = jnp.sum(all_ref[...], axis=0)
-    row = jnp.concatenate([total[0:1], total[1:2]], axis=1)
-    row = jnp.broadcast_to(row, (8, 2 * LANES))
-    row = pltpu.roll(row, (2 * LANES - 12 * ref_ref[0]) % (2 * LANES), 1)
-    out_ref[...] = row[0:1, :LANES]
 
 
 def call(name, kernel, ins, outs, specs=None, scratch=(), mebibytes=16, micros=1):
@@ -395,11 +447,14 @@
     mine = call(
         "pack", pack_kernel, [column, core, refs], shape(1, 2, HALF, LANES), [SMEM, SMEM, VMEM]
     )
+    four = call(
+        "stack", stack_kernel, [mine, over_z(mine, 4)], shape(2, 2, HALF, LANES)
+    )
     half = shape(2, 4, parts, BLOCK)
     own, other = call(
         "weighted",
         weighted_kernel,
-        [core, x, images, ctf, mine],
+        [core, x, images, ctf, four],
         [half, half],
         [SMEM, SMEM, VMEM, VMEM, ANY],
     )
@@ -408,26 +463,37 @@
     used = jnp.where(slot < counts[:, None], lists, -1)
     used_pair = jnp.stack([used, lax.ppermute(used, "core", swap)])
     tables = [pltpu.VMEM((trans, CHUNK), f32)] * 2
-    rot = call(
-        "rotate",
-        rotate_kernel,
-        [core, x, y_lo, shifts, own, recv],
-        shape(2, 4, rows, BLOCK),
-        [SMEM] * 3 + [VMEM] * 3,
-        tables,
-        8,
-        6,
-    )
-
-    blocks = mine
-    for bits in (4, 2, 1):
-        came = over_z(blocks, bits)
-        blocks = call(
-            "stack", stack_kernel, [blocks, came], shape(2 * blocks.shape[0], 2, HALF, LANES)
+    rots = []
+    for first_xr in (0, 2):
+        rots.append(
+            call(
+                "rotate",
+                functools.partial(rotate_kernel, first_xr),
+                [core, x, y_lo, shifts, own, recv],
+                shape(2, 2, rows, BLOCK),
+                [SMEM] * 3 + [VMEM] * 3,
+                tables,
+                8,
+                3,
+            )
         )
+    two = call(
+        "stack",
+        stack_kernel,
+        [four, over_z(four, 2), recv],
+        shape(4, 2, HALF, LANES),
+        [VMEM, VMEM, ANY],
+    )
+    blocks = call(
+        "stack",
+        stack_kernel,
+        [two, over_z(two, 1), rots[0]],
+        shape(8, 2, HALF, LANES),
+        [VMEM, VMEM, ANY],
+    )
     fours = [blocks] + [over(blocks, m, 1) for m in (1, 2, 3)]
     low, high = call(
-        "join", join_kernel, fours + [rot], [shape(2, 8, 2, HALF, LANES)] * 2, [VMEM] * 4 + [ANY]
+        "join", join_kernel, fours + [rots[1]], [shape(2, 8, 2, HALF, LANES)] * 2, [VMEM] * 4 + [ANY]
     )
     one_low, three_high = over(low, 1, 0), over(high, 3, 0)
     one_high, three_low = over(high, 1, 0), over(low, 3, 0)
@@ -436,9 +502,10 @@
     scores = call(
         "forward",
         forward_kernel,
-        [core, low, high, one_low, one_high, two_low, two_high, three_low, three_high, rot],
+        [core, low, high, one_low, one_high, two_low, two_high, three_low, three_high]
+        + rots,
         shape(rows, lanes, dtype=f32),
-        [SMEM] + [VMEM] * 9,
+        [SMEM] + [VMEM] * 10,
         [pltpu.VMEM((2, refs_all, BLOCK), f32)],
         16,
         4,
@@ -446,13 +513,14 @@
     theirs = lax.ppermute(scores, "core", swap)
 
     scale = (2 * ctf.shape[1]) ** -0.5
-    part16, part32 = shape(4, 4, 2, HALF, LANES), shape(4, 4, 2, HALF, LANES, dtype=f32)
+    part16, part32 = shape(32, HALF, LANES), shape(32, HALF, LANES, dtype=f32)
+    more16, row = shape(33, HALF, LANES), shape(8, LANES, dtype=f32)
     stays, far_low, far_high, one_low, one_high, three_low, three_high, evidence, totals = call(
         "backward",
         lambda *args: backward_kernel(scale, *args),
         [core, x, y_lo, z, y_hi, scores, theirs, used_pair, shifts, own, recv],
-        [shape(4, 8, 2, HALF, LANES, dtype=f32), part16, part16, part16, part32, part32, part16]
-        + [shape(parts, 1, dtype=f32), shape(8, LANES, dtype=f32)],
+        [shape(4, 8, 2, HALF, LANES, dtype=f32), more16, more16, part16, part32, part32, part16]
+        + [shape(parts, 1, dtype=f32), row],
         [SMEM] * 5 + [VMEM] * 6,
         [
             pltpu.VMEM((rows + 8, refs_all), f32),
@@ -464,48 +532,52 @@
         24,
         10,
     )
-    all_totals = lax.all_gather(totals, CHIPS, axis=0, tiled=False)
     far_one, far_three = over(far_low, 1, 0), over(far_high, 3, 0)
     one_low, three_high = over(one_low, 1, 0), over(three_high, 3, 0)
-    one_high, three_low = call(
-        "add", add_kernel, [one_high, far_three, three_low, far_one], [part16, part16]
+    one_high, three_low, both, third = call(
+        "add",
+        add_kernel,
+        [totals, one_high, far_three, three_low, far_one],
+        [more16, part16, row, row],
     )
     one_high, three_low = over(one_high, 1, 0), over(three_low, 3, 0)
-    eight16, eight32 = shape(8, 2, HALF, LANES), shape(8, 2, HALF, LANES, dtype=f32)
-    middle = call(
+    *middle, totals = call(
         "middle",
         middle_kernel,
-        [stays, one_low, one_high, three_low, three_high],
-        [eight32, eight16, eight16, eight16],
+        [both, third, stays, one_low, one_high, three_low, three_high],
+        [shape(16, HALF, LANES, dtype=f32)] + [shape(17, HALF, LANES)] * 3 + [row],
     )
     came = [over(middle[m], m, 1) for m in (1, 2, 3)]
-    even, odd = call(
+    even, odd, totals = call(
         "late",
         late_kernel,
-        [middle[0]] + came,
-        [shape(4, 2, HALF, LANES, dtype=f32), shape(4, 2, HALF, LANES)],
-    )
-    came = over_z(odd, 1)
-    two32 = shape(2, 2, HALF, LANES, dtype=f32)
-    even, odd = call("halve", halve_kernel, [even, came], [two32, two32])
-    came = over_z(odd, 2)
-    one32 = shape(1, 2, HALF, LANES, dtype=f32)
-    even, odd = call("halve", halve_kernel, [even, came], [one32, one32])
-    came = over_z(odd, 4)
-    block = shape(HALF, LANES, dtype=f32)
-    mine, give = call("deal", deal_kernel, [core, even, came], [block, block], [SMEM, VMEM, VMEM])
+        [totals, middle[0]] + came,
+        [shape(8, HALF, LANES, dtype=f32), shape(9, HALF, LANES), row],
+    )
+    for bits, count in ((1, 4), (2, 2)):
+        even, odd, totals = call(
+            "halve",
+            halve_kernel,
+            [totals, even, over_z(odd, bits)],
+            [
+                shape(count, HALF, LANES, dtype=f32),
+                shape(count + 1, HALF, LANES, dtype=f32),
+                row,
+            ],
+        )
+    two32 = shape(2, HALF, LANES, dtype=f32)
+    mine, give = call(
+        "deal", deal_kernel, [core, totals, even, over_z(odd, 4)], [two32, two32], [SMEM] + [VMEM] * 3
+    )
     came = lax.ppermute(give, "core", swap)
-    result = call(
+    result, totals = call(
         "last",
         last_kernel,
-        [core, mine, came],
-        shape(rdev, BLOCK, dtype=f32),
-        [SMEM, VMEM, VMEM],
-    )
-    my_totals = call(
-        "totals", totals_kernel, [ref, all_totals], shape(1, LANES, dtype=f32), [SMEM, VMEM]
-    )
-    return (result, my_totals[0, :rdev], evidence[:, 0])
+        [core, ref, mine, came],
+        [shape(rdev, BLOCK, dtype=f32), shape(1, LANES, dtype=f32)],
+        [SMEM, SMEM, VMEM, VMEM],
+    )
+    return (result, totals[0, :rdev], evidence[:, 0])
 
 
 def solution(mesh):

time: 468 us -> 135 us (0.29)
  blocking collectives: 288 us -> 0 us
  starting transfers between devices: 107 us -> 50.1 us
  waiting for transfers between devices: 46.1 us -> 56.7 us
    all_gather x1 -> x0, blocking collectives: 288 us -> none  [local(): all_totals = lax.all_gather(totals, CHIPS, axis=0, tiled=False)]
    ppermute x1, starting transfers between devices: 61.7 us -> 5.73 us  [local(): came = lax.ppermute(give, 'core', swap)]
    ppermute x18, waiting for transfers between devices: 30.9 us -> 41.1 us  [over(): return lax.ppermute(value, ('y_lo', 'x', 'core', 'y_hi'), pairs)]
  transfers between devices with their start and end apart: 28 -> 28, of which waited for: 20 -> 20; matrix products, arithmetic and copies ran while one was open for 0% -> 1% of each run, Pallas kernels for 1% -> 4%
where the time goes in v1:
time: 135 us; the launch traced here: 134 us
  waiting for transfers between devices  56.7 us (42%)
  starting transfers between devices  50.1 us (37%)
  Pallas kernels  20.5 us (15%)
  local copies, waits for them, and re-layouts  4.95 us (4%)
    ppermute x18, waiting for transfers between devices, over(): return lax.ppermute(value, ('y_lo', 'x', 'core', 'y_hi'), pairs)  41.1 us
    pallas_call x17, Pallas kernels, call(): pl.pallas_call(kernel, out_shape=outs, in_specs=specs or [VMEM] * len(ins...  20.5 us
    ppermute x6, starting transfers between devices, over_z(): return lax.ppermute(value, 'z', [(i, i ^ bits) for i in range(8)])  19.5 us
    ppermute x18, starting transfers between devices, over(): return lax.ppermute(value, ('y_lo', 'x', 'core', 'y_hi'), pairs)  17.8 us
    ppermute x6, waiting for transfers between devices, over_z(): return lax.ppermute(value, 'z', [(i, i ^ bits) for i in range(8)])  13.6 us
    ppermute x1, starting transfers between devices, local(): came = lax.ppermute(give, 'core', swap)  5.73 us
    ppermute x1, starting transfers between devices, local(): theirs = lax.ppermute(scores, 'core', swap)  4.81 us
    unnamed x12, local copies, waits for them, and re-layouts  4.44 us
  transfers between devices with their start and end apart: 28, of which 20 were waited for; matrix products, arithmetic and copies ran while one was open for 1% of the time, Pallas kernels for 4%

profile of v1, /device:TPU:1, one launch (start us, length us, event | category | flops | bytes accessed | tf_op | source)
XLA Modules:
  0.0 133.8 jit_solution(9273682914540091690)
XLA Ops:
  0.7 1.0 copy-done.2
  1.7 7.8 %collective-permute-start = (bf16[1,2,48,128]{3,2,1,0:T(8,128)(2,1)S(1)}, bf16[1,2,48,128]{3,2,1,0:T(8,128)(2,1)S(1)}, u32[]{:S(2)}, u32[]{:S(2)}) collective-permute-start(bf16[1,2,48,128]{3,2,1,0:T(8,128)(2,1)S(1)} %pack.1.own_ref), channel_id=1, source_target_pairs={{0,8},{2,10},{4,12},{6,14},{8,0},{10,2},{12,4},{14,6},{1,9},{3,11}... | collective-permute-start | bytes 73736 | tf_op jit(solution)/shard_map/ppermute | solution.py:26
  9.5 1.2 collective-permute-done.came_ref
  10.7 1.4 %copy-done = bf16[48,16384]{1,0:T(8,128)(2,1)S(1)} copy-done((bf16[48,16384]{1,0:T(8,128)(2,1)S(1)}, bf16[48,16384]{1,0:T(8,128)(2,1)}, u32[]{:S(2)}) %copy-start) | copy-done | bytes 1572888
  12.1 1.1 copy-done.1
  13.3 0.3 weighted.1
  13.6 2.1 %collective-permute-start.2 = (bf16[2,4,48,1024]{3,2,1,0:T(8,128)(2,1)S(1)}, bf16[2,4,48,1024]{3,2,1,0:T(8,128)(2,1)S(1)}, u32[]{:S(2)}, u32[]{:S(2)}) collective-permute-start(bf16[2,4,48,1024]{3,2,1,0:T(8,128)(2,1)S(1)} %get-tuple-element.38), channel_id=1, source_target_pairs={{0,16},{16,0},{1,17},{17,1},{2,18},{18,2},{3,19},{19,3},{4,20},{20... | collective-permute-start | bytes 2359304 | tf_op jit(solution)/shard_map/ppermute | solution.py:461
  15.7 1.3 collective-permute-start.1
  17.0 4.1 %collective-permute-done.1.came_ref = bf16[2,2,48,128]{3,2,1,0:T(8,128)(2,1)S(1)} collective-permute-done((bf16[2,2,48,128]{3,2,1,0:T(8,128)(2,1)S(1)}, bf16[2,2,48,128]{3,2,1,0:T(8,128)(2,1)S(1)}, u32[]{:S(2)}, u32[]{:S(2)}) %collective-permute-start.1) | collective-permute-done | bytes 49184 | tf_op jit(solution)/shard_map/ppermute | solution.py:26
  21.1 0.1 collective-permute-start.3
  21.2 0.8 copy.22.shifts_ref.args_8_
  22.0 2.8 %rotate.2.rest_0_.args_9_ = bf16[2,2,864,1024]{3,2,1,0:T(8,128)(2,1)S(1)} custom-call(s32[1]{0:T(128)} %bitcast.core_ref.args_0_, s32[1]{0:T(128)} %bitcast.2.x_ref.args_1_, s32[1]{0:T(128)} %bitcast.3.part_ref.args_2_, s32[9,2]{1,0:T(8,128)S(1)} %copy.22.shifts_ref.args_8_, bf16[2,4,48,1024]{3,2,1,0:T(8,128)(2,1)S(1)} %get-tuple-element.39.own_ref.args_9_, ...), custom_call_target="tpu_custom_call" | custom-call | flops 3000000 | bytes 9000000 | tf_op jit(solution)/shard_map/rotate/pallas_call | solution.py:413
  24.9 0.9 collective-permute-start.4
  25.8 2.5 %collective-permute-start.5 = (bf16[8,2,48,128]{3,2,1,0:T(8,128)(2,1)S(1)}, bf16[8,2,48,128]{3,2,1,0:T(8,128)(2,1)S(1)}, u32[]{:S(2)}, u32[]{:S(2)}) collective-permute-start(bf16[8,2,48,128]{3,2,1,0:T(8,128)(2,1)S(1)} %stack.17.own_ref), channel_id=1, source_target_pairs={{0,1},{1,0},{16,80},{17,81},{32,33},{33,32},{48,112},{49,113},{64,... | collective-permute-start | bytes 589832 | tf_op jit(solution)/shard_map/ppermute | solution.py:41
  28.2 0.6 collective-permute-start.6
  28.8 2.8 %rotate.3.rot_ref.args_10_ = bf16[2,2,864,1024]{3,2,1,0:T(8,128)(2,1)S(1)} custom-call(s32[1]{0:T(128)} %bitcast.core_ref.args_0_, s32[1]{0:T(128)} %bitcast.2.x_ref.args_1_, s32[1]{0:T(128)} %bitcast.3.part_ref.args_2_, s32[9,2]{1,0:T(8,128)S(1)} %copy.22.shifts_ref.args_8_, bf16[2,4,48,1024]{3,2,1,0:T(8,128)(2,1)S(1)} %get-tuple-element.39.own_ref.args_9_, ...), custom_call_target="tpu_custom_call" | custom-call | flops 3000000 | bytes 9000000 | tf_op jit(solution)/shard_map/rotate/pallas_call | solution.py:413
  31.6 1.9 %collective-permute-done.5.two_ref = bf16[8,2,48,128]{3,2,1,0:T(8,128)(2,1)S(1)} collective-permute-done((bf16[8,2,48,128]{3,2,1,0:T(8,128)(2,1)S(1)}, bf16[8,2,48,128]{3,2,1,0:T(8,128)(2,1)S(1)}, u32[]{:S(2)}, u32[]{:S(2)}) %collective-permute-start.5) | collective-permute-done | bytes 196640 | tf_op jit(solution)/shard_map/ppermute | solution.py:41
  33.5 2.3 %collective-permute-done.6.three_ref = bf16[8,2,48,128]{3,2,1,0:T(8,128)(2,1)S(1)} collective-permute-done((bf16[8,2,48,128]{3,2,1,0:T(8,128)(2,1)S(1)}, bf16[8,2,48,128]{3,2,1,0:T(8,128)(2,1)S(1)}, u32[]{:S(2)}, u32[]{:S(2)}) %collective-permute-start.6) | collective-permute-done | bytes 196640 | tf_op jit(solution)/shard_map/ppermute | solution.py:41
  35.8 0.1 join.1
  35.9 2.8 %collective-permute-start.10 = (bf16[2,8,2,48,128]{4,3,2,1,0:T(8,128)(2,1)S(1)}, bf16[2,8,2,48,128]{4,3,2,1,0:T(8,128)(2,1)S(1)}, u32[]{:S(2)}, u32[]{:S(2)}) collective-permute-start(bf16[2,8,2,48,128]{4,3,2,1,0:T(8,128)(2,1)S(1)} %get-tuple-element.41.args_2_), channel_id=1, source_target_pairs={{0,96},{1,97},{16,145},{17,144},{32,64},{33,65},{48,177},{49,176},... | collective-permute-start | bytes 1179656 | tf_op jit(solution)/shard_map/ppermute | solution.py:41
  38.7 0.3 collective-permute-start.12
  39.0 1.1 collective-permute-start.8
  40.1 4.0 %collective-permute-done.10.args_8_ = bf16[2,8,2,48,128]{4,3,2,1,0:T(8,128)(2,1)S(1)} collective-permute-done((bf16[2,8,2,48,128]{4,3,2,1,0:T(8,128)(2,1)S(1)}, bf16[2,8,2,48,128]{4,3,2,1,0:T(8,128)(2,1)S(1)}, u32[]{:S(2)}, u32[]{:S(2)}) %collective-permute-start.10) | collective-permute-done | bytes 393248 | tf_op jit(solution)/shard_map/ppermute | solution.py:41
  44.1 1.5 %collective-permute-done.7.args_3_ = bf16[2,8,2,48,128]{4,3,2,1,0:T(8,128)(2,1)S(1)} collective-permute-done((bf16[2,8,2,48,128]{4,3,2,1,0:T(8,128)(2,1)S(1)}, bf16[2,8,2,48,128]{4,3,2,1,0:T(8,128)(2,1)S(1)}, u32[]{:S(2)}, u32[]{:S(2)}) %collective-permute-start.7) | collective-permute-done | bytes 393248 | tf_op jit(solution)/shard_map/ppermute | solution.py:41
  45.6 1.2 collective-permute-start.9
  46.8 1.5 %collective-permute-done.12.args_7_ = bf16[2,8,2,48,128]{4,3,2,1,0:T(8,128)(2,1)S(1)} collective-permute-done((bf16[2,8,2,48,128]{4,3,2,1,0:T(8,128)(2,1)S(1)}, bf16[2,8,2,48,128]{4,3,2,1,0:T(8,128)(2,1)S(1)}, u32[]{:S(2)}, u32[]{:S(2)}) %collective-permute-start.12) | collective-permute-done | bytes 393248 | tf_op jit(solution)/shard_map/ppermute | solution.py:41
  48.3 1.5 %collective-permute-done.8.args_4_ = bf16[2,8,2,48,128]{4,3,2,1,0:T(8,128)(2,1)S(1)} collective-permute-done((bf16[2,8,2,48,128]{4,3,2,1,0:T(8,128)(2,1)S(1)}, bf16[2,8,2,48,128]{4,3,2,1,0:T(8,128)(2,1)S(1)}, u32[]{:S(2)}, u32[]{:S(2)}) %collective-permute-start.8) | collective-permute-done | bytes 393248 | tf_op jit(solution)/shard_map/ppermute | solution.py:41
  49.8 4.2 %collective-permute-done.11.args_6_ = bf16[2,8,2,48,128]{4,3,2,1,0:T(8,128)(2,1)S(1)} collective-permute-done((bf16[2,8,2,48,128]{4,3,2,1,0:T(8,128)(2,1)S(1)}, bf16[2,8,2,48,128]{4,3,2,1,0:T(8,128)(2,1)S(1)}, u32[]{:S(2)}, u32[]{:S(2)}) %collective-permute-start.11) | collective-permute-done | bytes 393248 | tf_op jit(solution)/shard_map/ppermute | solution.py:41
  54.0 4.2 %forward.1.args_5_ = f32[864,256]{1,0:T(8,128)S(1)} custom-call(s32[1]{0:T(128)} %bitcast.core_ref.args_0_, bf16[2,8,2,48,128]{4,3,2,1,0:T(8,128)(2,1)S(1)} %get-tuple-element.40.args_1_, bf16[2,8,2,48,128]{4,3,2,1,0:T(8,128)(2,1)S(1)} %get-tuple-element.41.args_2_, bf16[2,8,2,48,128]{4,3,2,1,0:T(8,128)(2,1)S(1)} %collective-permute-done.7.args_3_, ...), custom_call_target="tpu_custom_call" | custom-call | flops 4000000 | bytes 12000000 | tf_op jit(solution)/shard_map/forward/pallas_call | solution.py:413
  58.3 4.8 %collective-permute-start.13 = (f32[864,256]{1,0:T(8,128)S(1)}, f32[864,256]{1,0:T(8,128)S(1)}, u32[]{:S(2)}, u32[]{:S(2)}) collective-permute-start(f32[864,256]{1,0:T(8,128)S(1)} %forward.1.args_5_), channel_id=1, source_target_pairs={{0,16},{16,0},{1,17},{17,1},{2,18},{18,2},{3,19},{19,3},{4,20},{20... | collective-permute-start | bytes 2654216 | tf_op jit(solution)/shard_map/ppermute | solution.py:513
  63.1 0.1 copy.24
  63.2 0.1 fusion
  63.3 0.1 fusion.1
  63.4 1.8 %collective-permute-done.14 = s32[48,12]{1,0:T(8,128)S(1)} collective-permute-done((s32[48,12]{1,0:T(8,128)S(1)}, s32[48,12]{1,0:T(8,128)S(1)}, u32[]{:S(2)}, u32[]{:S(2)}) %collective-permute-start.14) | collective-permute-done | bytes 2336 | tf_op jit(solution)/shard_map/ppermute | solution.py:464
  65.2 9.1 %backward.1 = (f32[4,8,2,48,128]{4,3,2,1,0:T(8,128)S(1)}, bf16[33,48,128]{2,1,0:T(8,128)(2,1)S(1)}, bf16[33,48,128]{2,1,0:T(8,128)(2,1)S(1)}, bf16[32,48,128]{2,...) custom-call(s32[1]{0:T(128)} %bitcast.core_ref.args_0_, ...), custom_call_target="tpu_custom_call" | custom-call | flops 10000000 | bytes 30000000 | tf_op jit(solution)/shard_map/backward/pallas_call | solution.py:413
  74.3 0.1 collective-permute-start.15
  74.4 0.1 collective-permute-start.16
  74.5 8.2 %collective-permute-done.15.far_three = bf16[33,48,128]{2,1,0:T(8,128)(2,1)S(1)} collective-permute-done((bf16[33,48,128]{2,1,0:T(8,128)(2,1)S(1)}, bf16[33,48,128]{2,1,0:T(8,128)(2,1)S(1)}, u32[]{:S(2)}, u32[]{:S(2)}) %collective-permute-start.15) | collective-permute-done | bytes 405536 | tf_op jit(solution)/shard_map/ppermute | solution.py:41
  82.6 0.1 add.12
  82.8 0.1 collective-permute-start.18
  82.9 1.5 %collective-permute-start.17 = (bf16[32,48,128]{2,1,0:T(8,128)(2,1)S(1)}, bf16[32,48,128]{2,1,0:T(8,128)(2,1)S(1)}, u32[]{:S(2)}, u32[]{:S(2)}) collective-permute-start(bf16[32,48,128]{2,1,0:T(8,128)(2,1)S(1)} %get-tuple-element.50), channel_id=1, source_target_pairs={{0,32},{1,33},{16,144},{17,145},{32,0},{33,1},{48,176},{49,177},{6... | collective-permute-start | bytes 1179656 | tf_op jit(solution)/shard_map/ppermute | solution.py:41
  84.3 1.2 collective-permute-start.20
  85.5 1.5 %collective-permute-start.19 = (bf16[32,48,128]{2,1,0:T(8,128)(2,1)S(1)}, bf16[32,48,128]{2,1,0:T(8,128)(2,1)S(1)}, u32[]{:S(2)}, u32[]{:S(2)}) collective-permute-start(bf16[32,48,128]{2,1,0:T(8,128)(2,1)S(1)} %get-tuple-element.52), channel_id=1, source_target_pairs={{0,96},{1,97},{16,145},{17,144},{32,64},{33,65},{48,177},{49,176},... | collective-permute-start | bytes 1179656 | tf_op jit(solution)/shard_map/ppermute | solution.py:41
  87.0 7.1 %collective-permute-done.17.one_low = bf16[32,48,128]{2,1,0:T(8,128)(2,1)S(1)} collective-permute-done((bf16[32,48,128]{2,1,0:T(8,128)(2,1)S(1)}, bf16[32,48,128]{2,1,0:T(8,128)(2,1)S(1)}, u32[]{:S(2)}, u32[]{:S(2)}) %collective-permute-start.17) | collective-permute-done | bytes 393248 | tf_op jit(solution)/shard_map/ppermute | solution.py:41
  94.1 2.5 %collective-permute-done.19.three_low = bf16[32,48,128]{2,1,0:T(8,128)(2,1)S(1)} collective-permute-done((bf16[32,48,128]{2,1,0:T(8,128)(2,1)S(1)}, bf16[32,48,128]{2,1,0:T(8,128)(2,1)S(1)}, u32[]{:S(2)}, u32[]{:S(2)}) %collective-permute-start.19) | collective-permute-done | bytes 393248 | tf_op jit(solution)/shard_map/ppermute | solution.py:41
  96.7 0.2 middle.1
  96.9 0.1 collective-permute-start.21
  97.0 2.3 %collective-permute-start.22 = (bf16[17,48,128]{2,1,0:T(8,128)(2,1)S(1)}, bf16[17,48,128]{2,1,0:T(8,128)(2,1)S(1)}, u32[]{:S(2)}, u32[]{:S(2)}) collective-permute-start(bf16[17,48,128]{2,1,0:T(8,128)(2,1)S(1)} %get-tuple-element.57), channel_id=1, source_target_pairs={{0,1},{1,0},{16,80},{17,81},{32,33},{33,32},{48,112},{49,113},{64,... | collective-permute-start | bytes 626696 | tf_op jit(solution)/shard_map/ppermute | solution.py:41
  99.3 1.5 %collective-permute-start.23 = (bf16[17,48,128]{2,1,0:T(8,128)(2,1)S(1)}, bf16[17,48,128]{2,1,0:T(8,128)(2,1)S(1)}, u32[]{:S(2)}, u32[]{:S(2)}) collective-permute-start(bf16[17,48,128]{2,1,0:T(8,128)(2,1)S(1)} %get-tuple-element.58), channel_id=1, source_target_pairs={{0,129},{1,128},{16,112},{17,113},{32,161},{33,160},{48,80},{49,81... | collective-permute-start | bytes 626696 | tf_op jit(solution)/shard_map/ppermute | solution.py:41
  100.9 0.8 collective-permute-done.21.one
  101.7 3.4 %collective-permute-done.22.two = bf16[17,48,128]{2,1,0:T(8,128)(2,1)S(1)} collective-permute-done((bf16[17,48,128]{2,1,0:T(8,128)(2,1)S(1)}, bf16[17,48,128]{2,1,0:T(8,128)(2,1)S(1)}, u32[]{:S(2)}, u32[]{:S(2)}) %collective-permute-start.22) | collective-permute-done | bytes 208928 | tf_op jit(solution)/shard_map/ppermute | solution.py:41
  105.1 2.2 %collective-permute-done.23.three = bf16[17,48,128]{2,1,0:T(8,128)(2,1)S(1)} collective-permute-done((bf16[17,48,128]{2,1,0:T(8,128)(2,1)S(1)}, bf16[17,48,128]{2,1,0:T(8,128)(2,1)S(1)}, u32[]{:S(2)}, u32[]{:S(2)}) %collective-permute-start.23) | collective-permute-done | bytes 208928 | tf_op jit(solution)/shard_map/ppermute | solution.py:41
  107.3 0.1 late.1
  107.4 1.2 collective-permute-start.24
  108.6 2.5 %collective-permute-done.24.came = bf16[9,48,128]{2,1,0:T(8,128)(2,1)S(1)} collective-permute-done((bf16[9,48,128]{2,1,0:T(8,128)(2,1)S(1)}, bf16[9,48,128]{2,1,0:T(8,128)(2,1)S(1)}, u32[]{:S(2)}, u32[]{:S(2)}) %collective-permute-start.24) | collective-permute-done | bytes 110624 | tf_op jit(solution)/shard_map/ppermute | solution.py:26
  111.1 1.7 %collective-permute-start.25 = (f32[5,48,128]{2,1,0:T(8,128)S(1)}, f32[5,48,128]{2,1,0:T(8,128)S(1)}, u32[]{:S(2)}, u32[]{:S(2)}) collective-permute-start(f32[5,48,128]{2,1,0:T(8,128)S(1)} %get-tuple-element.64), channel_id=1, source_target_pairs={{0,4},{2,6},{4,0},{6,2},{8,12},{10,14},{12,8},{14,10},{1,5},{3,7},... | collective-permute-start | bytes 368648 | tf_op jit(solution)/shard_map/ppermute | solution.py:26
  112.8 3.5 %collective-permute-done.25.came = f32[5,48,128]{2,1,0:T(8,128)S(1)} collective-permute-done((f32[5,48,128]{2,1,0:T(8,128)S(1)}, f32[5,48,128]{2,1,0:T(8,128)S(1)}, u32[]{:S(2)}, u32[]{:S(2)}) %collective-permute-start.25) | collective-permute-done | bytes 122912 | tf_op jit(solution)/shard_map/ppermute | solution.py:26
  116.3 7.4 %collective-permute-start.26 = (f32[3,48,128]{2,1,0:T(8,128)S(1)}, f32[3,48,128]{2,1,0:T(8,128)S(1)}, u32[]{:S(2)}, u32[]{:S(2)}) collective-permute-start(f32[3,48,128]{2,1,0:T(8,128)S(1)} %get-tuple-element.67), channel_id=1, source_target_pairs={{0,8},{2,10},{4,12},{6,14},{8,0},{10,2},{12,4},{14,6},{1,9},{3,11}... | collective-permute-start | bytes 221192 | tf_op jit(solution)/shard_map/ppermute | solution.py:26
  123.8 2.3 %collective-permute-done.26.came = f32[3,48,128]{2,1,0:T(8,128)S(1)} collective-permute-done((f32[3,48,128]{2,1,0:T(8,128)S(1)}, f32[3,48,128]{2,1,0:T(8,128)S(1)}, u32[]{:S(2)}, u32[]{:S(2)}) %collective-permute-start.26) | collective-permute-done | bytes 73760 | tf_op jit(solution)/shard_map/ppermute | solution.py:26
  126.0 5.7 %collective-permute-start.27 = (f32[2,48,128]{2,1,0:T(8,128)S(1)}, f32[2,48,128]{2,1,0:T(8,128)S(1)}, u32[]{:S(2)}, u32[]{:S(2)}) collective-permute-start(f32[2,48,128]{2,1,0:T(8,128)S(1)} %get-tuple-element.69), channel_id=1, source_target_pairs={{0,16},{16,0},{1,17},{17,1},{2,18},{18,2},{3,19},{19,3},{4,20},{20... | collective-permute-start | bytes 147464 | tf_op jit(solution)/shard_map/ppermute | solution.py:572
  131.8 0.6 reduce
  132.4 0.3 collective-permute-done.27.came_ref
  132.6 0.6 last.1
  133.3 0.5 slice_bitcast_fusion
  (26 shorter events, 0.2 us)
Async XLA Ops:
  0.6 1.0 copy-start.2
  1.7 9.0 %collective-permute-start = (bf16[1,2,48,128]{3,2,1,0:T(8,128)(2,1)S(1)}, bf16[1,2,48,128]{3,2,1,0:T(8,128)(2,1)S(1)}, u32[]{:S(2)}, u32[]{:S(2)}) collective-permute-start(bf16[1,2,48,128]{3,2,1,0:T(8,128)(2,1)S(1)} %pack.1.own_ref), channel_id=1, source_target_pairs={{0,8},{2,10},{4,12},{6,14},{8,0},{10,2},{12,4},{14,6},{1,9},{3,11}... | collective-permute-start | bytes 73736 | tf_op jit(solution)/shard_map/ppermute | solution.py:26
  10.7 1.4 %copy-start = (bf16[48,16384]{1,0:T(8,128)(2,1)S(1)}, bf16[48,16384]{1,0:T(8,128)(2,1)}, u32[]{:S(2)}) copy-start(bf16[48,16384]{1,0:T(8,128)(2,1)} %images_ref.1) | copy-start | bytes 4718596
  12.1 1.1 copy-start.1
  13.6 7.5 %collective-permute-start.2 = (bf16[2,4,48,1024]{3,2,1,0:T(8,128)(2,1)S(1)}, bf16[2,4,48,1024]{3,2,1,0:T(8,128)(2,1)S(1)}, u32[]{:S(2)}, u32[]{:S(2)}) collective-permute-start(bf16[2,4,48,1024]{3,2,1,0:T(8,128)(2,1)S(1)} %get-tuple-element.38), channel_id=1, source_target_pairs={{0,16},{16,0},{1,17},{17,1},{2,18},{18,2},{3,19},{19,3},{4,20},{20... | collective-permute-start | bytes 2359304 | tf_op jit(solution)/shard_map/ppermute | solution.py:461
  15.7 5.4 %collective-permute-start.1 = (bf16[2,2,48,128]{3,2,1,0:T(8,128)(2,1)S(1)}, bf16[2,2,48,128]{3,2,1,0:T(8,128)(2,1)S(1)}, u32[]{:S(2)}, u32[]{:S(2)}) collective-permute-start(bf16[2,2,48,128]{3,2,1,0:T(8,128)(2,1)S(1)} %stack.15.packed_ref.own_ref), channel_id=1, source_target_pairs={{0,4},{2,6},{4,0},{6,2},{8,12},{10,14},{12,8},{14,10},{1,5},{3,7},... | collective-permute-start | bytes 147464 | tf_op jit(solution)/shard_map/ppermute | solution.py:26
  21.1 3.7 %collective-permute-start.3 = (bf16[4,2,48,128]{3,2,1,0:T(8,128)(2,1)S(1)}, bf16[4,2,48,128]{3,2,1,0:T(8,128)(2,1)S(1)}, u32[]{:S(2)}, u32[]{:S(2)}) collective-permute-start(bf16[4,2,48,128]{3,2,1,0:T(8,128)(2,1)S(1)} %stack.16.own_ref), channel_id=1, source_target_pairs={{0,2},{2,0},{4,6},{6,4},{8,10},{10,8},{12,14},{14,12},{1,3},{3,1},... | collective-permute-start | bytes 294920 | tf_op jit(solution)/shard_map/ppermute | solution.py:26
  24.9 6.8 %collective-permute-start.4 = (bf16[8,2,48,128]{3,2,1,0:T(8,128)(2,1)S(1)}, bf16[8,2,48,128]{3,2,1,0:T(8,128)(2,1)S(1)}, u32[]{:S(2)}, u32[]{:S(2)}) collective-permute-start(bf16[8,2,48,128]{3,2,1,0:T(8,128)(2,1)S(1)} %stack.17.own_ref), channel_id=1, source_target_pairs={{0,128},{1,129},{16,48},{17,49},{32,160},{33,161},{48,16},{49,17},... | collective-permute-start | bytes 589832 | tf_op jit(solution)/shard_map/ppermute | solution.py:41
  25.8 7.7 %collective-permute-start.5 = (bf16[8,2,48,128]{3,2,1,0:T(8,128)(2,1)S(1)}, bf16[8,2,48,128]{3,2,1,0:T(8,128)(2,1)S(1)}, u32[]{:S(2)}, u32[]{:S(2)}) collective-permute-start(bf16[8,2,48,128]{3,2,1,0:T(8,128)(2,1)S(1)} %stack.17.own_ref), channel_id=1, source_target_pairs={{0,1},{1,0},{16,80},{17,81},{32,33},{33,32},{48,112},{49,113},{64,... | collective-permute-start | bytes 589832 | tf_op jit(solution)/shard_map/ppermute | solution.py:41
  28.2 7.6 %collective-permute-start.6 = (bf16[8,2,48,128]{3,2,1,0:T(8,128)(2,1)S(1)}, bf16[8,2,48,128]{3,2,1,0:T(8,128)(2,1)S(1)}, u32[]{:S(2)}, u32[]{:S(2)}) collective-permute-start(bf16[8,2,48,128]{3,2,1,0:T(8,128)(2,1)S(1)} %stack.17.own_ref), channel_id=1, source_target_pairs={{0,129},{1,128},{16,112},{17,113},{32,161},{33,160},{48,80},{49,81... | collective-permute-start | bytes 589832 | tf_op jit(solution)/shard_map/ppermute | solution.py:41
  35.9 8.3 %collective-permute-start.10 = (bf16[2,8,2,48,128]{4,3,2,1,0:T(8,128)(2,1)S(1)}, bf16[2,8,2,48,128]{4,3,2,1,0:T(8,128)(2,1)S(1)}, u32[]{:S(2)}, u32[]{:S(2)}) collective-permute-start(bf16[2,8,2,48,128]{4,3,2,1,0:T(8,128)(2,1)S(1)} %get-tuple-element.41.args_2_), channel_id=1, source_target_pairs={{0,96},{1,97},{16,145},{17,144},{32,64},{33,65},{48,177},{49,176},... | collective-permute-start | bytes 1179656 | tf_op jit(solution)/shard_map/ppermute | solution.py:41
  38.7 24.4 %copy-start.3 = (s32[48,12]{0,1:T(8,128)S(1)}, s32[48,12]{0,1:T(8,128)}, u32[]{:S(2)}) copy-start(s32[48,12]{0,1:T(8,128)} %param.10) | copy-start | bytes 6916
  38.7 24.5 %copy-start.4 = (s32[48]{0:T(128)S(1)}, s32[48]{0:T(128)}, u32[]{:S(2)}) copy-start(s32[48]{0:T(128)} %param.11) | copy-start | bytes 580
  38.7 6.9 %collective-permute-start.7 = (bf16[2,8,2,48,128]{4,3,2,1,0:T(8,128)(2,1)S(1)}, bf16[2,8,2,48,128]{4,3,2,1,0:T(8,128)(2,1)S(1)}, u32[]{:S(2)}, u32[]{:S(2)}) collective-permute-start(bf16[2,8,2,48,128]{4,3,2,1,0:T(8,128)(2,1)S(1)} %get-tuple-element.40.args_1_), channel_id=1, source_target_pairs={{0,32},{1,33},{16,144},{17,145},{32,0},{33,1},{48,176},{49,177},{6... | collective-permute-start | bytes 1179656 | tf_op jit(solution)/shard_map/ppermute | solution.py:41
  38.7 9.7 %collective-permute-start.12 = (bf16[2,8,2,48,128]{4,3,2,1,0:T(8,128)(2,1)S(1)}, bf16[2,8,2,48,128]{4,3,2,1,0:T(8,128)(2,1)S(1)}, u32[]{:S(2)}, u32[]{:S(2)}) collective-permute-start(bf16[2,8,2,48,128]{4,3,2,1,0:T(8,128)(2,1)S(1)} %get-tuple-element.40.args_1_), channel_id=1, source_target_pairs={{0,96},{1,97},{16,145},{17,144},{32,64},{33,65},{48,177},{49,176},... | collective-permute-start | bytes 1179656 | tf_op jit(solution)/shard_map/ppermute | solution.py:41
  39.0 10.8 %collective-permute-start.8 = (bf16[2,8,2,48,128]{4,3,2,1,0:T(8,128)(2,1)S(1)}, bf16[2,8,2,48,128]{4,3,2,1,0:T(8,128)(2,1)S(1)}, u32[]{:S(2)}, u32[]{:S(2)}) collective-permute-start(bf16[2,8,2,48,128]{4,3,2,1,0:T(8,128)(2,1)S(1)} %get-tuple-element.41.args_2_), channel_id=1, source_target_pairs={{0,32},{1,33},{16,144},{17,145},{32,0},{33,1},{48,176},{49,177},{6... | collective-permute-start | bytes 1179656 | tf_op jit(solution)/shard_map/ppermute | solution.py:41
  44.1 9.9 %collective-permute-start.11 = (bf16[2,8,2,48,128]{4,3,2,1,0:T(8,128)(2,1)S(1)}, bf16[2,8,2,48,128]{4,3,2,1,0:T(8,128)(2,1)S(1)}, u32[]{:S(2)}, u32[]{:S(2)}) collective-permute-start(bf16[2,8,2,48,128]{4,3,2,1,0:T(8,128)(2,1)S(1)} %collective-permute-done.10.args_8_), channel_id=1, source_target_pairs={{0,32},{1,33},{16,144},{17,145},{32,0},{33,1},{48,176},{49,177},{6... | collective-permute-start | bytes 1179656 | tf_op jit(solution)/shard_map/ppermute | solution.py:41
  45.6 8.4 %collective-permute-start.9 = (bf16[2,8,2,48,128]{4,3,2,1,0:T(8,128)(2,1)S(1)}, bf16[2,8,2,48,128]{4,3,2,1,0:T(8,128)(2,1)S(1)}, u32[]{:S(2)}, u32[]{:S(2)}) collective-permute-start(bf16[2,8,2,48,128]{4,3,2,1,0:T(8,128)(2,1)S(1)} %collective-permute-done.7.args_3_), channel_id=1, source_target_pairs={{0,96},{1,97},{16,145},{17,144},{32,64},{33,65},{48,177},{49,176},... | collective-permute-start | bytes 1179656 | tf_op jit(solution)/shard_map/ppermute | solution.py:41
  58.3 6.9 %collective-permute-start.13 = (f32[864,256]{1,0:T(8,128)S(1)}, f32[864,256]{1,0:T(8,128)S(1)}, u32[]{:S(2)}, u32[]{:S(2)}) collective-permute-start(f32[864,256]{1,0:T(8,128)S(1)} %forward.1.args_5_), channel_id=1, source_target_pairs={{0,16},{16,0},{1,17},{17,1},{2,18},{18,2},{3,19},{19,3},{4,20},{20... | collective-permute-start | bytes 2654216 | tf_op jit(solution)/shard_map/ppermute | solution.py:513
  63.3 1.9 %collective-permute-start.14 = (s32[48,12]{1,0:T(8,128)S(1)}, s32[48,12]{1,0:T(8,128)S(1)}, u32[]{:S(2)}, u32[]{:S(2)}) collective-permute-start(s32[48,12]{1,0:T(8,128)S(1)} %fusion), channel_id=1, source_target_pairs={{0,16},{16,0},{1,17},{17,1},{2,18},{18,2},{3,19},{19,3},{4,20},{20... | collective-permute-start | bytes 6920 | tf_op jit(solution)/shard_map/ppermute | solution.py:464
  74.3 8.4 %collective-permute-start.15 = (bf16[33,48,128]{2,1,0:T(8,128)(2,1)S(1)}, bf16[33,48,128]{2,1,0:T(8,128)(2,1)S(1)}, u32[]{:S(2)}, u32[]{:S(2)}) collective-permute-start(bf16[33,48,128]{2,1,0:T(8,128)(2,1)S(1)} %get-tuple-element.44), channel_id=1, source_target_pairs={{0,96},{1,97},{16,145},{17,144},{32,64},{33,65},{48,177},{49,176},... | collective-permute-start | bytes 1216520 | tf_op jit(solution)/shard_map/ppermute | solution.py:41
  74.4 8.2 %collective-permute-start.16 = (bf16[33,48,128]{2,1,0:T(8,128)(2,1)S(1)}, bf16[33,48,128]{2,1,0:T(8,128)(2,1)S(1)}, u32[]{:S(2)}, u32[]{:S(2)}) collective-permute-start(bf16[33,48,128]{2,1,0:T(8,128)(2,1)S(1)} %get-tuple-element.46), channel_id=1, source_target_pairs={{0,32},{1,33},{16,144},{17,145},{32,0},{33,1},{48,176},{49,177},{6... | collective-permute-start | bytes 1216520 | tf_op jit(solution)/shard_map/ppermute | solution.py:41
  82.8 13.9 %collective-permute-start.18 = (bf16[33,48,128]{2,1,0:T(8,128)(2,1)S(1)}, bf16[33,48,128]{2,1,0:T(8,128)(2,1)S(1)}, u32[]{:S(2)}, u32[]{:S(2)}) collective-permute-start(bf16[33,48,128]{2,1,0:T(8,128)(2,1)S(1)} %get-tuple-element.51), channel_id=1, source_target_pairs={{0,32},{1,33},{16,144},{17,145},{32,0},{33,1},{48,176},{49,177},{6... | collective-permute-start | bytes 1216520 | tf_op jit(solution)/shard_map/ppermute | solution.py:41
  82.9 11.3 %collective-permute-start.17 = (bf16[32,48,128]{2,1,0:T(8,128)(2,1)S(1)}, bf16[32,48,128]{2,1,0:T(8,128)(2,1)S(1)}, u32[]{:S(2)}, u32[]{:S(2)}) collective-permute-start(bf16[32,48,128]{2,1,0:T(8,128)(2,1)S(1)} %get-tuple-element.50), channel_id=1, source_target_pairs={{0,32},{1,33},{16,144},{17,145},{32,0},{33,1},{48,176},{49,177},{6... | collective-permute-start | bytes 1179656 | tf_op jit(solution)/shard_map/ppermute | solution.py:41
  84.3 9.8 %collective-permute-start.20 = (bf16[32,48,128]{2,1,0:T(8,128)(2,1)S(1)}, bf16[32,48,128]{2,1,0:T(8,128)(2,1)S(1)}, u32[]{:S(2)}, u32[]{:S(2)}) collective-permute-start(bf16[32,48,128]{2,1,0:T(8,128)(2,1)S(1)} %get-tuple-element.53), channel_id=1, source_target_pairs={{0,96},{1,97},{16,145},{17,144},{32,64},{33,65},{48,177},{49,176},... | collective-permute-start | bytes 1179656 | tf_op jit(solution)/shard_map/ppermute | solution.py:41
  85.5 11.2 %collective-permute-start.19 = (bf16[32,48,128]{2,1,0:T(8,128)(2,1)S(1)}, bf16[32,48,128]{2,1,0:T(8,128)(2,1)S(1)}, u32[]{:S(2)}, u32[]{:S(2)}) collective-permute-start(bf16[32,48,128]{2,1,0:T(8,128)(2,1)S(1)} %get-tuple-element.52), channel_id=1, source_target_pairs={{0,96},{1,97},{16,145},{17,144},{32,64},{33,65},{48,177},{49,176},... | collective-permute-start | bytes 1179656 | tf_op jit(solution)/shard_map/ppermute | solution.py:41
  96.9 4.7 %collective-permute-start.21 = (bf16[17,48,128]{2,1,0:T(8,128)(2,1)S(1)}, bf16[17,48,128]{2,1,0:T(8,128)(2,1)S(1)}, u32[]{:S(2)}, u32[]{:S(2)}) collective-permute-start(bf16[17,48,128]{2,1,0:T(8,128)(2,1)S(1)} %get-tuple-element.56), channel_id=1, source_target_pairs={{0,128},{1,129},{16,48},{17,49},{32,160},{33,161},{48,16},{49,17},... | collective-permute-start | bytes 626696 | tf_op jit(solution)/shard_map/ppermute | solution.py:41
  97.0 8.1 %collective-permute-start.22 = (bf16[17,48,128]{2,1,0:T(8,128)(2,1)S(1)}, bf16[17,48,128]{2,1,0:T(8,128)(2,1)S(1)}, u32[]{:S(2)}, u32[]{:S(2)}) collective-permute-start(bf16[17,48,128]{2,1,0:T(8,128)(2,1)S(1)} %get-tuple-element.57), channel_id=1, source_target_pairs={{0,1},{1,0},{16,80},{17,81},{32,33},{33,32},{48,112},{49,113},{64,... | collective-permute-start | bytes 626696 | tf_op jit(solution)/shard_map/ppermute | solution.py:41
  99.3 8.0 %collective-permute-start.23 = (bf16[17,48,128]{2,1,0:T(8,128)(2,1)S(1)}, bf16[17,48,128]{2,1,0:T(8,128)(2,1)S(1)}, u32[]{:S(2)}, u32[]{:S(2)}) collective-permute-start(bf16[17,48,128]{2,1,0:T(8,128)(2,1)S(1)} %get-tuple-element.58), channel_id=1, source_target_pairs={{0,129},{1,128},{16,112},{17,113},{32,161},{33,160},{48,80},{49,81... | collective-permute-start | bytes 626696 | tf_op jit(solution)/shard_map/ppermute | solution.py:41
  107.4 3.7 %collective-permute-start.24 = (bf16[9,48,128]{2,1,0:T(8,128)(2,1)S(1)}, bf16[9,48,128]{2,1,0:T(8,128)(2,1)S(1)}, u32[]{:S(2)}, u32[]{:S(2)}) collective-permute-start(bf16[9,48,128]{2,1,0:T(8,128)(2,1)S(1)} %get-tuple-element.61), channel_id=1, source_target_pairs={{0,2},{2,0},{4,6},{6,4},{8,10},{10,8},{12,14},{14,12},{1,3},{3,1},... | collective-permute-start | bytes 331784 | tf_op jit(solution)/shard_map/ppermute | solution.py:26
  111.1 5.2 %collective-permute-start.25 = (f32[5,48,128]{2,1,0:T(8,128)S(1)}, f32[5,48,128]{2,1,0:T(8,128)S(1)}, u32[]{:S(2)}, u32[]{:S(2)}) collective-permute-start(f32[5,48,128]{2,1,0:T(8,128)S(1)} %get-tuple-element.64), channel_id=1, source_target_pairs={{0,4},{2,6},{4,0},{6,2},{8,12},{10,14},{12,8},{14,10},{1,5},{3,7},... | collective-permute-start | bytes 368648 | tf_op jit(solution)/shard_map/ppermute | solution.py:26
  116.3 9.7 %collective-permute-start.26 = (f32[3,48,128]{2,1,0:T(8,128)S(1)}, f32[3,48,128]{2,1,0:T(8,128)S(1)}, u32[]{:S(2)}, u32[]{:S(2)}) collective-permute-start(f32[3,48,128]{2,1,0:T(8,128)S(1)} %get-tuple-element.67), channel_id=1, source_target_pairs={{0,8},{2,10},{4,12},{6,14},{8,0},{10,2},{12,4},{14,6},{1,9},{3,11}... | collective-permute-start | bytes 221192 | tf_op jit(solution)/shard_map/ppermute | solution.py:26
  126.0 6.6 %collective-permute-start.27 = (f32[2,48,128]{2,1,0:T(8,128)S(1)}, f32[2,48,128]{2,1,0:T(8,128)S(1)}, u32[]{:S(2)}, u32[]{:S(2)}) collective-permute-start(f32[2,48,128]{2,1,0:T(8,128)S(1)} %get-tuple-element.69), channel_id=1, source_target_pairs={{0,16},{16,0},{1,17},{17,1},{2,18},{18,2},{3,19},{19,3},{4,20},{20... | collective-permute-start | bytes 147464 | tf_op jit(solution)/shard_map/ppermute | solution.py:572

commit v2 on v1

--- a/solution.py
+++ b/solution.py
@@ -15,7 +15,7 @@
 GROUPS = SIDE // LANES
 HALF = 48
 CHUNK = 256
-STACKED = (0, 4, 2, 6, 1, 5, 3, 7)
+STACKED = (0, 4, 1, 5, 2, 6, 3, 7)
 EVERYONE = ("y_lo", "x", "core", "z", "y_hi")
 SMEM = pl.BlockSpec(memory_space=pltpu.SMEM)
 VMEM = pl.BlockSpec(memory_space=pltpu.VMEM)
@@ -50,11 +50,12 @@
         out_ref[0, p] = jnp.concatenate(tiles, axis=0).astype(jnp.bfloat16)
 
 
-def stack_kernel(own_ref, came_ref, *rest):
-    out_ref = rest[-1]
-    count = own_ref.shape[0]
-    out_ref[:count] = own_ref[...]
-    out_ref[count:] = came_ref[...]
+def stack_kernel(*args):
+    row = 0
+    for ref in args[:-2]:
+        count = ref.shape[0]
+        args[-1][row : row + count] = ref[...]
+        row += count
 
 
 def join_kernel(own_ref, one_ref, two_ref, three_ref, rot_ref, low_ref, high_ref):
@@ -64,7 +65,7 @@
     high_ref[1] = three_ref[...]
 
 
-def weighted_kernel(core_ref, x_ref, images_ref, ctf_ref, packed_ref, own_ref, other_ref):
+def weighted_kernel(core_ref, x_ref, images_ref, ctf_ref, before_ref, own_ref, other_ref):
     core, x = core_ref[0], x_ref[0]
     for out_ref, side in ((own_ref, core), (other_ref, 1 - core)):
         for xr in range(4):
@@ -244,8 +245,8 @@
 def backward_kernel(scale, *args):
     core_ref, x_ref, y_lo_ref, z_ref, y_hi_ref, mine_ref, theirs_ref, lists_ref = args[:8]
     shifts_ref, own_ref, recv_ref = args[8:11]
-    stays, far_low, far_high, one_low, one_high, three_low, three_high = args[11:18]
-    evidence_ref, totals_ref, weights_ref, rot_ref, sums_ref, cos_ref, sin_ref = args[18:]
+    stays, to_one, to_three, one_high, three_low = args[11:16]
+    evidence_ref, totals_ref, weights_ref, rot_ref, sums_ref, cos_ref, sin_ref = args[16:]
     core, x, y_lo, z, y_hi = core_ref[0], x_ref[0], y_lo_ref[0], z_ref[0], y_hi_ref[0]
     softmax(scale, z, y_hi, mine_ref, theirs_ref, lists_ref, weights_ref, evidence_ref)
     flipped = weights_ref[...].T
@@ -259,8 +260,8 @@
     totals_ref[1:2, : refs_all - LANES] = totals[:, LANES:]
     parts = three_parts(totals_ref[...])
     totals_ref[...] = whole(parts)
-    far_low[32] = parts
-    far_high[32] = parts
+    to_one[64] = parts
+    to_three[64] = parts
     weights = flipped[:, :rows].astype(jnp.bfloat16)
     low = low_rows()
 
@@ -305,29 +306,31 @@
     lax.fori_loop(0, 8, step, 0)
     for place in range(4):
         stays[place] = sums_ref[0, place]
-        for distance, low_ref, high_ref in (
-            (2, far_low, far_high),
-            (1, one_low, one_high),
-            (3, three_low, three_high),
+        for distance, low_ref, low_at, high_ref, high_at in (
+            (2, to_one, 0, to_three, 0),
+            (1, to_one, 32, one_high, 0),
+            (3, three_low, 0, to_three, 32),
         ):
             for k in range(4):
                 for p in range(2):
                     at = 8 * place + 2 * k + p
-                    low_ref[at] = sums_ref[distance, place, k, p].astype(low_ref.dtype)
-                    high_ref[at] = sums_ref[distance, place, 4 + k, p].astype(high_ref.dtype)
+                    low = sums_ref[distance, place, k, p]
+                    high = sums_ref[distance, place, 4 + k, p]
+                    low_ref[low_at + at] = low.astype(low_ref.dtype)
+                    high_ref[high_at + at] = high.astype(high_ref.dtype)
 
 
 def add_kernel(
-    totals_ref, one_ref, far_three, three_ref, far_one, one_out, three_out, both_ref, third_ref
+    totals_ref, one_ref, three_ref, from_one, from_three, one_out, three_out, both_ref, third_ref
 ):
-    one_out[0:32] = (one_ref[...] + far_three[0:32].astype(jnp.float32)).astype(jnp.bfloat16)
-    one_out[32] = far_three[32]
-    three_out[...] = (three_ref[...] + far_one[0:32].astype(jnp.float32)).astype(jnp.bfloat16)
-    both_ref[...] = totals_ref[...] + whole(far_one[32])
-    third_ref[...] = whole(far_three[32])
-
-
-def middle_kernel(both_ref, third_ref, stays, one_low, one_high, three_low, three_high, *outs):
+    one_out[0:32] = (one_ref[...] + from_three[0:32].astype(jnp.float32)).astype(jnp.bfloat16)
+    one_out[32] = from_three[64]
+    three_out[...] = (three_ref[...] + from_one[0:32].astype(jnp.float32)).astype(jnp.bfloat16)
+    both_ref[...] = totals_ref[...] + whole(from_one[64])
+    third_ref[...] = whole(from_three[64])
+
+
+def middle_kernel(both_ref, third_ref, stays, from_one, one_high, three_low, from_three, *outs):
     totals_ref = outs[-1]
     totals = both_ref[...] + (whole(one_high[32]) + third_ref[...])
     parts = three_parts(totals)
@@ -335,12 +338,15 @@
     for n, out_ref in enumerate(outs[:-1]):
         if n:
             out_ref[16] = parts
-        for ks, one, three in ((0, one_low, three_low), (4, one_high, three_high)):
+        for ks, one, one_at, three, three_at in (
+            (0, from_one, 32, three_low, 0),
+            (4, one_high, 0, from_three, 32),
+        ):
             for k in range(4):
                 for p in range(2):
                     at = 8 * n + 2 * k + p
-                    total = stays[n, ks + k, p] + one[at].astype(jnp.float32)
-                    total = total + three[at].astype(jnp.float32)
+                    total = stays[n, ks + k, p] + one[one_at + at].astype(jnp.float32)
+                    total = total + three[three_at + at].astype(jnp.float32)
                     out_ref[2 * (ks + k) + p] = total.astype(out_ref.dtype)
 
 
@@ -361,29 +367,21 @@
                 odd_ref[2 * (k // 2) + p] = total.astype(odd_ref.dtype)
 
 
-def halve_kernel(totals_ref, stays, came, even_ref, odd_ref, sum_ref):
-    count = stays.shape[0] // 2
-    last = came[2 * count]
-    if last.dtype == jnp.bfloat16:
-        totals = totals_ref[...] + whole(last)
-    else:
-        totals = totals_ref[...] + last[0:8]
+def halve_kernel(totals_ref, stays, came, own_ref, two_ref, four_ref, six_ref, sum_ref):
+    totals = totals_ref[...] + whole(came[8])
     sum_ref[...] = totals
-    odd_ref[count] = jnp.zeros((HALF, LANES), jnp.float32)
-    odd_ref[count, 0:8] = totals
-    for k in range(count):
+    for k, ref in enumerate((own_ref, two_ref, four_ref, six_ref)):
         for p in range(2):
-            total = stays[2 * k + p] + came[2 * k + p].astype(jnp.float32)
-            if k % 2 == 0:
-                even_ref[2 * (k // 2) + p] = total
-            else:
-                odd_ref[2 * (k // 2) + p] = total
-
-
-def deal_kernel(core_ref, totals_ref, stays, came, mine_ref, give_ref):
+            ref[p] = stays[2 * k + p] + came[2 * k + p].astype(jnp.float32)
+        if k:
+            ref[2] = jnp.zeros((HALF, LANES), jnp.float32)
+            ref[2, 0:8] = totals
+
+
+def deal_kernel(core_ref, totals_ref, stays, two, four, six, mine_ref, give_ref):
     first = core_ref[0] == 0
-    low, high = stays[0] + came[0], stays[1] + came[1]
-    totals = totals_ref[...] + came[2, 0:8]
+    low, high = [(stays[p] + two[p]) + (four[p] + six[p]) for p in range(2)]
+    totals = (totals_ref[...] + two[2, 0:8]) + (four[2, 0:8] + six[2, 0:8])
     mine_ref[0] = jnp.where(first, low, high)
     give_ref[0] = jnp.where(first, high, low)
     for ref in (mine_ref, give_ref):
@@ -447,17 +445,24 @@
     mine = call(
         "pack", pack_kernel, [column, core, refs], shape(1, 2, HALF, LANES), [SMEM, SMEM, VMEM]
     )
-    four = call(
-        "stack", stack_kernel, [mine, over_z(mine, 4)], shape(2, 2, HALF, LANES)
-    )
+    came = [over_z(mine, bits) for bits in (2, 4, 6)]
     half = shape(2, 4, parts, BLOCK)
     own, other = call(
         "weighted",
         weighted_kernel,
-        [core, x, images, ctf, four],
+        [core, x, images, ctf, mine],
         [half, half],
         [SMEM, SMEM, VMEM, VMEM, ANY],
-    )
+        micros=3,
+    )
+    evens = call(
+        "stack",
+        stack_kernel,
+        [mine] + came + [own],
+        shape(4, 2, HALF, LANES),
+        [VMEM] * 4 + [ANY],
+    )
+    other = call("hold", stack_kernel, [other, evens], half, [VMEM, ANY])
     recv = lax.ppermute(other, "core", swap)
     slot = jnp.arange(lists.shape[1], dtype=jnp.int32)[None, :]
     used = jnp.where(slot < counts[:, None], lists, -1)
@@ -477,17 +482,10 @@
                 3,
             )
         )
-    two = call(
-        "stack",
-        stack_kernel,
-        [four, over_z(four, 2), recv],
-        shape(4, 2, HALF, LANES),
-        [VMEM, VMEM, ANY],
-    )
     blocks = call(
         "stack",
         stack_kernel,
-        [two, over_z(two, 1), rots[0]],
+        [evens, over_z(evens, 1), rots[0]],
         shape(8, 2, HALF, LANES),
         [VMEM, VMEM, ANY],
     )
@@ -514,12 +512,13 @@
 
     scale = (2 * ctf.shape[1]) ** -0.5
     part16, part32 = shape(32, HALF, LANES), shape(32, HALF, LANES, dtype=f32)
-    more16, row = shape(33, HALF, LANES), shape(8, LANES, dtype=f32)
-    stays, far_low, far_high, one_low, one_high, three_low, three_high, evidence, totals = call(
+    more16, both16 = shape(33, HALF, LANES), shape(65, HALF, LANES)
+    row = shape(8, LANES, dtype=f32)
+    stays, to_one, to_three, one_high, three_low, evidence, totals = call(
         "backward",
         lambda *args: backward_kernel(scale, *args),
         [core, x, y_lo, z, y_hi, scores, theirs, used_pair, shifts, own, recv],
-        [shape(4, 8, 2, HALF, LANES, dtype=f32), more16, more16, part16, part32, part32, part16]
+        [shape(4, 8, 2, HALF, LANES, dtype=f32), both16, both16, part32, part32]
         + [shape(parts, 1, dtype=f32), row],
         [SMEM] * 5 + [VMEM] * 6,
         [
@@ -532,19 +531,18 @@
         24,
         10,
     )
-    far_one, far_three = over(far_low, 1, 0), over(far_high, 3, 0)
-    one_low, three_high = over(one_low, 1, 0), over(three_high, 3, 0)
+    from_one, from_three = over(to_one, 1, 0), over(to_three, 3, 0)
     one_high, three_low, both, third = call(
         "add",
         add_kernel,
-        [totals, one_high, far_three, three_low, far_one],
+        [totals, one_high, three_low, from_one, from_three],
         [more16, part16, row, row],
     )
     one_high, three_low = over(one_high, 1, 0), over(three_low, 3, 0)
     *middle, totals = call(
         "middle",
         middle_kernel,
-        [both, third, stays, one_low, one_high, three_low, three_high],
+        [both, third, stays, from_one, one_high, three_low, from_three],
         [shape(16, HALF, LANES, dtype=f32)] + [shape(17, HALF, LANES)] * 3 + [row],
     )
     came = [over(middle[m], m, 1) for m in (1, 2, 3)]
@@ -554,20 +552,13 @@
         [totals, middle[0]] + came,
         [shape(8, HALF, LANES, dtype=f32), shape(9, HALF, LANES), row],
     )
-    for bits, count in ((1, 4), (2, 2)):
-        even, odd, totals = call(
-            "halve",
-            halve_kernel,
-            [totals, even, over_z(odd, bits)],
-            [
-                shape(count, HALF, LANES, dtype=f32),
-                shape(count + 1, HALF, LANES, dtype=f32),
-                row,
-            ],
-        )
-    two32 = shape(2, HALF, LANES, dtype=f32)
+    two32, three32 = shape(2, HALF, LANES, dtype=f32), shape(3, HALF, LANES, dtype=f32)
+    own, *others, totals = call(
+        "halve", halve_kernel, [totals, even, over_z(odd, 1)], [two32, three32, three32, three32, row]
+    )
+    others = [over_z(other, bits) for other, bits in zip(others, (2, 4, 6))]
     mine, give = call(
-        "deal", deal_kernel, [core, totals, even, over_z(odd, 4)], [two32, two32], [SMEM] + [VMEM] * 3
+        "deal", deal_kernel, [core, totals, own] + others, [two32, two32], [SMEM] + [VMEM] * 5
     )
     came = lax.ppermute(give, "core", swap)
     result, totals = call(

time: 135 us -> 123 us (0.911)
  starting transfers between devices: 50.1 us -> 41.4 us
  waiting for transfers between devices: 56.7 us -> 54 us
    ppermute x6 -> x8, waiting for transfers between devices: 13.6 us -> 9 us  [over_z(): return lax.ppermute(value, 'z', [(i, i ^ bits) for i in range(8)])]
    ppermute x6 -> x8, starting transfers between devices: 19.5 us -> 16.3 us  [over_z(): return lax.ppermute(value, 'z', [(i, i ^ bits) for i in range(8)])]
    ppermute x18 -> x16, starting transfers between devices: 17.8 us -> 15.6 us  [over(): return lax.ppermute(value, ('y_lo', 'x', 'core', 'y_hi'), pairs)]
    ppermute x1, starting transfers between devices: 4.81 us -> 3.01 us  [local(): theirs = lax.ppermute(scores, 'core', swap)]
    ppermute x1, starting transfers between devices: 5.73 us -> 3.97 us  [local(): came = lax.ppermute(give, 'core', swap)]
    ppermute x18 -> x16, waiting for transfers between devices: 41.1 us -> 42.6 us  [over(): return lax.ppermute(value, ('y_lo', 'x', 'core', 'y_hi'), pairs)]
    pallas_call x17 -> x16, Pallas kernels: 20.5 us -> 20.6 us  [call(): pl.pallas_call(kernel, out_shape=outs, in_specs=specs or [VMEM] * len(ins...]
  transfers between devices with their start and end apart: 28 -> 28, of which waited for: 20 -> 17; matrix products, arithmetic and copies ran while one was open for 1% -> 1% of each run, Pallas kernels for 4% -> 5%
where the time goes in v2:
time: 123 us
  waiting for transfers between devices  54 us (44%)
  starting transfers between devices  41.4 us (34%)
  Pallas kernels  20.6 us (17%)
  local copies, waits for them, and re-layouts  4.95 us (4%)
    ppermute x16, waiting for transfers between devices, over(): return lax.ppermute(value, ('y_lo', 'x', 'core', 'y_hi'), pairs)  42.6 us
    pallas_call x16, Pallas kernels, call(): pl.pallas_call(kernel, out_shape=outs, in_specs=specs or [VMEM] * len(ins...  20.6 us
    ppermute x8, starting transfers between devices, over_z(): return lax.ppermute(value, 'z', [(i, i ^ bits) for i in range(8)])  16.3 us
    ppermute x16, starting transfers between devices, over(): return lax.ppermute(value, ('y_lo', 'x', 'core', 'y_hi'), pairs)  15.6 us
    ppermute x8, waiting for transfers between devices, over_z(): return lax.ppermute(value, 'z', [(i, i ^ bits) for i in range(8)])  9 us
    unnamed x12, local copies, waits for them, and re-layouts  4.44 us
    ppermute x1, starting transfers between devices, local(): came = lax.ppermute(give, 'core', swap)  3.97 us
    ppermute x1, starting transfers between devices, local(): theirs = lax.ppermute(scores, 'core', swap)  3.01 us
  transfers between devices with their start and end apart: 28, of which 17 were waited for; matrix products, arithmetic and copies ran while one was open for 1% of the time, Pallas kernels for 5%

profile of v2, /device:TPU:1, one launch (start us, length us, event | category | flops | bytes accessed | tf_op | source)
XLA Modules:
  0.0 122.6 jit_solution(14108066409897438984)
XLA Ops:
  0.7 1.0 copy-done.2
  1.7 3.9 %collective-permute-start = (bf16[1,2,48,128]{3,2,1,0:T(8,128)(2,1)S(1)}, bf16[1,2,48,128]{3,2,1,0:T(8,128)(2,1)S(1)}, u32[]{:S(2)}, u32[]{:S(2)}) collective-permute-start(bf16[1,2,48,128]{3,2,1,0:T(8,128)(2,1)S(1)} %pack.1.before_ref.args_0_), channel_id=1, source_target_pairs={{0,4},{2,6},{4,0},{6,2},{8,12},{10,14},{12,8},{14,10},{1,5},{3,7},... | collective-permute-start | bytes 73736 | tf_op jit(solution)/shard_map/ppermute | solution.py:26
  5.6 5.1 %collective-permute-start.1 = (bf16[1,2,48,128]{3,2,1,0:T(8,128)(2,1)S(1)}, bf16[1,2,48,128]{3,2,1,0:T(8,128)(2,1)S(1)}, u32[]{:S(2)}, u32[]{:S(2)}) collective-permute-start(bf16[1,2,48,128]{3,2,1,0:T(8,128)(2,1)S(1)} %pack.1.before_ref.args_0_), channel_id=1, source_target_pairs={{0,8},{2,10},{4,12},{6,14},{8,0},{10,2},{12,4},{14,6},{1,9},{3,11}... | collective-permute-start | bytes 73736 | tf_op jit(solution)/shard_map/ppermute | solution.py:26
  10.7 1.4 %copy-done = bf16[48,16384]{1,0:T(8,128)(2,1)S(1)} copy-done((bf16[48,16384]{1,0:T(8,128)(2,1)S(1)}, bf16[48,16384]{1,0:T(8,128)(2,1)}, u32[]{:S(2)}) %copy-start) | copy-done | bytes 1572888
  12.1 1.1 copy-done.1
  13.3 0.3 weighted.1
  13.6 0.0 collective-permute-done.1.args_2_
  13.6 1.9 %collective-permute-done.2.args_3_ = bf16[1,2,48,128]{3,2,1,0:T(8,128)(2,1)S(1)} collective-permute-done((bf16[1,2,48,128]{3,2,1,0:T(8,128)(2,1)S(1)}, bf16[1,2,48,128]{3,2,1,0:T(8,128)(2,1)S(1)}, u32[]{:S(2)}, u32[]{:S(2)}) %collective-permute-start.2) | collective-permute-done | bytes 24608 | tf_op jit(solution)/shard_map/ppermute | solution.py:26
  15.5 0.1 hold.1
  15.6 2.5 %collective-permute-start.4 = (bf16[2,4,48,1024]{3,2,1,0:T(8,128)(2,1)S(1)}, bf16[2,4,48,1024]{3,2,1,0:T(8,128)(2,1)S(1)}, u32[]{:S(2)}, u32[]{:S(2)}) collective-permute-start(bf16[2,4,48,1024]{3,2,1,0:T(8,128)(2,1)S(1)} %hold.1), channel_id=1, source_target_pairs={{0,16},{16,0},{1,17},{17,1},{2,18},{18,2},{3,19},{19,3},{4,20},{20... | collective-permute-start | bytes 2359304 | tf_op jit(solution)/shard_map/ppermute | solution.py:466
  18.0 0.8 collective-permute-start.3
  18.8 0.8 copy.22.shifts_ref.args_8_
  19.6 0.4 collective-permute-done.4.recv_ref.args_10_
  19.9 2.8 %rotate.2.args_2_.args_9_ = bf16[2,2,864,1024]{3,2,1,0:T(8,128)(2,1)S(1)} custom-call(s32[1]{0:T(128)} %bitcast.core_ref.args_0_, s32[1]{0:T(128)} %bitcast.2.x_ref.args_1_, s32[1]{0:T(128)} %bitcast.3.part_ref.args_2_, s32[9,2]{1,0:T(8,128)S(1)} %copy.22.shifts_ref.args_8_, bf16[2,4,48,1024]{3,2,1,0:T(8,128)(2,1)S(1)} %get-tuple-element.35.args_4_.own_ref.args_9_, ...), custom_call_target="tpu_custom_call" | custom-call | flops 3000000 | bytes 9000000 | tf_op jit(solution)/shard_map/rotate/pallas_call | solution.py:411
  22.8 1.3 %collective-permute-start.5 = (bf16[8,2,48,128]{3,2,1,0:T(8,128)(2,1)S(1)}, bf16[8,2,48,128]{3,2,1,0:T(8,128)(2,1)S(1)}, u32[]{:S(2)}, u32[]{:S(2)}) collective-permute-start(bf16[8,2,48,128]{3,2,1,0:T(8,128)(2,1)S(1)} %stack.15.own_ref), channel_id=1, source_target_pairs={{0,128},{1,129},{16,48},{17,49},{32,160},{33,161},{48,16},{49,17},... | collective-permute-start | bytes 589832 | tf_op jit(solution)/shard_map/ppermute | solution.py:41
  24.1 2.5 %collective-permute-start.6 = (bf16[8,2,48,128]{3,2,1,0:T(8,128)(2,1)S(1)}, bf16[8,2,48,128]{3,2,1,0:T(8,128)(2,1)S(1)}, u32[]{:S(2)}, u32[]{:S(2)}) collective-permute-start(bf16[8,2,48,128]{3,2,1,0:T(8,128)(2,1)S(1)} %stack.15.own_ref), channel_id=1, source_target_pairs={{0,1},{1,0},{16,80},{17,81},{32,33},{33,32},{48,112},{49,113},{64,... | collective-permute-start | bytes 589832 | tf_op jit(solution)/shard_map/ppermute | solution.py:41
  26.6 0.2 collective-permute-start.7
  26.8 2.8 %rotate.3.rot_ref.args_10_ = bf16[2,2,864,1024]{3,2,1,0:T(8,128)(2,1)S(1)} custom-call(s32[1]{0:T(128)} %bitcast.core_ref.args_0_, s32[1]{0:T(128)} %bitcast.2.x_ref.args_1_, s32[1]{0:T(128)} %bitcast.3.part_ref.args_2_, s32[9,2]{1,0:T(8,128)S(1)} %copy.22.shifts_ref.args_8_, bf16[2,4,48,1024]{3,2,1,0:T(8,128)(2,1)S(1)} %get-tuple-element.35.args_4_.own_ref.args_9_, ...), custom_call_target="tpu_custom_call" | custom-call | flops 3000000 | bytes 9000000 | tf_op jit(solution)/shard_map/rotate/pallas_call | solution.py:411
  29.6 2.4 %collective-permute-done.6.two_ref = bf16[8,2,48,128]{3,2,1,0:T(8,128)(2,1)S(1)} collective-permute-done((bf16[8,2,48,128]{3,2,1,0:T(8,128)(2,1)S(1)}, bf16[8,2,48,128]{3,2,1,0:T(8,128)(2,1)S(1)}, u32[]{:S(2)}, u32[]{:S(2)}) %collective-permute-start.6) | collective-permute-done | bytes 196640 | tf_op jit(solution)/shard_map/ppermute | solution.py:41
  32.0 2.1 %collective-permute-done.7.three_ref = bf16[8,2,48,128]{3,2,1,0:T(8,128)(2,1)S(1)} collective-permute-done((bf16[8,2,48,128]{3,2,1,0:T(8,128)(2,1)S(1)}, bf16[8,2,48,128]{3,2,1,0:T(8,128)(2,1)S(1)}, u32[]{:S(2)}, u32[]{:S(2)}) %collective-permute-start.7) | collective-permute-done | bytes 196640 | tf_op jit(solution)/shard_map/ppermute | solution.py:41
  34.1 0.1 join.1
  34.2 1.1 collective-permute-start.8
  35.3 1.9 %collective-permute-start.11 = (bf16[2,8,2,48,128]{4,3,2,1,0:T(8,128)(2,1)S(1)}, bf16[2,8,2,48,128]{4,3,2,1,0:T(8,128)(2,1)S(1)}, u32[]{:S(2)}, u32[]{:S(2)}) collective-permute-start(bf16[2,8,2,48,128]{4,3,2,1,0:T(8,128)(2,1)S(1)} %get-tuple-element.38.args_2_), channel_id=1, source_target_pairs={{0,96},{1,97},{16,145},{17,144},{32,64},{33,65},{48,177},{49,176},... | collective-permute-start | bytes 1179656 | tf_op jit(solution)/shard_map/ppermute | solution.py:41
  37.2 0.8 collective-permute-start.13
  38.0 3.2 %collective-permute-done.8.args_3_ = bf16[2,8,2,48,128]{4,3,2,1,0:T(8,128)(2,1)S(1)} collective-permute-done((bf16[2,8,2,48,128]{4,3,2,1,0:T(8,128)(2,1)S(1)}, bf16[2,8,2,48,128]{4,3,2,1,0:T(8,128)(2,1)S(1)}, u32[]{:S(2)}, u32[]{:S(2)}) %collective-permute-start.8) | collective-permute-done | bytes 393248 | tf_op jit(solution)/shard_map/ppermute | solution.py:41
  41.2 2.4 %collective-permute-start.10 = (bf16[2,8,2,48,128]{4,3,2,1,0:T(8,128)(2,1)S(1)}, bf16[2,8,2,48,128]{4,3,2,1,0:T(8,128)(2,1)S(1)}, u32[]{:S(2)}, u32[]{:S(2)}) collective-permute-start(bf16[2,8,2,48,128]{4,3,2,1,0:T(8,128)(2,1)S(1)} %collective-permute-done.8.args_3_), channel_id=1, source_target_pairs={{0,96},{1,97},{16,145},{17,144},{32,64},{33,65},{48,177},{49,176},... | collective-permute-start | bytes 1179656 | tf_op jit(solution)/shard_map/ppermute | solution.py:41
  43.6 0.0 collective-permute-start.12
  43.6 4.0 %collective-permute-done.13.args_7_ = bf16[2,8,2,48,128]{4,3,2,1,0:T(8,128)(2,1)S(1)} collective-permute-done((bf16[2,8,2,48,128]{4,3,2,1,0:T(8,128)(2,1)S(1)}, bf16[2,8,2,48,128]{4,3,2,1,0:T(8,128)(2,1)S(1)}, u32[]{:S(2)}, u32[]{:S(2)}) %collective-permute-start.13) | collective-permute-done | bytes 393248 | tf_op jit(solution)/shard_map/ppermute | solution.py:41
  47.6 4.2 %collective-permute-done.10.args_5_ = bf16[2,8,2,48,128]{4,3,2,1,0:T(8,128)(2,1)S(1)} collective-permute-done((bf16[2,8,2,48,128]{4,3,2,1,0:T(8,128)(2,1)S(1)}, bf16[2,8,2,48,128]{4,3,2,1,0:T(8,128)(2,1)S(1)}, u32[]{:S(2)}, u32[]{:S(2)}) %collective-permute-start.10) | collective-permute-done | bytes 393248 | tf_op jit(solution)/shard_map/ppermute | solution.py:41
  51.8 4.3 %forward.1.args_5_ = f32[864,256]{1,0:T(8,128)S(1)} custom-call(s32[1]{0:T(128)} %bitcast.core_ref.args_0_, bf16[2,8,2,48,128]{4,3,2,1,0:T(8,128)(2,1)S(1)} %get-tuple-element.37.args_1_, bf16[2,8,2,48,128]{4,3,2,1,0:T(8,128)(2,1)S(1)} %get-tuple-element.38.args_2_, bf16[2,8,2,48,128]{4,3,2,1,0:T(8,128)(2,1)S(1)} %collective-permute-done.8.args_3_, ...), custom_call_target="tpu_custom_call" | custom-call | flops 4000000 | bytes 12000000 | tf_op jit(solution)/shard_map/forward/pallas_call | solution.py:411
  56.1 3.0 %collective-permute-start.14 = (f32[864,256]{1,0:T(8,128)S(1)}, f32[864,256]{1,0:T(8,128)S(1)}, u32[]{:S(2)}, u32[]{:S(2)}) collective-permute-start(f32[864,256]{1,0:T(8,128)S(1)} %forward.1.args_5_), channel_id=1, source_target_pairs={{0,16},{16,0},{1,17},{17,1},{2,18},{18,2},{3,19},{19,3},{4,20},{20... | collective-permute-start | bytes 2654216 | tf_op jit(solution)/shard_map/ppermute | solution.py:511
  59.1 0.1 copy.24
  59.2 0.1 fusion
  59.3 0.1 collective-permute-start.15
  59.3 0.1 fusion.1
  59.4 1.8 %collective-permute-done.15 = s32[48,12]{1,0:T(8,128)S(1)} collective-permute-done((s32[48,12]{1,0:T(8,128)S(1)}, s32[48,12]{1,0:T(8,128)S(1)}, u32[]{:S(2)}, u32[]{:S(2)}) %collective-permute-start.15) | collective-permute-done | bytes 2336 | tf_op jit(solution)/shard_map/ppermute | solution.py:469
  61.2 9.1 %backward.1 = (f32[4,8,2,48,128]{4,3,2,1,0:T(8,128)S(1)}, bf16[65,48,128]{2,1,0:T(8,128)(2,1)S(1)}, bf16[65,48,128]{2,1,0:T(8,128)(2,1)S(1)}, f32[32,48,128]{2,1...) custom-call(s32[1]{0:T(128)} %bitcast.core_ref.args_0_, ...), custom_call_target="tpu_custom_call" | custom-call | flops 10000000 | bytes 30000000 | tf_op jit(solution)/shard_map/backward/pallas_call | solution.py:411
  70.3 0.1 collective-permute-start.16
  70.4 0.5 collective-permute-start.17
  70.9 10.7 %collective-permute-done.16.from_one = bf16[65,48,128]{2,1,0:T(8,128)(2,1)S(1)} collective-permute-done((bf16[65,48,128]{2,1,0:T(8,128)(2,1)S(1)}, bf16[65,48,128]{2,1,0:T(8,128)(2,1)S(1)}, u32[]{:S(2)}, u32[]{:S(2)}) %collective-permute-start.16) | collective-permute-done | bytes 798752 | tf_op jit(solution)/shard_map/ppermute | solution.py:41
  81.6 1.3 %collective-permute-done.17.from_three = bf16[65,48,128]{2,1,0:T(8,128)(2,1)S(1)} collective-permute-done((bf16[65,48,128]{2,1,0:T(8,128)(2,1)S(1)}, bf16[65,48,128]{2,1,0:T(8,128)(2,1)S(1)}, u32[]{:S(2)}, u32[]{:S(2)}) %collective-permute-start.17) | collective-permute-done | bytes 798752 | tf_op jit(solution)/shard_map/ppermute | solution.py:41
  82.9 0.2 add.12
  83.1 0.2 collective-permute-start.18
  83.3 0.6 collective-permute-start.19
  84.0 7.5 %collective-permute-done.19.three_low = bf16[32,48,128]{2,1,0:T(8,128)(2,1)S(1)} collective-permute-done((bf16[32,48,128]{2,1,0:T(8,128)(2,1)S(1)}, bf16[32,48,128]{2,1,0:T(8,128)(2,1)S(1)}, u32[]{:S(2)}, u32[]{:S(2)}) %collective-permute-start.19) | collective-permute-done | bytes 393248 | tf_op jit(solution)/shard_map/ppermute | solution.py:41
  91.5 0.3 middle.1
  91.8 0.1 collective-permute-start.20
  91.9 3.0 %collective-permute-start.21 = (bf16[17,48,128]{2,1,0:T(8,128)(2,1)S(1)}, bf16[17,48,128]{2,1,0:T(8,128)(2,1)S(1)}, u32[]{:S(2)}, u32[]{:S(2)}) collective-permute-start(bf16[17,48,128]{2,1,0:T(8,128)(2,1)S(1)} %get-tuple-element.52), channel_id=1, source_target_pairs={{0,1},{1,0},{16,80},{17,81},{32,33},{33,32},{48,112},{49,113},{64,... | collective-permute-start | bytes 626696 | tf_op jit(solution)/shard_map/ppermute | solution.py:41
  94.8 0.9 collective-permute-start.22
  95.7 0.8 collective-permute-done.20.one
  96.5 4.1 %collective-permute-done.21.two = bf16[17,48,128]{2,1,0:T(8,128)(2,1)S(1)} collective-permute-done((bf16[17,48,128]{2,1,0:T(8,128)(2,1)S(1)}, bf16[17,48,128]{2,1,0:T(8,128)(2,1)S(1)}, u32[]{:S(2)}, u32[]{:S(2)}) %collective-permute-start.21) | collective-permute-done | bytes 208928 | tf_op jit(solution)/shard_map/ppermute | solution.py:41
  100.6 2.2 %collective-permute-done.22.three = bf16[17,48,128]{2,1,0:T(8,128)(2,1)S(1)} collective-permute-done((bf16[17,48,128]{2,1,0:T(8,128)(2,1)S(1)}, bf16[17,48,128]{2,1,0:T(8,128)(2,1)S(1)}, u32[]{:S(2)}, u32[]{:S(2)}) %collective-permute-start.22) | collective-permute-done | bytes 208928 | tf_op jit(solution)/shard_map/ppermute | solution.py:41
  102.8 0.1 late.1
  102.9 0.8 collective-permute-start.23
  103.7 2.9 %collective-permute-done.23.came = bf16[9,48,128]{2,1,0:T(8,128)(2,1)S(1)} collective-permute-done((bf16[9,48,128]{2,1,0:T(8,128)(2,1)S(1)}, bf16[9,48,128]{2,1,0:T(8,128)(2,1)S(1)}, u32[]{:S(2)}, u32[]{:S(2)}) %collective-permute-start.23) | collective-permute-done | bytes 110624 | tf_op jit(solution)/shard_map/ppermute | solution.py:26
  106.6 1.3 %collective-permute-start.24 = (f32[3,48,128]{2,1,0:T(8,128)S(1)}, f32[3,48,128]{2,1,0:T(8,128)S(1)}, u32[]{:S(2)}, u32[]{:S(2)}) collective-permute-start(f32[3,48,128]{2,1,0:T(8,128)S(1)} %get-tuple-element.59), channel_id=1, source_target_pairs={{0,4},{2,6},{4,0},{6,2},{8,12},{10,14},{12,8},{14,10},{1,5},{3,7},... | collective-permute-start | bytes 221192 | tf_op jit(solution)/shard_map/ppermute | solution.py:26
  107.9 1.7 %collective-permute-start.25 = (f32[3,48,128]{2,1,0:T(8,128)S(1)}, f32[3,48,128]{2,1,0:T(8,128)S(1)}, u32[]{:S(2)}, u32[]{:S(2)}) collective-permute-start(f32[3,48,128]{2,1,0:T(8,128)S(1)} %get-tuple-element.60), channel_id=1, source_target_pairs={{0,8},{2,10},{4,12},{6,14},{8,0},{10,2},{12,4},{14,6},{1,9},{3,11}... | collective-permute-start | bytes 221192 | tf_op jit(solution)/shard_map/ppermute | solution.py:26
  109.6 2.8 %collective-permute-start.26 = (f32[3,48,128]{2,1,0:T(8,128)S(1)}, f32[3,48,128]{2,1,0:T(8,128)S(1)}, u32[]{:S(2)}, u32[]{:S(2)}) collective-permute-start(f32[3,48,128]{2,1,0:T(8,128)S(1)} %get-tuple-element.61), channel_id=1, source_target_pairs={{0,12},{2,14},{4,8},{6,10},{8,4},{10,6},{12,0},{14,2},{1,13},{3,15... | collective-permute-start | bytes 221192 | tf_op jit(solution)/shard_map/ppermute | solution.py:26
  112.4 4.2 %collective-permute-done.25.four = f32[3,48,128]{2,1,0:T(8,128)S(1)} collective-permute-done((f32[3,48,128]{2,1,0:T(8,128)S(1)}, f32[3,48,128]{2,1,0:T(8,128)S(1)}, u32[]{:S(2)}, u32[]{:S(2)}) %collective-permute-start.25) | collective-permute-done | bytes 73760 | tf_op jit(solution)/shard_map/ppermute | solution.py:26
  116.6 4.0 %collective-permute-start.27 = (f32[2,48,128]{2,1,0:T(8,128)S(1)}, f32[2,48,128]{2,1,0:T(8,128)S(1)}, u32[]{:S(2)}, u32[]{:S(2)}) collective-permute-start(f32[2,48,128]{2,1,0:T(8,128)S(1)} %get-tuple-element.63), channel_id=1, source_target_pairs={{0,16},{16,0},{1,17},{17,1},{2,18},{18,2},{3,19},{19,3},{4,20},{20... | collective-permute-start | bytes 147464 | tf_op jit(solution)/shard_map/ppermute | solution.py:563
  120.6 0.6 reduce
  121.2 0.3 collective-permute-done.27.came_ref
  121.5 0.6 last.1
  122.1 0.5 slice_bitcast_fusion
  (25 shorter events, 0.1 us)
Async XLA Ops:
  0.6 1.0 copy-start.2
  1.7 11.9 %collective-permute-start = (bf16[1,2,48,128]{3,2,1,0:T(8,128)(2,1)S(1)}, bf16[1,2,48,128]{3,2,1,0:T(8,128)(2,1)S(1)}, u32[]{:S(2)}, u32[]{:S(2)}) collective-permute-start(bf16[1,2,48,128]{3,2,1,0:T(8,128)(2,1)S(1)} %pack.1.before_ref.args_0_), channel_id=1, source_target_pairs={{0,4},{2,6},{4,0},{6,2},{8,12},{10,14},{12,8},{14,10},{1,5},{3,7},... | collective-permute-start | bytes 73736 | tf_op jit(solution)/shard_map/ppermute | solution.py:26
  5.6 8.0 %collective-permute-start.1 = (bf16[1,2,48,128]{3,2,1,0:T(8,128)(2,1)S(1)}, bf16[1,2,48,128]{3,2,1,0:T(8,128)(2,1)S(1)}, u32[]{:S(2)}, u32[]{:S(2)}) collective-permute-start(bf16[1,2,48,128]{3,2,1,0:T(8,128)(2,1)S(1)} %pack.1.before_ref.args_0_), channel_id=1, source_target_pairs={{0,8},{2,10},{4,12},{6,14},{8,0},{10,2},{12,4},{14,6},{1,9},{3,11}... | collective-permute-start | bytes 73736 | tf_op jit(solution)/shard_map/ppermute | solution.py:26
  10.7 4.8 %collective-permute-start.2 = (bf16[1,2,48,128]{3,2,1,0:T(8,128)(2,1)S(1)}, bf16[1,2,48,128]{3,2,1,0:T(8,128)(2,1)S(1)}, u32[]{:S(2)}, u32[]{:S(2)}) collective-permute-start(bf16[1,2,48,128]{3,2,1,0:T(8,128)(2,1)S(1)} %pack.1.before_ref.args_0_), channel_id=1, source_target_pairs={{0,12},{2,14},{4,8},{6,10},{8,4},{10,6},{12,0},{14,2},{1,13},{3,15... | collective-permute-start | bytes 73736 | tf_op jit(solution)/shard_map/ppermute | solution.py:26
  10.7 1.4 %copy-start = (bf16[48,16384]{1,0:T(8,128)(2,1)S(1)}, bf16[48,16384]{1,0:T(8,128)(2,1)}, u32[]{:S(2)}) copy-start(bf16[48,16384]{1,0:T(8,128)(2,1)} %images_ref.1) | copy-start | bytes 4718596
  12.1 1.1 copy-start.1
  15.6 4.4 %collective-permute-start.4 = (bf16[2,4,48,1024]{3,2,1,0:T(8,128)(2,1)S(1)}, bf16[2,4,48,1024]{3,2,1,0:T(8,128)(2,1)S(1)}, u32[]{:S(2)}, u32[]{:S(2)}) collective-permute-start(bf16[2,4,48,1024]{3,2,1,0:T(8,128)(2,1)S(1)} %hold.1), channel_id=1, source_target_pairs={{0,16},{16,0},{1,17},{17,1},{2,18},{18,2},{3,19},{19,3},{4,20},{20... | collective-permute-start | bytes 2359304 | tf_op jit(solution)/shard_map/ppermute | solution.py:466
  18.0 4.7 %collective-permute-start.3 = (bf16[4,2,48,128]{3,2,1,0:T(8,128)(2,1)S(1)}, bf16[4,2,48,128]{3,2,1,0:T(8,128)(2,1)S(1)}, u32[]{:S(2)}, u32[]{:S(2)}) collective-permute-start(bf16[4,2,48,128]{3,2,1,0:T(8,128)(2,1)S(1)} %stack.14.args_1_.args_0_), channel_id=1, source_target_pairs={{0,2},{2,0},{4,6},{6,4},{8,10},{10,8},{12,14},{14,12},{1,3},{3,1},... | collective-permute-start | bytes 294920 | tf_op jit(solution)/shard_map/ppermute | solution.py:26
  22.8 6.8 %collective-permute-start.5 = (bf16[8,2,48,128]{3,2,1,0:T(8,128)(2,1)S(1)}, bf16[8,2,48,128]{3,2,1,0:T(8,128)(2,1)S(1)}, u32[]{:S(2)}, u32[]{:S(2)}) collective-permute-start(bf16[8,2,48,128]{3,2,1,0:T(8,128)(2,1)S(1)} %stack.15.own_ref), channel_id=1, source_target_pairs={{0,128},{1,129},{16,48},{17,49},{32,160},{33,161},{48,16},{49,17},... | collective-permute-start | bytes 589832 | tf_op jit(solution)/shard_map/ppermute | solution.py:41
  24.1 7.9 %collective-permute-start.6 = (bf16[8,2,48,128]{3,2,1,0:T(8,128)(2,1)S(1)}, bf16[8,2,48,128]{3,2,1,0:T(8,128)(2,1)S(1)}, u32[]{:S(2)}, u32[]{:S(2)}) collective-permute-start(bf16[8,2,48,128]{3,2,1,0:T(8,128)(2,1)S(1)} %stack.15.own_ref), channel_id=1, source_target_pairs={{0,1},{1,0},{16,80},{17,81},{32,33},{33,32},{48,112},{49,113},{64,... | collective-permute-start | bytes 589832 | tf_op jit(solution)/shard_map/ppermute | solution.py:41
  26.6 7.6 %collective-permute-start.7 = (bf16[8,2,48,128]{3,2,1,0:T(8,128)(2,1)S(1)}, bf16[8,2,48,128]{3,2,1,0:T(8,128)(2,1)S(1)}, u32[]{:S(2)}, u32[]{:S(2)}) collective-permute-start(bf16[8,2,48,128]{3,2,1,0:T(8,128)(2,1)S(1)} %stack.15.own_ref), channel_id=1, source_target_pairs={{0,129},{1,128},{16,112},{17,113},{32,161},{33,160},{48,80},{49,81... | collective-permute-start | bytes 589832 | tf_op jit(solution)/shard_map/ppermute | solution.py:41
  34.2 7.0 %collective-permute-start.8 = (bf16[2,8,2,48,128]{4,3,2,1,0:T(8,128)(2,1)S(1)}, bf16[2,8,2,48,128]{4,3,2,1,0:T(8,128)(2,1)S(1)}, u32[]{:S(2)}, u32[]{:S(2)}) collective-permute-start(bf16[2,8,2,48,128]{4,3,2,1,0:T(8,128)(2,1)S(1)} %get-tuple-element.37.args_1_), channel_id=1, source_target_pairs={{0,32},{1,33},{16,144},{17,145},{32,0},{33,1},{48,176},{49,177},{6... | collective-permute-start | bytes 1179656 | tf_op jit(solution)/shard_map/ppermute | solution.py:41
  35.3 23.8 %copy-start.3 = (s32[48,12]{0,1:T(8,128)S(1)}, s32[48,12]{0,1:T(8,128)}, u32[]{:S(2)}) copy-start(s32[48,12]{0,1:T(8,128)} %param.10) | copy-start | bytes 6916
  35.3 23.9 %copy-start.4 = (s32[48]{0:T(128)S(1)}, s32[48]{0:T(128)}, u32[]{:S(2)}) copy-start(s32[48]{0:T(128)} %param.11) | copy-start | bytes 580
  35.3 8.4 %collective-permute-start.11 = (bf16[2,8,2,48,128]{4,3,2,1,0:T(8,128)(2,1)S(1)}, bf16[2,8,2,48,128]{4,3,2,1,0:T(8,128)(2,1)S(1)}, u32[]{:S(2)}, u32[]{:S(2)}) collective-permute-start(bf16[2,8,2,48,128]{4,3,2,1,0:T(8,128)(2,1)S(1)} %get-tuple-element.38.args_2_), channel_id=1, source_target_pairs={{0,96},{1,97},{16,145},{17,144},{32,64},{33,65},{48,177},{49,176},... | collective-permute-start | bytes 1179656 | tf_op jit(solution)/shard_map/ppermute | solution.py:41
  37.2 10.4 %collective-permute-start.13 = (bf16[2,8,2,48,128]{4,3,2,1,0:T(8,128)(2,1)S(1)}, bf16[2,8,2,48,128]{4,3,2,1,0:T(8,128)(2,1)S(1)}, u32[]{:S(2)}, u32[]{:S(2)}) collective-permute-start(bf16[2,8,2,48,128]{4,3,2,1,0:T(8,128)(2,1)S(1)} %get-tuple-element.37.args_1_), channel_id=1, source_target_pairs={{0,96},{1,97},{16,145},{17,144},{32,64},{33,65},{48,177},{49,176},... | collective-permute-start | bytes 1179656 | tf_op jit(solution)/shard_map/ppermute | solution.py:41
  38.0 9.7 %collective-permute-start.9 = (bf16[2,8,2,48,128]{4,3,2,1,0:T(8,128)(2,1)S(1)}, bf16[2,8,2,48,128]{4,3,2,1,0:T(8,128)(2,1)S(1)}, u32[]{:S(2)}, u32[]{:S(2)}) collective-permute-start(bf16[2,8,2,48,128]{4,3,2,1,0:T(8,128)(2,1)S(1)} %get-tuple-element.38.args_2_), channel_id=1, source_target_pairs={{0,32},{1,33},{16,144},{17,145},{32,0},{33,1},{48,176},{49,177},{6... | collective-permute-start | bytes 1179656 | tf_op jit(solution)/shard_map/ppermute | solution.py:41
  41.2 10.6 %collective-permute-start.10 = (bf16[2,8,2,48,128]{4,3,2,1,0:T(8,128)(2,1)S(1)}, bf16[2,8,2,48,128]{4,3,2,1,0:T(8,128)(2,1)S(1)}, u32[]{:S(2)}, u32[]{:S(2)}) collective-permute-start(bf16[2,8,2,48,128]{4,3,2,1,0:T(8,128)(2,1)S(1)} %collective-permute-done.8.args_3_), channel_id=1, source_target_pairs={{0,96},{1,97},{16,145},{17,144},{32,64},{33,65},{48,177},{49,176},... | collective-permute-start | bytes 1179656 | tf_op jit(solution)/shard_map/ppermute | solution.py:41
  43.6 8.2 %collective-permute-start.12 = (bf16[2,8,2,48,128]{4,3,2,1,0:T(8,128)(2,1)S(1)}, bf16[2,8,2,48,128]{4,3,2,1,0:T(8,128)(2,1)S(1)}, u32[]{:S(2)}, u32[]{:S(2)}) collective-permute-start(bf16[2,8,2,48,128]{4,3,2,1,0:T(8,128)(2,1)S(1)} %collective-permute-done.11.args_8_), channel_id=1, source_target_pairs={{0,32},{1,33},{16,144},{17,145},{32,0},{33,1},{48,176},{49,177},{6... | collective-permute-start | bytes 1179656 | tf_op jit(solution)/shard_map/ppermute | solution.py:41
  56.1 5.1 %collective-permute-start.14 = (f32[864,256]{1,0:T(8,128)S(1)}, f32[864,256]{1,0:T(8,128)S(1)}, u32[]{:S(2)}, u32[]{:S(2)}) collective-permute-start(f32[864,256]{1,0:T(8,128)S(1)} %forward.1.args_5_), channel_id=1, source_target_pairs={{0,16},{16,0},{1,17},{17,1},{2,18},{18,2},{3,19},{19,3},{4,20},{20... | collective-permute-start | bytes 2654216 | tf_op jit(solution)/shard_map/ppermute | solution.py:511
  59.3 1.9 %collective-permute-start.15 = (s32[48,12]{1,0:T(8,128)S(1)}, s32[48,12]{1,0:T(8,128)S(1)}, u32[]{:S(2)}, u32[]{:S(2)}) collective-permute-start(s32[48,12]{1,0:T(8,128)S(1)} %fusion), channel_id=1, source_target_pairs={{0,16},{16,0},{1,17},{17,1},{2,18},{18,2},{3,19},{19,3},{4,20},{20... | collective-permute-start | bytes 6920 | tf_op jit(solution)/shard_map/ppermute | solution.py:469
  70.3 11.4 %collective-permute-start.16 = (bf16[65,48,128]{2,1,0:T(8,128)(2,1)S(1)}, bf16[65,48,128]{2,1,0:T(8,128)(2,1)S(1)}, u32[]{:S(2)}, u32[]{:S(2)}) collective-permute-start(bf16[65,48,128]{2,1,0:T(8,128)(2,1)S(1)} %get-tuple-element.42), channel_id=1, source_target_pairs={{0,32},{1,33},{16,144},{17,145},{32,0},{33,1},{48,176},{49,177},{6... | collective-permute-start | bytes 2396168 | tf_op jit(solution)/shard_map/ppermute | solution.py:41
  70.4 12.6 %collective-permute-start.17 = (bf16[65,48,128]{2,1,0:T(8,128)(2,1)S(1)}, bf16[65,48,128]{2,1,0:T(8,128)(2,1)S(1)}, u32[]{:S(2)}, u32[]{:S(2)}) collective-permute-start(bf16[65,48,128]{2,1,0:T(8,128)(2,1)S(1)} %get-tuple-element.43), channel_id=1, source_target_pairs={{0,96},{1,97},{16,145},{17,144},{32,64},{33,65},{48,177},{49,176},... | collective-permute-start | bytes 2396168 | tf_op jit(solution)/shard_map/ppermute | solution.py:41
  83.1 8.4 %collective-permute-start.18 = (bf16[33,48,128]{2,1,0:T(8,128)(2,1)S(1)}, bf16[33,48,128]{2,1,0:T(8,128)(2,1)S(1)}, u32[]{:S(2)}, u32[]{:S(2)}) collective-permute-start(bf16[33,48,128]{2,1,0:T(8,128)(2,1)S(1)} %get-tuple-element.47), channel_id=1, source_target_pairs={{0,32},{1,33},{16,144},{17,145},{32,0},{33,1},{48,176},{49,177},{6... | collective-permute-start | bytes 1216520 | tf_op jit(solution)/shard_map/ppermute | solution.py:41
  83.3 8.1 %collective-permute-start.19 = (bf16[32,48,128]{2,1,0:T(8,128)(2,1)S(1)}, bf16[32,48,128]{2,1,0:T(8,128)(2,1)S(1)}, u32[]{:S(2)}, u32[]{:S(2)}) collective-permute-start(bf16[32,48,128]{2,1,0:T(8,128)(2,1)S(1)} %get-tuple-element.48), channel_id=1, source_target_pairs={{0,96},{1,97},{16,145},{17,144},{32,64},{33,65},{48,177},{49,176},... | collective-permute-start | bytes 1179656 | tf_op jit(solution)/shard_map/ppermute | solution.py:41
  91.8 4.7 %collective-permute-start.20 = (bf16[17,48,128]{2,1,0:T(8,128)(2,1)S(1)}, bf16[17,48,128]{2,1,0:T(8,128)(2,1)S(1)}, u32[]{:S(2)}, u32[]{:S(2)}) collective-permute-start(bf16[17,48,128]{2,1,0:T(8,128)(2,1)S(1)} %get-tuple-element.51), channel_id=1, source_target_pairs={{0,128},{1,129},{16,48},{17,49},{32,160},{33,161},{48,16},{49,17},... | collective-permute-start | bytes 626696 | tf_op jit(solution)/shard_map/ppermute | solution.py:41
  91.9 8.7 %collective-permute-start.21 = (bf16[17,48,128]{2,1,0:T(8,128)(2,1)S(1)}, bf16[17,48,128]{2,1,0:T(8,128)(2,1)S(1)}, u32[]{:S(2)}, u32[]{:S(2)}) collective-permute-start(bf16[17,48,128]{2,1,0:T(8,128)(2,1)S(1)} %get-tuple-element.52), channel_id=1, source_target_pairs={{0,1},{1,0},{16,80},{17,81},{32,33},{33,32},{48,112},{49,113},{64,... | collective-permute-start | bytes 626696 | tf_op jit(solution)/shard_map/ppermute | solution.py:41
  94.8 8.0 %collective-permute-start.22 = (bf16[17,48,128]{2,1,0:T(8,128)(2,1)S(1)}, bf16[17,48,128]{2,1,0:T(8,128)(2,1)S(1)}, u32[]{:S(2)}, u32[]{:S(2)}) collective-permute-start(bf16[17,48,128]{2,1,0:T(8,128)(2,1)S(1)} %get-tuple-element.53), channel_id=1, source_target_pairs={{0,129},{1,128},{16,112},{17,113},{32,161},{33,160},{48,80},{49,81... | collective-permute-start | bytes 626696 | tf_op jit(solution)/shard_map/ppermute | solution.py:41
  102.9 3.7 %collective-permute-start.23 = (bf16[9,48,128]{2,1,0:T(8,128)(2,1)S(1)}, bf16[9,48,128]{2,1,0:T(8,128)(2,1)S(1)}, u32[]{:S(2)}, u32[]{:S(2)}) collective-permute-start(bf16[9,48,128]{2,1,0:T(8,128)(2,1)S(1)} %get-tuple-element.56), channel_id=1, source_target_pairs={{0,2},{2,0},{4,6},{6,4},{8,10},{10,8},{12,14},{14,12},{1,3},{3,1},... | collective-permute-start | bytes 331784 | tf_op jit(solution)/shard_map/ppermute | solution.py:26
  106.6 5.7 %collective-permute-start.24 = (f32[3,48,128]{2,1,0:T(8,128)S(1)}, f32[3,48,128]{2,1,0:T(8,128)S(1)}, u32[]{:S(2)}, u32[]{:S(2)}) collective-permute-start(f32[3,48,128]{2,1,0:T(8,128)S(1)} %get-tuple-element.59), channel_id=1, source_target_pairs={{0,4},{2,6},{4,0},{6,2},{8,12},{10,14},{12,8},{14,10},{1,5},{3,7},... | collective-permute-start | bytes 221192 | tf_op jit(solution)/shard_map/ppermute | solution.py:26
  107.9 8.7 %collective-permute-start.25 = (f32[3,48,128]{2,1,0:T(8,128)S(1)}, f32[3,48,128]{2,1,0:T(8,128)S(1)}, u32[]{:S(2)}, u32[]{:S(2)}) collective-permute-start(f32[3,48,128]{2,1,0:T(8,128)S(1)} %get-tuple-element.60), channel_id=1, source_target_pairs={{0,8},{2,10},{4,12},{6,14},{8,0},{10,2},{12,4},{14,6},{1,9},{3,11}... | collective-permute-start | bytes 221192 | tf_op jit(solution)/shard_map/ppermute | solution.py:26
  109.6 7.0 %collective-permute-start.26 = (f32[3,48,128]{2,1,0:T(8,128)S(1)}, f32[3,48,128]{2,1,0:T(8,128)S(1)}, u32[]{:S(2)}, u32[]{:S(2)}) collective-permute-start(f32[3,48,128]{2,1,0:T(8,128)S(1)} %get-tuple-element.61), channel_id=1, source_target_pairs={{0,12},{2,14},{4,8},{6,10},{8,4},{10,6},{12,0},{14,2},{1,13},{3,15... | collective-permute-start | bytes 221192 | tf_op jit(solution)/shard_map/ppermute | solution.py:26
  116.6 4.8 %collective-permute-start.27 = (f32[2,48,128]{2,1,0:T(8,128)S(1)}, f32[2,48,128]{2,1,0:T(8,128)S(1)}, u32[]{:S(2)}, u32[]{:S(2)}) collective-permute-start(f32[2,48,128]{2,1,0:T(8,128)S(1)} %get-tuple-element.63), channel_id=1, source_target_pairs={{0,16},{16,0},{1,17},{17,1},{2,18},{18,2},{3,19},{19,3},{4,20},{20... | collective-permute-start | bytes 147464 | tf_op jit(solution)/shard_map/ppermute | solution.py:563

commit v3 on v2

--- a/solution.py
+++ b/solution.py
@@ -80,45 +80,40 @@
                     )
 
 
-def rotate_chunk(core, x, shifts_ref, own_ref, recv_ref, xr, start, tables, put):
+def rotate_kernel(first_xr, core_ref, x_ref, part_ref, shifts_ref, own_ref, recv_ref, *rest):
+    *before, rot_ref, cos_ref, sin_ref = rest
     rows = own_ref.shape[2]
     trans = shifts_ref.shape[0]
     half = GRID // 2
-    cos_ref, sin_ref = tables
-    lanes = pl.ds(start, CHUNK)
-    pixel = (2 * (x ^ xr) + start // SIDE) * BLOCK + core * SIDE + start % SIDE
-    pixel = pixel + lax.broadcasted_iota(jnp.int32, (trans, CHUNK), 1)
-    freq_y = (((pixel >> 6) + half) & (GRID - 1)) - half
-    turns = (pixel & (half - 1)) * shifts_ref[:, 0:1] + freq_y * shifts_ref[:, 1:2]
-    angle = (turns & (GRID - 1)).astype(jnp.float32) * jnp.float32(2.0 * math.pi / GRID)
-    cos_ref[...] = jnp.cos(angle)
-    sin_ref[...] = jnp.sin(angle)
-    for h, half_ref in enumerate((own_ref, recv_ref)):
-        re = half_ref[0, xr, :, lanes].astype(jnp.float32)
-        im = half_ref[1, xr, :, lanes].astype(jnp.float32)
-        for t in range(trans):
-            cosine, sine = cos_ref[t : t + 1, :], sin_ref[t : t + 1, :]
-            base = (h * trans + t) * rows
-            put(0, base, rows, (re * cosine + im * sine).astype(jnp.bfloat16))
-            put(1, base, rows, (im * cosine - re * sine).astype(jnp.bfloat16))
-
-
-def rotate_kernel(
-    first_xr, core_ref, x_ref, part_ref, shifts_ref, own_ref, recv_ref, rot_ref, cos_ref, sin_ref
-):
+    steps = BLOCK // CHUNK
     first = part_ref[0]
-    steps = BLOCK // CHUNK
+    for old_ref, new_ref in zip(before, (cos_ref, sin_ref)):
+        new_ref[:first_xr] = old_ref[...]
 
     def step(index, carry):
-        xr = index // steps
+        place = index // steps
+        xr = first_xr + place
         start = pl.multiple_of((index % steps) * CHUNK, CHUNK)
-
-        def put(part, base, rows, value, place=xr):
-            rot_ref[part ^ first, place, base : base + rows, pl.ds(start, CHUNK)] = value
-
-        tables = cos_ref, sin_ref
-        xr = first_xr + xr
-        rotate_chunk(core_ref[0], x_ref[0], shifts_ref, own_ref, recv_ref, xr, start, tables, put)
+        lanes = pl.ds(start, CHUNK)
+        pixel = (2 * (x_ref[0] ^ xr) + start // SIDE) * BLOCK + core_ref[0] * SIDE + start % SIDE
+        pixel = pixel + lax.broadcasted_iota(jnp.int32, (trans, CHUNK), 1)
+        freq_y = (((pixel >> 6) + half) & (GRID - 1)) - half
+        turns = (pixel & (half - 1)) * shifts_ref[:, 0:1] + freq_y * shifts_ref[:, 1:2]
+        angle = (turns & (GRID - 1)).astype(jnp.float32) * jnp.float32(2.0 * math.pi / GRID)
+        cos_ref[xr, :, lanes] = jnp.cos(angle)
+        sin_ref[xr, :, lanes] = jnp.sin(angle)
+        for h, half_ref in enumerate((own_ref, recv_ref)):
+            re = half_ref[0, xr, :, lanes].astype(jnp.float32)
+            im = half_ref[1, xr, :, lanes].astype(jnp.float32)
+            for t in range(trans):
+                cosine, sine = cos_ref[xr, t : t + 1, lanes], sin_ref[xr, t : t + 1, lanes]
+                base = (h * trans + t) * rows
+                rot_ref[first, place, base : base + rows, lanes] = (re * cosine + im * sine).astype(
+                    jnp.bfloat16
+                )
+                rot_ref[1 - first, place, base : base + rows, lanes] = (
+                    im * cosine - re * sine
+                ).astype(jnp.bfloat16)
         return carry
 
     lax.fori_loop(0, rot_ref.shape[1] * steps, step, 0)
@@ -242,12 +237,63 @@
     weights_ref[2 * trans * particles :] = jnp.broadcast_to(shares[0] + shares[1], (8, refs_all))
 
 
-def backward_kernel(scale, *args):
-    core_ref, x_ref, y_lo_ref, z_ref, y_hi_ref, mine_ref, theirs_ref, lists_ref = args[:8]
-    shifts_ref, own_ref, recv_ref = args[8:11]
-    stays, to_one, to_three, one_high, three_low = args[11:16]
-    evidence_ref, totals_ref, weights_ref, rot_ref, sums_ref, cos_ref, sin_ref = args[16:]
-    core, x, y_lo, z, y_hi = core_ref[0], x_ref[0], y_lo_ref[0], z_ref[0], y_hi_ref[0]
+def weights_times_images(which, core, y_lo, weights, ins, rot_ref, sums_ref):
+    cos_ref, sin_ref, own_ref, recv_ref = ins
+    rows = own_ref.shape[2]
+    trans = cos_ref.shape[1]
+    low = low_rows()
+    on_x = core == 0
+
+    def step(at, carry):
+        item, p = at // 2, at % 2
+        far = item // 2
+        xr = jnp.where(on_x, 1 + 2 * far if which else 2 - 2 * far, item)
+        part = jnp.where(on_x, item % 2, which ^ y_lo)
+        b = part ^ y_lo
+        sign = (1 - 2 * part).astype(jnp.float32)
+        for c in range(SIDE // CHUNK):
+            lanes = pl.ds(pl.multiple_of(p * SIDE + c * CHUNK, CHUNK), CHUNK)
+            for h, half_ref in enumerate((own_ref, recv_ref)):
+                one = half_ref[part, xr, :, lanes].astype(jnp.float32)
+                two = half_ref[1 - part, xr, :, lanes].astype(jnp.float32) * sign
+                for t in range(trans):
+                    cosine, sine = cos_ref[xr, t : t + 1, lanes], sin_ref[xr, t : t + 1, lanes]
+                    base = (h * trans + t) * rows
+                    rot_ref[c, base : base + rows, :] = (one * cosine + two * sine).astype(
+                        jnp.bfloat16
+                    )
+            product = lax.dot_general(
+                weights, rot_ref[c], (((1,), (0,)), ((), ())), preferred_element_type=jnp.float32
+            )
+            for a in range(2):
+                i = jnp.where(on_x, far, a if which else 1 - a)
+                j = jnp.where(on_x, 2 * a + b, xr)
+                for k in range(8):
+                    row = 24 * k
+                    ref = sums_ref.at[i, j, k, p]
+                    for g in range(2):
+                        to = 8 * (2 * c + g)
+                        ref[to : to + 8] = product[
+                            row + 8 * a : row + 8 * a + 8, g * LANES : (g + 1) * LANES
+                        ]
+                    one = product[row + 16 : row + 24, :LANES]
+                    two = product[row + 16 : row + 24, LANES:]
+                    if a == 0:
+                        tail = jnp.where(low, one, pltpu.roll(two, 4, 0))
+                    else:
+                        tail = jnp.where(low, pltpu.roll(one, 4, 0), two)
+                    to = 8 * (GROUPS + c)
+                    ref[to : to + 8] = tail
+        return carry
+
+    lax.fori_loop(0, 8, step, 0)
+
+
+def first_kernel(scale, *args):
+    core_ref, y_lo_ref, z_ref, y_hi_ref, mine_ref, theirs_ref, lists_ref = args[:7]
+    ins, (stays, to_one, to_three, flipped_ref, evidence_ref, totals_ref) = args[7:11], args[11:17]
+    weights_ref, rot_ref, sums_ref = args[17:]
+    z, y_hi = z_ref[0], y_hi_ref[0]
     softmax(scale, z, y_hi, mine_ref, theirs_ref, lists_ref, weights_ref, evidence_ref)
     flipped = weights_ref[...].T
     refs_all, rows = flipped.shape[0], flipped.shape[1] - 8
@@ -260,77 +306,44 @@
     totals_ref[1:2, : refs_all - LANES] = totals[:, LANES:]
     parts = three_parts(totals_ref[...])
     totals_ref[...] = whole(parts)
-    to_one[64] = parts
-    to_three[64] = parts
+    to_one[32] = parts
+    to_three[32] = parts
     weights = flipped[:, :rows].astype(jnp.bfloat16)
-    low = low_rows()
-
-    def step(at, carry):
-        xr, p = at // 2, at % 2
-        for c in range(SIDE // CHUNK):
-            start = pl.multiple_of(p * SIDE + c * CHUNK, CHUNK)
-
-            def put(part, base, rows, value):
-                rot_ref[c, part, base : base + rows, :] = value
-
-            tables = cos_ref.at[c], sin_ref.at[c]
-            rotate_chunk(core, x, shifts_ref, own_ref, recv_ref, xr, start, tables, put)
-            for part in range(2):
-                product = lax.dot_general(
-                    weights,
-                    rot_ref[c, part],
-                    (((1,), (0,)), ((), ())),
-                    preferred_element_type=jnp.float32,
-                )
-                for a in range(2):
-                    y = 2 * a + (part ^ y_lo)
-                    i, j = jnp.where(core == 0, xr, y), jnp.where(core == 0, y, xr)
-                    for k in range(8):
-                        row = 24 * k
-                        ref = sums_ref.at[i, j, k, p]
-                        for g in range(2):
-                            to = 8 * (2 * c + g)
-                            ref[to : to + 8] = product[
-                                row + 8 * a : row + 8 * a + 8, g * LANES : (g + 1) * LANES
-                            ]
-                        one = product[row + 16 : row + 24, :LANES]
-                        two = product[row + 16 : row + 24, LANES:]
-                        if a == 0:
-                            tail = jnp.where(low, one, pltpu.roll(two, 4, 0))
-                        else:
-                            tail = jnp.where(low, pltpu.roll(one, 4, 0), two)
-                        to = 8 * (GROUPS + c)
-                        ref[to : to + 8] = tail
-        return carry
-
-    lax.fori_loop(0, 8, step, 0)
+    flipped_ref[...] = weights
+    weights_times_images(0, core_ref[0], y_lo_ref[0], weights, ins, rot_ref, sums_ref)
     for place in range(4):
-        stays[place] = sums_ref[0, place]
-        for distance, low_ref, low_at, high_ref, high_at in (
-            (2, to_one, 0, to_three, 0),
-            (1, to_one, 32, one_high, 0),
-            (3, three_low, 0, to_three, 32),
-        ):
+        stays[place] = sums_ref[1, place]
+        for k in range(4):
+            for p in range(2):
+                at = 8 * place + 2 * k + p
+                to_one[at] = sums_ref[0, place, k, p].astype(jnp.bfloat16)
+                to_three[at] = sums_ref[0, place, 4 + k, p].astype(jnp.bfloat16)
+
+
+def second_kernel(core_ref, y_lo_ref, flipped_ref, *args):
+    ins, (one_low, one_high, three_low, three_high), (rot_ref, sums_ref) = args[:4], args[4:8], args[8:]
+    weights = flipped_ref[...]
+    weights_times_images(1, core_ref[0], y_lo_ref[0], weights, ins, rot_ref, sums_ref)
+    for place in range(4):
+        for n, (low_ref, high_ref) in enumerate(((one_low, one_high), (three_low, three_high))):
             for k in range(4):
                 for p in range(2):
                     at = 8 * place + 2 * k + p
-                    low = sums_ref[distance, place, k, p]
-                    high = sums_ref[distance, place, 4 + k, p]
-                    low_ref[low_at + at] = low.astype(low_ref.dtype)
-                    high_ref[high_at + at] = high.astype(high_ref.dtype)
+                    low_ref[at] = sums_ref[n, place, k, p].astype(low_ref.dtype)
+                    high_ref[at] = sums_ref[n, place, 4 + k, p].astype(high_ref.dtype)
 
 
 def add_kernel(
-    totals_ref, one_ref, three_ref, from_one, from_three, one_out, three_out, both_ref, third_ref
+    totals_ref, one_ref, three_ref, far_one, far_three, one_out, three_out, both_ref, third_ref
 ):
-    one_out[0:32] = (one_ref[...] + from_three[0:32].astype(jnp.float32)).astype(jnp.bfloat16)
-    one_out[32] = from_three[64]
-    three_out[...] = (three_ref[...] + from_one[0:32].astype(jnp.float32)).astype(jnp.bfloat16)
-    both_ref[...] = totals_ref[...] + whole(from_one[64])
-    third_ref[...] = whole(from_three[64])
-
-
-def middle_kernel(both_ref, third_ref, stays, from_one, one_high, three_low, from_three, *outs):
+    one_out[0:32] = (one_ref[...] + far_three[0:32].astype(jnp.float32)).astype(jnp.bfloat16)
+    one_out[32] = far_three[32]
+    three_out[...] = (three_ref[...] + far_one[0:32].astype(jnp.float32)).astype(jnp.bfloat16)
+    both_ref[...] = totals_ref[...] + whole(far_one[32])
+    third_ref[...] = whole(far_three[32])
+
+
+def middle_kernel(both_ref, third_ref, stays, one_low, one_high, three_low, three_high, *outs):
     totals_ref = outs[-1]
     totals = both_ref[...] + (whole(one_high[32]) + third_ref[...])
     parts = three_parts(totals)
@@ -338,15 +351,12 @@
     for n, out_ref in enumerate(outs[:-1]):
         if n:
             out_ref[16] = parts
-        for ks, one, one_at, three, three_at in (
-            (0, from_one, 32, three_low, 0),
-            (4, one_high, 0, from_three, 32),
-        ):
+        for ks, one, three in ((0, one_low, three_low), (4, one_high, three_high)):
             for k in range(4):
                 for p in range(2):
                     at = 8 * n + 2 * k + p
-                    total = stays[n, ks + k, p] + one[one_at + at].astype(jnp.float32)
-                    total = total + three[three_at + at].astype(jnp.float32)
+                    total = stays[n, ks + k, p] + one[at].astype(jnp.float32)
+                    total = total + three[at].astype(jnp.float32)
                     out_ref[2 * (ks + k) + p] = total.astype(out_ref.dtype)
 
 
@@ -467,21 +477,19 @@
     slot = jnp.arange(lists.shape[1], dtype=jnp.int32)[None, :]
     used = jnp.where(slot < counts[:, None], lists, -1)
     used_pair = jnp.stack([used, lax.ppermute(used, "core", swap)])
-    tables = [pltpu.VMEM((trans, CHUNK), f32)] * 2
-    rots = []
+    rots, tables = [], []
     for first_xr in (0, 2):
-        rots.append(
-            call(
-                "rotate",
-                functools.partial(rotate_kernel, first_xr),
-                [core, x, y_lo, shifts, own, recv],
-                shape(2, 2, rows, BLOCK),
-                [SMEM] * 3 + [VMEM] * 3,
-                tables,
-                8,
-                3,
-            )
+        table = shape(first_xr + 2, trans, BLOCK, dtype=f32)
+        rotated, *tables = call(
+            "rotate",
+            functools.partial(rotate_kernel, first_xr),
+            [core, x, y_lo, shifts, own, recv] + tables,
+            [shape(2, 2, rows, BLOCK), table, table],
+            [SMEM] * 3 + [VMEM] * (3 + len(tables)),
+            mebibytes=8,
+            micros=3,
         )
+        rots.append(rotated)
     blocks = call(
         "stack",
         stack_kernel,
@@ -512,37 +520,43 @@
 
     scale = (2 * ctf.shape[1]) ** -0.5
     part16, part32 = shape(32, HALF, LANES), shape(32, HALF, LANES, dtype=f32)
-    more16, both16 = shape(33, HALF, LANES), shape(65, HALF, LANES)
-    row = shape(8, LANES, dtype=f32)
-    stays, to_one, to_three, one_high, three_low, evidence, totals = call(
-        "backward",
-        lambda *args: backward_kernel(scale, *args),
-        [core, x, y_lo, z, y_hi, scores, theirs, used_pair, shifts, own, recv],
-        [shape(4, 8, 2, HALF, LANES, dtype=f32), both16, both16, part32, part32]
+    more16, row = shape(33, HALF, LANES), shape(8, LANES, dtype=f32)
+    ins = tables + [own, recv]
+    scratch = [pltpu.VMEM((2, rows, CHUNK), bf16), pltpu.VMEM((2, 4, 8, 2, HALF, LANES), f32)]
+    stays, to_one, to_three, flipped, evidence, totals = call(
+        "first",
+        functools.partial(first_kernel, scale),
+        [core, y_lo, z, y_hi, scores, theirs, used_pair] + ins,
+        [shape(4, 8, 2, HALF, LANES, dtype=f32), more16, more16, shape(refs_all, rows)]
         + [shape(parts, 1, dtype=f32), row],
-        [SMEM] * 5 + [VMEM] * 6,
-        [
-            pltpu.VMEM((rows + 8, refs_all), f32),
-            pltpu.VMEM((2, 2, rows, CHUNK), bf16),
-            pltpu.VMEM((4, 4, 8, 2, HALF, LANES), f32),
-            pltpu.VMEM((2, trans, CHUNK), f32),
-            pltpu.VMEM((2, trans, CHUNK), f32),
-        ],
-        24,
-        10,
-    )
-    from_one, from_three = over(to_one, 1, 0), over(to_three, 3, 0)
+        [SMEM] * 4 + [VMEM] * 7,
+        [pltpu.VMEM((rows + 8, refs_all), f32)] + scratch,
+        16,
+        6,
+    )
+    far_one, far_three = over(to_one, 1, 0), over(to_three, 3, 0)
+    one_low, one_high, three_low, three_high = call(
+        "second",
+        second_kernel,
+        [core, y_lo, flipped] + ins,
+        [part16, part32, part32, part16],
+        [SMEM] * 2 + [VMEM] * 5,
+        scratch,
+        16,
+        4,
+    )
+    one_low, three_high = over(one_low, 1, 0), over(three_high, 3, 0)
     one_high, three_low, both, third = call(
         "add",
         add_kernel,
-        [totals, one_high, three_low, from_one, from_three],
+        [totals, one_high, three_low, far_one, far_three],
         [more16, part16, row, row],
     )
     one_high, three_low = over(one_high, 1, 0), over(three_low, 3, 0)
     *middle, totals = call(
         "middle",
         middle_kernel,
-        [both, third, stays, from_one, one_high, three_low, from_three],
+        [both, third, stays, one_low, one_high, three_low, three_high],
         [shape(16, HALF, LANES, dtype=f32)] + [shape(17, HALF, LANES)] * 3 + [row],
     )
     came = [over(middle[m], m, 1) for m in (1, 2, 3)]

time: 123 us -> 122 us (level)
  waiting for transfers between devices: 54 us -> 47.9 us
  starting transfers between devices: 41.4 us -> 45 us
  Pallas kernels: 20.6 us -> 21.9 us
    ppermute x16 -> x18, waiting for transfers between devices: 42.6 us -> 36.4 us  [over(): return lax.ppermute(value, ('y_lo', 'x', 'core', 'y_hi'), pairs)]
    ppermute x16 -> x18, starting transfers between devices: 15.6 us -> 19 us  [over(): return lax.ppermute(value, ('y_lo', 'x', 'core', 'y_hi'), pairs)]
    pallas_call x16 -> x17, Pallas kernels: 20.6 us -> 21.9 us  [call(): pl.pallas_call(kernel, out_shape=outs, in_specs=specs or [VMEM] * len(ins...]
  transfers between devices with their start and end apart: 28 -> 30, of which waited for: 17 -> 19; matrix products, arithmetic and copies ran while one was open for 1% -> 1% of each run, Pallas kernels for 5% -> 8%
where the time goes in v3:
time: 122 us; the launch traced here: 121 us
  waiting for transfers between devices  47.9 us (39%)
  starting transfers between devices  45 us (37%)
  Pallas kernels  21.9 us (18%)
  local copies, waits for them, and re-layouts  4.95 us (4%)
    ppermute x18, waiting for transfers between devices, over(): return lax.ppermute(value, ('y_lo', 'x', 'core', 'y_hi'), pairs)  36.4 us
    pallas_call x17, Pallas kernels, call(): pl.pallas_call(kernel, out_shape=outs, in_specs=specs or [VMEM] * len(ins...  21.9 us
    ppermute x18, starting transfers between devices, over(): return lax.ppermute(value, ('y_lo', 'x', 'core', 'y_hi'), pairs)  19 us
    ppermute x8, starting transfers between devices, over_z(): return lax.ppermute(value, 'z', [(i, i ^ bits) for i in range(8)])  16.6 us
    ppermute x8, waiting for transfers between devices, over_z(): return lax.ppermute(value, 'z', [(i, i ^ bits) for i in range(8)])  9.01 us
    unnamed x12, local copies, waits for them, and re-layouts  4.44 us
    ppermute x1, starting transfers between devices, local(): came = lax.ppermute(give, 'core', swap)  3.96 us
    ppermute x1, starting transfers between devices, local(): theirs = lax.ppermute(scores, 'core', swap)  3.01 us
  transfers between devices with their start and end apart: 30, of which 19 were waited for; matrix products, arithmetic and copies ran while one was open for 1% of the time, Pallas kernels for 8%

profile of v3, /device:TPU:1, one launch (start us, length us, event | category | flops | bytes accessed | tf_op | source)
XLA Modules:
  0.0 121.4 jit_solution(3142158496615332977)
XLA Ops:
  0.7 1.0 copy-done.2
  1.7 3.9 %collective-permute-start = (bf16[1,2,48,128]{3,2,1,0:T(8,128)(2,1)S(1)}, bf16[1,2,48,128]{3,2,1,0:T(8,128)(2,1)S(1)}, u32[]{:S(2)}, u32[]{:S(2)}) collective-permute-start(bf16[1,2,48,128]{3,2,1,0:T(8,128)(2,1)S(1)} %pack.1.before_ref.args_0_), channel_id=1, source_target_pairs={{0,4},{2,6},{4,0},{6,2},{8,12},{10,14},{12,8},{14,10},{1,5},{3,7},... | collective-permute-start | bytes 73736 | tf_op jit(solution)/shard_map/ppermute | solution.py:26
  5.6 5.1 %collective-permute-start.1 = (bf16[1,2,48,128]{3,2,1,0:T(8,128)(2,1)S(1)}, bf16[1,2,48,128]{3,2,1,0:T(8,128)(2,1)S(1)}, u32[]{:S(2)}, u32[]{:S(2)}) collective-permute-start(bf16[1,2,48,128]{3,2,1,0:T(8,128)(2,1)S(1)} %pack.1.before_ref.args_0_), channel_id=1, source_target_pairs={{0,8},{2,10},{4,12},{6,14},{8,0},{10,2},{12,4},{14,6},{1,9},{3,11}... | collective-permute-start | bytes 73736 | tf_op jit(solution)/shard_map/ppermute | solution.py:26
  10.7 1.4 %copy-done = bf16[48,16384]{1,0:T(8,128)(2,1)S(1)} copy-done((bf16[48,16384]{1,0:T(8,128)(2,1)S(1)}, bf16[48,16384]{1,0:T(8,128)(2,1)}, u32[]{:S(2)}) %copy-start) | copy-done | bytes 1572888
  12.1 1.1 copy-done.1
  13.3 0.3 weighted.1
  13.6 1.9 %collective-permute-done.2.args_3_ = bf16[1,2,48,128]{3,2,1,0:T(8,128)(2,1)S(1)} collective-permute-done((bf16[1,2,48,128]{3,2,1,0:T(8,128)(2,1)S(1)}, bf16[1,2,48,128]{3,2,1,0:T(8,128)(2,1)S(1)}, u32[]{:S(2)}, u32[]{:S(2)}) %collective-permute-start.2) | collective-permute-done | bytes 24608 | tf_op jit(solution)/shard_map/ppermute | solution.py:26
  15.6 2.5 %collective-permute-start.4 = (bf16[2,4,48,1024]{3,2,1,0:T(8,128)(2,1)S(1)}, bf16[2,4,48,1024]{3,2,1,0:T(8,128)(2,1)S(1)}, u32[]{:S(2)}, u32[]{:S(2)}) collective-permute-start(bf16[2,4,48,1024]{3,2,1,0:T(8,128)(2,1)S(1)} %hold.1), channel_id=1, source_target_pairs={{0,16},{16,0},{1,17},{17,1},{2,18},{18,2},{3,19},{19,3},{4,20},{20... | collective-permute-start | bytes 2359304 | tf_op jit(solution)/shard_map/ppermute | solution.py:476
  18.0 0.8 collective-permute-start.3
  18.8 0.8 copy.19.shifts_ref
  19.6 0.4 collective-permute-done.4.recv_ref.args_10_.args_3_
  19.9 2.8 %rotate.2 = (bf16[2,2,864,1024]{3,2,1,0:T(8,128)(2,1)S(1)}, f32[2,9,1024]{2,1,0:T(8,128)S(1)}, f32[2,9,1024]{2,1,0:T(8,128)S(1)}) custom-call(s32[1]{0:T(128)} %bitcast.core_ref.args_0_, s32[1]{0:T(128)} %bitcast.6.x_ref, s32[1]{0:T(128)} %bitcast.2.part_ref.args_1_.y_lo_ref, s32[9,2]{1,0:T(8,128)S(1)} %copy.19.shifts_ref, ...), custom_call_target="tpu_custom_call" | custom-call | flops 3000000 | bytes 9000000 | tf_op jit(solution)/shard_map/rotate/pallas_call | solution.py:421
  22.8 1.3 %collective-permute-start.5 = (bf16[8,2,48,128]{3,2,1,0:T(8,128)(2,1)S(1)}, bf16[8,2,48,128]{3,2,1,0:T(8,128)(2,1)S(1)}, u32[]{:S(2)}, u32[]{:S(2)}) collective-permute-start(bf16[8,2,48,128]{3,2,1,0:T(8,128)(2,1)S(1)} %stack.15.own_ref), channel_id=1, source_target_pairs={{0,128},{1,129},{16,48},{17,49},{32,160},{33,161},{48,16},{49,17},... | collective-permute-start | bytes 589832 | tf_op jit(solution)/shard_map/ppermute | solution.py:41
  24.1 2.5 %collective-permute-start.6 = (bf16[8,2,48,128]{3,2,1,0:T(8,128)(2,1)S(1)}, bf16[8,2,48,128]{3,2,1,0:T(8,128)(2,1)S(1)}, u32[]{:S(2)}, u32[]{:S(2)}) collective-permute-start(bf16[8,2,48,128]{3,2,1,0:T(8,128)(2,1)S(1)} %stack.15.own_ref), channel_id=1, source_target_pairs={{0,1},{1,0},{16,80},{17,81},{32,33},{33,32},{48,112},{49,113},{64,... | collective-permute-start | bytes 589832 | tf_op jit(solution)/shard_map/ppermute | solution.py:41
  26.6 0.2 collective-permute-start.7
  26.8 2.8 %rotate.3 = (bf16[2,2,864,1024]{3,2,1,0:T(8,128)(2,1)S(1)}, f32[4,9,1024]{2,1,0:T(8,128)S(1)}, f32[4,9,1024]{2,1,0:T(8,128)S(1)}) custom-call(s32[1]{0:T(128)} %bitcast.core_ref.args_0_, s32[1]{0:T(128)} %bitcast.6.x_ref, s32[1]{0:T(128)} %bitcast.2.part_ref.args_1_.y_lo_ref, s32[9,2]{1,0:T(8,128)S(1)} %copy.19.shifts_ref, ...), custom_call_target="tpu_custom_call" | custom-call | flops 3000000 | bytes 9000000 | tf_op jit(solution)/shard_map/rotate/pallas_call | solution.py:421
  29.6 2.4 %collective-permute-done.6.two_ref = bf16[8,2,48,128]{3,2,1,0:T(8,128)(2,1)S(1)} collective-permute-done((bf16[8,2,48,128]{3,2,1,0:T(8,128)(2,1)S(1)}, bf16[8,2,48,128]{3,2,1,0:T(8,128)(2,1)S(1)}, u32[]{:S(2)}, u32[]{:S(2)}) %collective-permute-start.6) | collective-permute-done | bytes 196640 | tf_op jit(solution)/shard_map/ppermute | solution.py:41
  32.0 2.1 %collective-permute-done.7.three_ref = bf16[8,2,48,128]{3,2,1,0:T(8,128)(2,1)S(1)} collective-permute-done((bf16[8,2,48,128]{3,2,1,0:T(8,128)(2,1)S(1)}, bf16[8,2,48,128]{3,2,1,0:T(8,128)(2,1)S(1)}, u32[]{:S(2)}, u32[]{:S(2)}) %collective-permute-start.7) | collective-permute-done | bytes 196640 | tf_op jit(solution)/shard_map/ppermute | solution.py:41
  34.2 1.1 collective-permute-start.8
  35.3 1.9 %collective-permute-start.11 = (bf16[2,8,2,48,128]{4,3,2,1,0:T(8,128)(2,1)S(1)}, bf16[2,8,2,48,128]{4,3,2,1,0:T(8,128)(2,1)S(1)}, u32[]{:S(2)}, u32[]{:S(2)}) collective-permute-start(bf16[2,8,2,48,128]{4,3,2,1,0:T(8,128)(2,1)S(1)} %get-tuple-element.51.args_2_), channel_id=1, source_target_pairs={{0,96},{1,97},{16,145},{17,144},{32,64},{33,65},{48,177},{49,176},... | collective-permute-start | bytes 1179656 | tf_op jit(solution)/shard_map/ppermute | solution.py:41
  37.2 0.8 collective-permute-start.13
  38.0 3.2 %collective-permute-done.8.args_3_ = bf16[2,8,2,48,128]{4,3,2,1,0:T(8,128)(2,1)S(1)} collective-permute-done((bf16[2,8,2,48,128]{4,3,2,1,0:T(8,128)(2,1)S(1)}, bf16[2,8,2,48,128]{4,3,2,1,0:T(8,128)(2,1)S(1)}, u32[]{:S(2)}, u32[]{:S(2)}) %collective-permute-start.8) | collective-permute-done | bytes 393248 | tf_op jit(solution)/shard_map/ppermute | solution.py:41
  41.2 2.4 %collective-permute-start.10 = (bf16[2,8,2,48,128]{4,3,2,1,0:T(8,128)(2,1)S(1)}, bf16[2,8,2,48,128]{4,3,2,1,0:T(8,128)(2,1)S(1)}, u32[]{:S(2)}, u32[]{:S(2)}) collective-permute-start(bf16[2,8,2,48,128]{4,3,2,1,0:T(8,128)(2,1)S(1)} %collective-permute-done.8.args_3_), channel_id=1, source_target_pairs={{0,96},{1,97},{16,145},{17,144},{32,64},{33,65},{48,177},{49,176},... | collective-permute-start | bytes 1179656 | tf_op jit(solution)/shard_map/ppermute | solution.py:41
  43.6 4.0 %collective-permute-done.13.args_7_ = bf16[2,8,2,48,128]{4,3,2,1,0:T(8,128)(2,1)S(1)} collective-permute-done((bf16[2,8,2,48,128]{4,3,2,1,0:T(8,128)(2,1)S(1)}, bf16[2,8,2,48,128]{4,3,2,1,0:T(8,128)(2,1)S(1)}, u32[]{:S(2)}, u32[]{:S(2)}) %collective-permute-start.13) | collective-permute-done | bytes 393248 | tf_op jit(solution)/shard_map/ppermute | solution.py:41
  47.6 4.2 %collective-permute-done.10.args_5_ = bf16[2,8,2,48,128]{4,3,2,1,0:T(8,128)(2,1)S(1)} collective-permute-done((bf16[2,8,2,48,128]{4,3,2,1,0:T(8,128)(2,1)S(1)}, bf16[2,8,2,48,128]{4,3,2,1,0:T(8,128)(2,1)S(1)}, u32[]{:S(2)}, u32[]{:S(2)}) %collective-permute-start.10) | collective-permute-done | bytes 393248 | tf_op jit(solution)/shard_map/ppermute | solution.py:41
  51.8 4.3 %forward.1.args_4_ = f32[864,256]{1,0:T(8,128)S(1)} custom-call(s32[1]{0:T(128)} %bitcast.core_ref.args_0_, bf16[2,8,2,48,128]{4,3,2,1,0:T(8,128)(2,1)S(1)} %get-tuple-element.50.args_1_, bf16[2,8,2,48,128]{4,3,2,1,0:T(8,128)(2,1)S(1)} %get-tuple-element.51.args_2_, bf16[2,8,2,48,128]{4,3,2,1,0:T(8,128)(2,1)S(1)} %collective-permute-done.8.args_3_, ...), custom_call_target="tpu_custom_call" | custom-call | flops 4000000 | bytes 12000000 | tf_op jit(solution)/shard_map/forward/pallas_call | solution.py:421
  56.1 3.0 %collective-permute-start.14 = (f32[864,256]{1,0:T(8,128)S(1)}, f32[864,256]{1,0:T(8,128)}, u32[]{:S(2)}, u32[]{:S(2)}) collective-permute-start(f32[864,256]{1,0:T(8,128)S(1)} %forward.1.args_4_), channel_id=1, source_target_pairs={{0,16},{16,0},{1,17},{17,1},{2,18},{18,2},{3,19},{19,3},{4,20},{20... | collective-permute-start | bytes 2654216 | tf_op jit(solution)/shard_map/ppermute | solution.py:519
  59.1 0.1 copy.21
  59.2 0.1 fusion
  59.3 0.1 fusion.1
  59.4 1.8 %collective-permute-done.15 = s32[48,12]{1,0:T(8,128)S(1)} collective-permute-done((s32[48,12]{1,0:T(8,128)S(1)}, s32[48,12]{1,0:T(8,128)S(1)}, u32[]{:S(2)}, u32[]{:S(2)}) %collective-permute-start.15) | collective-permute-done | bytes 2336 | tf_op jit(solution)/shard_map/ppermute | solution.py:479
  61.2 0.1 collective-permute-done.14.args_5_
  61.3 6.2 %first.1 = (f32[4,8,2,48,128]{4,3,2,1,0:T(8,128)S(1)}, bf16[33,48,128]{2,1,0:T(8,128)(2,1)S(1)}, bf16[33,48,128]{2,1,0:T(8,128)(2,1)S(1)}, bf16[192,864]{1,0:T(8...) custom-call(s32[1]{0:T(128)} %bitcast.core_ref.args_0_, s32[1]{0:T(128)} %bitcast.2.part_ref.args_1_.y_lo_ref, ...), custom_call_target="tpu_custom_call" | custom-call | flops 6000000 | bytes 18000000 | tf_op jit(solution)/shard_map/first/pallas_call | solution.py:421
  67.5 0.1 collective-permute-start.16
  67.6 0.5 collective-permute-start.17
  68.2 4.1 %second.1 = (bf16[32,48,128]{2,1,0:T(8,128)(2,1)S(1)}, f32[32,48,128]{2,1,0:T(8,128)S(1)}, f32[32,48,128]{2,1,0:T(8,128)S(1)}, bf16[32,48,128]{2,1,0:T(8,128)(2,1)S(1)}) custom-call(s32[1]{0:T(128)} %bitcast.core_ref.args_0_, s32[1]{0:T(128)} %bitcast.2.part_ref.args_1_.y_lo_ref, bf16[192,864]{1,0:T(8,128)(2,1)S(1)} %get-tuple-element.55.flipped_ref, ...), custom_call_target="tpu_custom_call" | custom-call | flops 4000000 | bytes 12000000 | tf_op jit(solution)/shard_map/second/pallas_call | solution.py:421
  72.3 2.3 %collective-permute-done.16.far_one = bf16[33,48,128]{2,1,0:T(8,128)(2,1)S(1)} collective-permute-done((bf16[33,48,128]{2,1,0:T(8,128)(2,1)S(1)}, bf16[33,48,128]{2,1,0:T(8,128)(2,1)S(1)}, u32[]{:S(2)}, u32[]{:S(2)}) %collective-permute-start.16) | collective-permute-done | bytes 405536 | tf_op jit(solution)/shard_map/ppermute | solution.py:41
  74.7 1.3 %collective-permute-done.17.far_three = bf16[33,48,128]{2,1,0:T(8,128)(2,1)S(1)} collective-permute-done((bf16[33,48,128]{2,1,0:T(8,128)(2,1)S(1)}, bf16[33,48,128]{2,1,0:T(8,128)(2,1)S(1)}, u32[]{:S(2)}, u32[]{:S(2)}) %collective-permute-start.17) | collective-permute-done | bytes 405536 | tf_op jit(solution)/shard_map/ppermute | solution.py:41
  76.0 0.1 add.12
  76.1 0.2 collective-permute-start.19
  76.4 1.3 %collective-permute-start.18 = (bf16[32,48,128]{2,1,0:T(8,128)(2,1)S(1)}, bf16[32,48,128]{2,1,0:T(8,128)(2,1)S(1)}, u32[]{:S(2)}, u32[]{:S(2)}) collective-permute-start(bf16[32,48,128]{2,1,0:T(8,128)(2,1)S(1)} %get-tuple-element.63), channel_id=1, source_target_pairs={{0,32},{1,33},{16,144},{17,145},{32,0},{33,1},{48,176},{49,177},{6... | collective-permute-start | bytes 1179656 | tf_op jit(solution)/shard_map/ppermute | solution.py:41
  77.7 0.5 collective-permute-start.21
  78.1 2.2 %collective-permute-start.20 = (bf16[32,48,128]{2,1,0:T(8,128)(2,1)S(1)}, bf16[32,48,128]{2,1,0:T(8,128)(2,1)S(1)}, u32[]{:S(2)}, u32[]{:S(2)}) collective-permute-start(bf16[32,48,128]{2,1,0:T(8,128)(2,1)S(1)} %get-tuple-element.65), channel_id=1, source_target_pairs={{0,96},{1,97},{16,145},{17,144},{32,64},{33,65},{48,177},{49,176},... | collective-permute-start | bytes 1179656 | tf_op jit(solution)/shard_map/ppermute | solution.py:41
  80.4 7.1 %collective-permute-done.18.one_low = bf16[32,48,128]{2,1,0:T(8,128)(2,1)S(1)} collective-permute-done((bf16[32,48,128]{2,1,0:T(8,128)(2,1)S(1)}, bf16[32,48,128]{2,1,0:T(8,128)(2,1)S(1)}, u32[]{:S(2)}, u32[]{:S(2)}) %collective-permute-start.18) | collective-permute-done | bytes 393248 | tf_op jit(solution)/shard_map/ppermute | solution.py:41
  87.5 2.5 %collective-permute-done.20.three_low = bf16[32,48,128]{2,1,0:T(8,128)(2,1)S(1)} collective-permute-done((bf16[32,48,128]{2,1,0:T(8,128)(2,1)S(1)}, bf16[32,48,128]{2,1,0:T(8,128)(2,1)S(1)}, u32[]{:S(2)}, u32[]{:S(2)}) %collective-permute-start.20) | collective-permute-done | bytes 393248 | tf_op jit(solution)/shard_map/ppermute | solution.py:41
  90.0 0.3 middle.1
  90.3 0.1 collective-permute-start.22
  90.4 3.0 %collective-permute-start.23 = (bf16[17,48,128]{2,1,0:T(8,128)(2,1)S(1)}, bf16[17,48,128]{2,1,0:T(8,128)(2,1)S(1)}, u32[]{:S(2)}, u32[]{:S(2)}) collective-permute-start(bf16[17,48,128]{2,1,0:T(8,128)(2,1)S(1)} %get-tuple-element.70), channel_id=1, source_target_pairs={{0,1},{1,0},{16,80},{17,81},{32,33},{33,32},{48,112},{49,113},{64,... | collective-permute-start | bytes 626696 | tf_op jit(solution)/shard_map/ppermute | solution.py:41
  93.4 0.9 collective-permute-start.24
  94.3 0.8 collective-permute-done.22.one
  95.1 4.1 %collective-permute-done.23.two = bf16[17,48,128]{2,1,0:T(8,128)(2,1)S(1)} collective-permute-done((bf16[17,48,128]{2,1,0:T(8,128)(2,1)S(1)}, bf16[17,48,128]{2,1,0:T(8,128)(2,1)S(1)}, u32[]{:S(2)}, u32[]{:S(2)}) %collective-permute-start.23) | collective-permute-done | bytes 208928 | tf_op jit(solution)/shard_map/ppermute | solution.py:41
  99.1 2.2 %collective-permute-done.24.three = bf16[17,48,128]{2,1,0:T(8,128)(2,1)S(1)} collective-permute-done((bf16[17,48,128]{2,1,0:T(8,128)(2,1)S(1)}, bf16[17,48,128]{2,1,0:T(8,128)(2,1)S(1)}, u32[]{:S(2)}, u32[]{:S(2)}) %collective-permute-start.24) | collective-permute-done | bytes 208928 | tf_op jit(solution)/shard_map/ppermute | solution.py:41
  101.3 0.1 late.1
  101.4 1.0 collective-permute-start.25
  102.5 2.9 %collective-permute-done.25.came = bf16[9,48,128]{2,1,0:T(8,128)(2,1)S(1)} collective-permute-done((bf16[9,48,128]{2,1,0:T(8,128)(2,1)S(1)}, bf16[9,48,128]{2,1,0:T(8,128)(2,1)S(1)}, u32[]{:S(2)}, u32[]{:S(2)}) %collective-permute-start.25) | collective-permute-done | bytes 110624 | tf_op jit(solution)/shard_map/ppermute | solution.py:26
  105.4 1.3 %collective-permute-start.26 = (f32[3,48,128]{2,1,0:T(8,128)S(1)}, f32[3,48,128]{2,1,0:T(8,128)S(1)}, u32[]{:S(2)}, u32[]{:S(2)}) collective-permute-start(f32[3,48,128]{2,1,0:T(8,128)S(1)} %get-tuple-element.77), channel_id=1, source_target_pairs={{0,4},{2,6},{4,0},{6,2},{8,12},{10,14},{12,8},{14,10},{1,5},{3,7},... | collective-permute-start | bytes 221192 | tf_op jit(solution)/shard_map/ppermute | solution.py:26
  106.7 1.7 %collective-permute-start.27 = (f32[3,48,128]{2,1,0:T(8,128)S(1)}, f32[3,48,128]{2,1,0:T(8,128)S(1)}, u32[]{:S(2)}, u32[]{:S(2)}) collective-permute-start(f32[3,48,128]{2,1,0:T(8,128)S(1)} %get-tuple-element.78), channel_id=1, source_target_pairs={{0,8},{2,10},{4,12},{6,14},{8,0},{10,2},{12,4},{14,6},{1,9},{3,11}... | collective-permute-start | bytes 221192 | tf_op jit(solution)/shard_map/ppermute | solution.py:26
  108.4 2.8 %collective-permute-start.28 = (f32[3,48,128]{2,1,0:T(8,128)S(1)}, f32[3,48,128]{2,1,0:T(8,128)S(1)}, u32[]{:S(2)}, u32[]{:S(2)}) collective-permute-start(f32[3,48,128]{2,1,0:T(8,128)S(1)} %get-tuple-element.79), channel_id=1, source_target_pairs={{0,12},{2,14},{4,8},{6,10},{8,4},{10,6},{12,0},{14,2},{1,13},{3,15... | collective-permute-start | bytes 221192 | tf_op jit(solution)/shard_map/ppermute | solution.py:26
  111.1 4.2 %collective-permute-done.27.four = f32[3,48,128]{2,1,0:T(8,128)S(1)} collective-permute-done((f32[3,48,128]{2,1,0:T(8,128)S(1)}, f32[3,48,128]{2,1,0:T(8,128)S(1)}, u32[]{:S(2)}, u32[]{:S(2)}) %collective-permute-start.27) | collective-permute-done | bytes 73760 | tf_op jit(solution)/shard_map/ppermute | solution.py:26
  115.4 4.0 %collective-permute-start.29 = (f32[2,48,128]{2,1,0:T(8,128)S(1)}, f32[2,48,128]{2,1,0:T(8,128)S(1)}, u32[]{:S(2)}, u32[]{:S(2)}) collective-permute-start(f32[2,48,128]{2,1,0:T(8,128)S(1)} %get-tuple-element.81), channel_id=1, source_target_pairs={{0,16},{16,0},{1,17},{17,1},{2,18},{18,2},{3,19},{19,3},{4,20},{20... | collective-permute-start | bytes 147464 | tf_op jit(solution)/shard_map/ppermute | solution.py:577
  119.3 0.6 reduce
  120.0 0.3 collective-permute-done.29.came_ref
  120.2 0.6 last.1
  120.9 0.5 slice_bitcast_fusion
  (30 shorter events, 0.3 us)
Async XLA Ops:
  0.6 1.0 copy-start.2
  1.7 11.9 %collective-permute-start = (bf16[1,2,48,128]{3,2,1,0:T(8,128)(2,1)S(1)}, bf16[1,2,48,128]{3,2,1,0:T(8,128)(2,1)S(1)}, u32[]{:S(2)}, u32[]{:S(2)}) collective-permute-start(bf16[1,2,48,128]{3,2,1,0:T(8,128)(2,1)S(1)} %pack.1.before_ref.args_0_), channel_id=1, source_target_pairs={{0,4},{2,6},{4,0},{6,2},{8,12},{10,14},{12,8},{14,10},{1,5},{3,7},... | collective-permute-start | bytes 73736 | tf_op jit(solution)/shard_map/ppermute | solution.py:26
  5.6 8.0 %collective-permute-start.1 = (bf16[1,2,48,128]{3,2,1,0:T(8,128)(2,1)S(1)}, bf16[1,2,48,128]{3,2,1,0:T(8,128)(2,1)S(1)}, u32[]{:S(2)}, u32[]{:S(2)}) collective-permute-start(bf16[1,2,48,128]{3,2,1,0:T(8,128)(2,1)S(1)} %pack.1.before_ref.args_0_), channel_id=1, source_target_pairs={{0,8},{2,10},{4,12},{6,14},{8,0},{10,2},{12,4},{14,6},{1,9},{3,11}... | collective-permute-start | bytes 73736 | tf_op jit(solution)/shard_map/ppermute | solution.py:26
  10.7 4.8 %collective-permute-start.2 = (bf16[1,2,48,128]{3,2,1,0:T(8,128)(2,1)S(1)}, bf16[1,2,48,128]{3,2,1,0:T(8,128)(2,1)S(1)}, u32[]{:S(2)}, u32[]{:S(2)}) collective-permute-start(bf16[1,2,48,128]{3,2,1,0:T(8,128)(2,1)S(1)} %pack.1.before_ref.args_0_), channel_id=1, source_target_pairs={{0,12},{2,14},{4,8},{6,10},{8,4},{10,6},{12,0},{14,2},{1,13},{3,15... | collective-permute-start | bytes 73736 | tf_op jit(solution)/shard_map/ppermute | solution.py:26
  10.7 1.4 %copy-start = (bf16[48,16384]{1,0:T(8,128)(2,1)S(1)}, bf16[48,16384]{1,0:T(8,128)(2,1)}, u32[]{:S(2)}) copy-start(bf16[48,16384]{1,0:T(8,128)(2,1)} %images_ref.1) | copy-start | bytes 4718596
  12.1 1.1 copy-start.1
  15.6 4.4 %collective-permute-start.4 = (bf16[2,4,48,1024]{3,2,1,0:T(8,128)(2,1)S(1)}, bf16[2,4,48,1024]{3,2,1,0:T(8,128)(2,1)S(1)}, u32[]{:S(2)}, u32[]{:S(2)}) collective-permute-start(bf16[2,4,48,1024]{3,2,1,0:T(8,128)(2,1)S(1)} %hold.1), channel_id=1, source_target_pairs={{0,16},{16,0},{1,17},{17,1},{2,18},{18,2},{3,19},{19,3},{4,20},{20... | collective-permute-start | bytes 2359304 | tf_op jit(solution)/shard_map/ppermute | solution.py:476
  18.0 4.7 %collective-permute-start.3 = (bf16[4,2,48,128]{3,2,1,0:T(8,128)(2,1)S(1)}, bf16[4,2,48,128]{3,2,1,0:T(8,128)(2,1)S(1)}, u32[]{:S(2)}, u32[]{:S(2)}) collective-permute-start(bf16[4,2,48,128]{3,2,1,0:T(8,128)(2,1)S(1)} %stack.14.args_1_.args_0_), channel_id=1, source_target_pairs={{0,2},{2,0},{4,6},{6,4},{8,10},{10,8},{12,14},{14,12},{1,3},{3,1},... | collective-permute-start | bytes 294920 | tf_op jit(solution)/shard_map/ppermute | solution.py:26
  22.8 6.8 %collective-permute-start.5 = (bf16[8,2,48,128]{3,2,1,0:T(8,128)(2,1)S(1)}, bf16[8,2,48,128]{3,2,1,0:T(8,128)(2,1)S(1)}, u32[]{:S(2)}, u32[]{:S(2)}) collective-permute-start(bf16[8,2,48,128]{3,2,1,0:T(8,128)(2,1)S(1)} %stack.15.own_ref), channel_id=1, source_target_pairs={{0,128},{1,129},{16,48},{17,49},{32,160},{33,161},{48,16},{49,17},... | collective-permute-start | bytes 589832 | tf_op jit(solution)/shard_map/ppermute | solution.py:41
  24.1 7.9 %collective-permute-start.6 = (bf16[8,2,48,128]{3,2,1,0:T(8,128)(2,1)S(1)}, bf16[8,2,48,128]{3,2,1,0:T(8,128)(2,1)S(1)}, u32[]{:S(2)}, u32[]{:S(2)}) collective-permute-start(bf16[8,2,48,128]{3,2,1,0:T(8,128)(2,1)S(1)} %stack.15.own_ref), channel_id=1, source_target_pairs={{0,1},{1,0},{16,80},{17,81},{32,33},{33,32},{48,112},{49,113},{64,... | collective-permute-start | bytes 589832 | tf_op jit(solution)/shard_map/ppermute | solution.py:41
  26.6 7.6 %collective-permute-start.7 = (bf16[8,2,48,128]{3,2,1,0:T(8,128)(2,1)S(1)}, bf16[8,2,48,128]{3,2,1,0:T(8,128)(2,1)S(1)}, u32[]{:S(2)}, u32[]{:S(2)}) collective-permute-start(bf16[8,2,48,128]{3,2,1,0:T(8,128)(2,1)S(1)} %stack.15.own_ref), channel_id=1, source_target_pairs={{0,129},{1,128},{16,112},{17,113},{32,161},{33,160},{48,80},{49,81... | collective-permute-start | bytes 589832 | tf_op jit(solution)/shard_map/ppermute | solution.py:41
  34.2 7.0 %collective-permute-start.8 = (bf16[2,8,2,48,128]{4,3,2,1,0:T(8,128)(2,1)S(1)}, bf16[2,8,2,48,128]{4,3,2,1,0:T(8,128)(2,1)S(1)}, u32[]{:S(2)}, u32[]{:S(2)}) collective-permute-start(bf16[2,8,2,48,128]{4,3,2,1,0:T(8,128)(2,1)S(1)} %get-tuple-element.50.args_1_), channel_id=1, source_target_pairs={{0,32},{1,33},{16,144},{17,145},{32,0},{33,1},{48,176},{49,177},{6... | collective-permute-start | bytes 1179656 | tf_op jit(solution)/shard_map/ppermute | solution.py:41
  35.3 23.8 %copy-start.3 = (s32[48,12]{0,1:T(8,128)S(1)}, s32[48,12]{0,1:T(8,128)}, u32[]{:S(2)}) copy-start(s32[48,12]{0,1:T(8,128)} %param.10) | copy-start | bytes 6916
  35.3 23.9 %copy-start.4 = (s32[48]{0:T(128)S(1)}, s32[48]{0:T(128)}, u32[]{:S(2)}) copy-start(s32[48]{0:T(128)} %param.11) | copy-start | bytes 580
  35.3 8.4 %collective-permute-start.11 = (bf16[2,8,2,48,128]{4,3,2,1,0:T(8,128)(2,1)S(1)}, bf16[2,8,2,48,128]{4,3,2,1,0:T(8,128)(2,1)S(1)}, u32[]{:S(2)}, u32[]{:S(2)}) collective-permute-start(bf16[2,8,2,48,128]{4,3,2,1,0:T(8,128)(2,1)S(1)} %get-tuple-element.51.args_2_), channel_id=1, source_target_pairs={{0,96},{1,97},{16,145},{17,144},{32,64},{33,65},{48,177},{49,176},... | collective-permute-start | bytes 1179656 | tf_op jit(solution)/shard_map/ppermute | solution.py:41
  37.2 10.4 %collective-permute-start.13 = (bf16[2,8,2,48,128]{4,3,2,1,0:T(8,128)(2,1)S(1)}, bf16[2,8,2,48,128]{4,3,2,1,0:T(8,128)(2,1)S(1)}, u32[]{:S(2)}, u32[]{:S(2)}) collective-permute-start(bf16[2,8,2,48,128]{4,3,2,1,0:T(8,128)(2,1)S(1)} %get-tuple-element.50.args_1_), channel_id=1, source_target_pairs={{0,96},{1,97},{16,145},{17,144},{32,64},{33,65},{48,177},{49,176},... | collective-permute-start | bytes 1179656 | tf_op jit(solution)/shard_map/ppermute | solution.py:41
  38.0 9.7 %collective-permute-start.9 = (bf16[2,8,2,48,128]{4,3,2,1,0:T(8,128)(2,1)S(1)}, bf16[2,8,2,48,128]{4,3,2,1,0:T(8,128)(2,1)S(1)}, u32[]{:S(2)}, u32[]{:S(2)}) collective-permute-start(bf16[2,8,2,48,128]{4,3,2,1,0:T(8,128)(2,1)S(1)} %get-tuple-element.51.args_2_), channel_id=1, source_target_pairs={{0,32},{1,33},{16,144},{17,145},{32,0},{33,1},{48,176},{49,177},{6... | collective-permute-start | bytes 1179656 | tf_op jit(solution)/shard_map/ppermute | solution.py:41
  41.2 10.6 %collective-permute-start.10 = (bf16[2,8,2,48,128]{4,3,2,1,0:T(8,128)(2,1)S(1)}, bf16[2,8,2,48,128]{4,3,2,1,0:T(8,128)(2,1)S(1)}, u32[]{:S(2)}, u32[]{:S(2)}) collective-permute-start(bf16[2,8,2,48,128]{4,3,2,1,0:T(8,128)(2,1)S(1)} %collective-permute-done.8.args_3_), channel_id=1, source_target_pairs={{0,96},{1,97},{16,145},{17,144},{32,64},{33,65},{48,177},{49,176},... | collective-permute-start | bytes 1179656 | tf_op jit(solution)/shard_map/ppermute | solution.py:41
  43.6 8.2 %collective-permute-start.12 = (bf16[2,8,2,48,128]{4,3,2,1,0:T(8,128)(2,1)S(1)}, bf16[2,8,2,48,128]{4,3,2,1,0:T(8,128)(2,1)S(1)}, u32[]{:S(2)}, u32[]{:S(2)}) collective-permute-start(bf16[2,8,2,48,128]{4,3,2,1,0:T(8,128)(2,1)S(1)} %collective-permute-done.11.args_8_), channel_id=1, source_target_pairs={{0,32},{1,33},{16,144},{17,145},{32,0},{33,1},{48,176},{49,177},{6... | collective-permute-start | bytes 1179656 | tf_op jit(solution)/shard_map/ppermute | solution.py:41
  56.1 5.2 %collective-permute-start.14 = (f32[864,256]{1,0:T(8,128)S(1)}, f32[864,256]{1,0:T(8,128)}, u32[]{:S(2)}, u32[]{:S(2)}) collective-permute-start(f32[864,256]{1,0:T(8,128)S(1)} %forward.1.args_4_), channel_id=1, source_target_pairs={{0,16},{16,0},{1,17},{17,1},{2,18},{18,2},{3,19},{19,3},{4,20},{20... | collective-permute-start | bytes 2654216 | tf_op jit(solution)/shard_map/ppermute | solution.py:519
  59.3 1.9 %collective-permute-start.15 = (s32[48,12]{1,0:T(8,128)S(1)}, s32[48,12]{1,0:T(8,128)S(1)}, u32[]{:S(2)}, u32[]{:S(2)}) collective-permute-start(s32[48,12]{1,0:T(8,128)S(1)} %fusion), channel_id=1, source_target_pairs={{0,16},{16,0},{1,17},{17,1},{2,18},{18,2},{3,19},{19,3},{4,20},{20... | collective-permute-start | bytes 6920 | tf_op jit(solution)/shard_map/ppermute | solution.py:479
  67.5 7.1 %collective-permute-start.16 = (bf16[33,48,128]{2,1,0:T(8,128)(2,1)S(1)}, bf16[33,48,128]{2,1,0:T(8,128)(2,1)S(1)}, u32[]{:S(2)}, u32[]{:S(2)}) collective-permute-start(bf16[33,48,128]{2,1,0:T(8,128)(2,1)S(1)} %get-tuple-element.58), channel_id=1, source_target_pairs={{0,32},{1,33},{16,144},{17,145},{32,0},{33,1},{48,176},{49,177},{6... | collective-permute-start | bytes 1216520 | tf_op jit(solution)/shard_map/ppermute | solution.py:41
  67.6 8.4 %collective-permute-start.17 = (bf16[33,48,128]{2,1,0:T(8,128)(2,1)S(1)}, bf16[33,48,128]{2,1,0:T(8,128)(2,1)S(1)}, u32[]{:S(2)}, u32[]{:S(2)}) collective-permute-start(bf16[33,48,128]{2,1,0:T(8,128)(2,1)S(1)} %get-tuple-element.59), channel_id=1, source_target_pairs={{0,96},{1,97},{16,145},{17,144},{32,64},{33,65},{48,177},{49,176},... | collective-permute-start | bytes 1216520 | tf_op jit(solution)/shard_map/ppermute | solution.py:41
  76.1 13.9 %collective-permute-start.19 = (bf16[33,48,128]{2,1,0:T(8,128)(2,1)S(1)}, bf16[33,48,128]{2,1,0:T(8,128)(2,1)S(1)}, u32[]{:S(2)}, u32[]{:S(2)}) collective-permute-start(bf16[33,48,128]{2,1,0:T(8,128)(2,1)S(1)} %get-tuple-element.64), channel_id=1, source_target_pairs={{0,32},{1,33},{16,144},{17,145},{32,0},{33,1},{48,176},{49,177},{6... | collective-permute-start | bytes 1216520 | tf_op jit(solution)/shard_map/ppermute | solution.py:41
  76.4 11.1 %collective-permute-start.18 = (bf16[32,48,128]{2,1,0:T(8,128)(2,1)S(1)}, bf16[32,48,128]{2,1,0:T(8,128)(2,1)S(1)}, u32[]{:S(2)}, u32[]{:S(2)}) collective-permute-start(bf16[32,48,128]{2,1,0:T(8,128)(2,1)S(1)} %get-tuple-element.63), channel_id=1, source_target_pairs={{0,32},{1,33},{16,144},{17,145},{32,0},{33,1},{48,176},{49,177},{6... | collective-permute-start | bytes 1179656 | tf_op jit(solution)/shard_map/ppermute | solution.py:41
  77.7 9.8 %collective-permute-start.21 = (bf16[32,48,128]{2,1,0:T(8,128)(2,1)S(1)}, bf16[32,48,128]{2,1,0:T(8,128)(2,1)S(1)}, u32[]{:S(2)}, u32[]{:S(2)}) collective-permute-start(bf16[32,48,128]{2,1,0:T(8,128)(2,1)S(1)} %get-tuple-element.66), channel_id=1, source_target_pairs={{0,96},{1,97},{16,145},{17,144},{32,64},{33,65},{48,177},{49,176},... | collective-permute-start | bytes 1179656 | tf_op jit(solution)/shard_map/ppermute | solution.py:41
  78.1 11.9 %collective-permute-start.20 = (bf16[32,48,128]{2,1,0:T(8,128)(2,1)S(1)}, bf16[32,48,128]{2,1,0:T(8,128)(2,1)S(1)}, u32[]{:S(2)}, u32[]{:S(2)}) collective-permute-start(bf16[32,48,128]{2,1,0:T(8,128)(2,1)S(1)} %get-tuple-element.65), channel_id=1, source_target_pairs={{0,96},{1,97},{16,145},{17,144},{32,64},{33,65},{48,177},{49,176},... | collective-permute-start | bytes 1179656 | tf_op jit(solution)/shard_map/ppermute | solution.py:41
  90.3 4.7 %collective-permute-start.22 = (bf16[17,48,128]{2,1,0:T(8,128)(2,1)S(1)}, bf16[17,48,128]{2,1,0:T(8,128)(2,1)S(1)}, u32[]{:S(2)}, u32[]{:S(2)}) collective-permute-start(bf16[17,48,128]{2,1,0:T(8,128)(2,1)S(1)} %get-tuple-element.69), channel_id=1, source_target_pairs={{0,128},{1,129},{16,48},{17,49},{32,160},{33,161},{48,16},{49,17},... | collective-permute-start | bytes 626696 | tf_op jit(solution)/shard_map/ppermute | solution.py:41
  90.4 8.7 %collective-permute-start.23 = (bf16[17,48,128]{2,1,0:T(8,128)(2,1)S(1)}, bf16[17,48,128]{2,1,0:T(8,128)(2,1)S(1)}, u32[]{:S(2)}, u32[]{:S(2)}) collective-permute-start(bf16[17,48,128]{2,1,0:T(8,128)(2,1)S(1)} %get-tuple-element.70), channel_id=1, source_target_pairs={{0,1},{1,0},{16,80},{17,81},{32,33},{33,32},{48,112},{49,113},{64,... | collective-permute-start | bytes 626696 | tf_op jit(solution)/shard_map/ppermute | solution.py:41
  93.4 8.0 %collective-permute-start.24 = (bf16[17,48,128]{2,1,0:T(8,128)(2,1)S(1)}, bf16[17,48,128]{2,1,0:T(8,128)(2,1)S(1)}, u32[]{:S(2)}, u32[]{:S(2)}) collective-permute-start(bf16[17,48,128]{2,1,0:T(8,128)(2,1)S(1)} %get-tuple-element.71), channel_id=1, source_target_pairs={{0,129},{1,128},{16,112},{17,113},{32,161},{33,160},{48,80},{49,81... | collective-permute-start | bytes 626696 | tf_op jit(solution)/shard_map/ppermute | solution.py:41
  101.4 3.9 %collective-permute-start.25 = (bf16[9,48,128]{2,1,0:T(8,128)(2,1)S(1)}, bf16[9,48,128]{2,1,0:T(8,128)(2,1)S(1)}, u32[]{:S(2)}, u32[]{:S(2)}) collective-permute-start(bf16[9,48,128]{2,1,0:T(8,128)(2,1)S(1)} %get-tuple-element.74), channel_id=1, source_target_pairs={{0,2},{2,0},{4,6},{6,4},{8,10},{10,8},{12,14},{14,12},{1,3},{3,1},... | collective-permute-start | bytes 331784 | tf_op jit(solution)/shard_map/ppermute | solution.py:26
  105.4 5.7 %collective-permute-start.26 = (f32[3,48,128]{2,1,0:T(8,128)S(1)}, f32[3,48,128]{2,1,0:T(8,128)S(1)}, u32[]{:S(2)}, u32[]{:S(2)}) collective-permute-start(f32[3,48,128]{2,1,0:T(8,128)S(1)} %get-tuple-element.77), channel_id=1, source_target_pairs={{0,4},{2,6},{4,0},{6,2},{8,12},{10,14},{12,8},{14,10},{1,5},{3,7},... | collective-permute-start | bytes 221192 | tf_op jit(solution)/shard_map/ppermute | solution.py:26
  106.7 8.7 %collective-permute-start.27 = (f32[3,48,128]{2,1,0:T(8,128)S(1)}, f32[3,48,128]{2,1,0:T(8,128)S(1)}, u32[]{:S(2)}, u32[]{:S(2)}) collective-permute-start(f32[3,48,128]{2,1,0:T(8,128)S(1)} %get-tuple-element.78), channel_id=1, source_target_pairs={{0,8},{2,10},{4,12},{6,14},{8,0},{10,2},{12,4},{14,6},{1,9},{3,11}... | collective-permute-start | bytes 221192 | tf_op jit(solution)/shard_map/ppermute | solution.py:26
  108.4 7.0 %collective-permute-start.28 = (f32[3,48,128]{2,1,0:T(8,128)S(1)}, f32[3,48,128]{2,1,0:T(8,128)S(1)}, u32[]{:S(2)}, u32[]{:S(2)}) collective-permute-start(f32[3,48,128]{2,1,0:T(8,128)S(1)} %get-tuple-element.79), channel_id=1, source_target_pairs={{0,12},{2,14},{4,8},{6,10},{8,4},{10,6},{12,0},{14,2},{1,13},{3,15... | collective-permute-start | bytes 221192 | tf_op jit(solution)/shard_map/ppermute | solution.py:26
  115.4 4.8 %collective-permute-start.29 = (f32[2,48,128]{2,1,0:T(8,128)S(1)}, f32[2,48,128]{2,1,0:T(8,128)S(1)}, u32[]{:S(2)}, u32[]{:S(2)}) collective-permute-start(f32[2,48,128]{2,1,0:T(8,128)S(1)} %get-tuple-element.81), channel_id=1, source_target_pairs={{0,16},{16,0},{1,17},{17,1},{2,18},{18,2},{3,19},{19,3},{4,20},{20... | collective-permute-start | bytes 147464 | tf_op jit(solution)/shard_map/ppermute | solution.py:577

commit v4 on v3

--- a/solution.py
+++ b/solution.py
@@ -333,28 +333,32 @@
                     high_ref[at] = sums_ref[n, place, 4 + k, p].astype(high_ref.dtype)
 
 
-def add_kernel(
-    totals_ref, one_ref, three_ref, far_one, far_three, one_out, three_out, both_ref, third_ref
-):
-    one_out[0:32] = (one_ref[...] + far_three[0:32].astype(jnp.float32)).astype(jnp.bfloat16)
-    one_out[32] = far_three[32]
-    three_out[...] = (three_ref[...] + far_one[0:32].astype(jnp.float32)).astype(jnp.bfloat16)
+def add_kernel(*args):
+    totals_ref, one_low, one_high, three_low, three_high, far_one, far_three = args[:7]
+    one_out, three_out, both_ref, third_ref = args[7:]
+    one_out[0:32] = one_low[...]
+    total = one_high[...] + far_three[0:32].astype(jnp.float32)
+    one_out[32:64] = total.astype(jnp.bfloat16)
+    one_out[64] = far_three[32]
+    total = three_low[...] + far_one[0:32].astype(jnp.float32)
+    three_out[0:32] = total.astype(jnp.bfloat16)
+    three_out[32:64] = three_high[...]
     both_ref[...] = totals_ref[...] + whole(far_one[32])
     third_ref[...] = whole(far_three[32])
 
 
-def middle_kernel(both_ref, third_ref, stays, one_low, one_high, three_low, three_high, *outs):
+def middle_kernel(both_ref, third_ref, stays, one, three, *outs):
     totals_ref = outs[-1]
-    totals = both_ref[...] + (whole(one_high[32]) + third_ref[...])
+    totals = both_ref[...] + (whole(one[64]) + third_ref[...])
     parts = three_parts(totals)
     totals_ref[...] = whole(parts)
     for n, out_ref in enumerate(outs[:-1]):
         if n:
             out_ref[16] = parts
-        for ks, one, three in ((0, one_low, three_low), (4, one_high, three_high)):
+        for ks in (0, 4):
             for k in range(4):
                 for p in range(2):
-                    at = 8 * n + 2 * k + p
+                    at = 8 * ks + 8 * n + 2 * k + p
                     total = stays[n, ks + k, p] + one[at].astype(jnp.float32)
                     total = total + three[at].astype(jnp.float32)
                     out_ref[2 * (ks + k) + p] = total.astype(out_ref.dtype)
@@ -378,20 +382,24 @@
 
 
 def halve_kernel(totals_ref, stays, came, own_ref, two_ref, four_ref, six_ref, sum_ref):
-    totals = totals_ref[...] + whole(came[8])
-    sum_ref[...] = totals
+    parts = three_parts(totals_ref[...] + whole(came[8]))
+    sum_ref[...] = whole(parts)
     for k, ref in enumerate((own_ref, two_ref, four_ref, six_ref)):
         for p in range(2):
-            ref[p] = stays[2 * k + p] + came[2 * k + p].astype(jnp.float32)
+            total = stays[2 * k + p] + came[2 * k + p].astype(jnp.float32)
+            ref[p] = total.astype(ref.dtype)
         if k:
-            ref[2] = jnp.zeros((HALF, LANES), jnp.float32)
-            ref[2, 0:8] = totals
+            ref[2] = parts
 
 
 def deal_kernel(core_ref, totals_ref, stays, two, four, six, mine_ref, give_ref):
     first = core_ref[0] == 0
-    low, high = [(stays[p] + two[p]) + (four[p] + six[p]) for p in range(2)]
-    totals = (totals_ref[...] + two[2, 0:8]) + (four[2, 0:8] + six[2, 0:8])
+    sides = []
+    for p in range(2):
+        total = stays[p] + two[p].astype(jnp.float32)
+        sides.append(total + (four[p].astype(jnp.float32) + six[p].astype(jnp.float32)))
+    low, high = sides
+    totals = (totals_ref[...] + whole(two[2])) + (whole(four[2]) + whole(six[2]))
     mine_ref[0] = jnp.where(first, low, high)
     give_ref[0] = jnp.where(first, high, low)
     for ref in (mine_ref, give_ref):
@@ -545,18 +553,17 @@
         16,
         4,
     )
-    one_low, three_high = over(one_low, 1, 0), over(three_high, 3, 0)
-    one_high, three_low, both, third = call(
+    one, three, both, third = call(
         "add",
         add_kernel,
-        [totals, one_high, three_low, far_one, far_three],
-        [more16, part16, row, row],
-    )
-    one_high, three_low = over(one_high, 1, 0), over(three_low, 3, 0)
+        [totals, one_low, one_high, three_low, three_high, far_one, far_three],
+        [shape(65, HALF, LANES), shape(64, HALF, LANES), row, row],
+    )
+    one, three = over(one, 1, 0), over(three, 3, 0)
     *middle, totals = call(
         "middle",
         middle_kernel,
-        [both, third, stays, one_low, one_high, three_low, three_high],
+        [both, third, stays, one, three],
         [shape(16, HALF, LANES, dtype=f32)] + [shape(17, HALF, LANES)] * 3 + [row],
     )
     came = [over(middle[m], m, 1) for m in (1, 2, 3)]
@@ -566,9 +573,9 @@
         [totals, middle[0]] + came,
         [shape(8, HALF, LANES, dtype=f32), shape(9, HALF, LANES), row],
     )
-    two32, three32 = shape(2, HALF, LANES, dtype=f32), shape(3, HALF, LANES, dtype=f32)
+    two32, three16 = shape(2, HALF, LANES, dtype=f32), shape(3, HALF, LANES)
     own, *others, totals = call(
-        "halve", halve_kernel, [totals, even, over_z(odd, 1)], [two32, three32, three32, three32, row]
+        "halve", halve_kernel, [totals, even, over_z(odd, 1)], [two32, three16, three16, three16, row]
     )
     others = [over_z(other, bits) for other, bits in zip(others, (2, 4, 6))]
     mine, give = call(

time: 122 us -> 120 us (0.984)
  starting transfers between devices: 45 us -> 41.9 us
    ppermute x18 -> x16, starting transfers between devices: 19 us -> 15.6 us  [over(): return lax.ppermute(value, ('y_lo', 'x', 'core', 'y_hi'), pairs)]
    ppermute x18 -> x16, waiting for transfers between devices: 36.4 us -> 38.4 us  [over(): return lax.ppermute(value, ('y_lo', 'x', 'core', 'y_hi'), pairs)]
  transfers between devices with their start and end apart: 30 -> 28, of which waited for: 19 -> 18; matrix products, arithmetic and copies ran while one was open for 1% -> 1% of each run, Pallas kernels for 8% -> 8%
where the time goes in v4:
time: 120 us; the launch traced here: 119 us
  waiting for transfers between devices  48.8 us (41%)
  starting transfers between devices  41.9 us (35%)
  Pallas kernels  22 us (18%)
  local copies, waits for them, and re-layouts  4.95 us (4%)
    ppermute x16, waiting for transfers between devices, over(): return lax.ppermute(value, ('y_lo', 'x', 'core', 'y_hi'), pairs)  38.4 us
    pallas_call x17, Pallas kernels, call(): pl.pallas_call(kernel, out_shape=outs, in_specs=specs or [VMEM] * len(ins...  22 us
    ppermute x8, starting transfers between devices, over_z(): return lax.ppermute(value, 'z', [(i, i ^ bits) for i in range(8)])  16.3 us
    ppermute x16, starting transfers between devices, over(): return lax.ppermute(value, ('y_lo', 'x', 'core', 'y_hi'), pairs)  15.6 us
    ppermute x8, waiting for transfers between devices, over_z(): return lax.ppermute(value, 'z', [(i, i ^ bits) for i in range(8)])  7.81 us
    ppermute x1, starting transfers between devices, local(): came = lax.ppermute(give, 'core', swap)  4.47 us
    unnamed x12, local copies, waits for them, and re-layouts  4.44 us
    ppermute x1, starting transfers between devices, local(): theirs = lax.ppermute(scores, 'core', swap)  3.01 us
  transfers between devices with their start and end apart: 28, of which 18 were waited for; matrix products, arithmetic and copies ran while one was open for 1% of the time, Pallas kernels for 8%

profile of v4, /device:TPU:1, one launch (start us, length us, event | category | flops | bytes accessed | tf_op | source)
XLA Modules:
  0.0 119.2 jit_solution(14340124282862528178)
XLA Ops:
  0.7 1.0 copy-done.2
  1.7 3.9 %collective-permute-start = (bf16[1,2,48,128]{3,2,1,0:T(8,128)(2,1)S(1)}, bf16[1,2,48,128]{3,2,1,0:T(8,128)(2,1)S(1)}, u32[]{:S(2)}, u32[]{:S(2)}) collective-permute-start(bf16[1,2,48,128]{3,2,1,0:T(8,128)(2,1)S(1)} %pack.1.before_ref.args_0_), channel_id=1, source_target_pairs={{0,4},{2,6},{4,0},{6,2},{8,12},{10,14},{12,8},{14,10},{1,5},{3,7},... | collective-permute-start | bytes 73736 | tf_op jit(solution)/shard_map/ppermute | solution.py:26
  5.6 5.1 %collective-permute-start.1 = (bf16[1,2,48,128]{3,2,1,0:T(8,128)(2,1)S(1)}, bf16[1,2,48,128]{3,2,1,0:T(8,128)(2,1)S(1)}, u32[]{:S(2)}, u32[]{:S(2)}) collective-permute-start(bf16[1,2,48,128]{3,2,1,0:T(8,128)(2,1)S(1)} %pack.1.before_ref.args_0_), channel_id=1, source_target_pairs={{0,8},{2,10},{4,12},{6,14},{8,0},{10,2},{12,4},{14,6},{1,9},{3,11}... | collective-permute-start | bytes 73736 | tf_op jit(solution)/shard_map/ppermute | solution.py:26
  10.7 1.4 %copy-done = bf16[48,16384]{1,0:T(8,128)(2,1)S(1)} copy-done((bf16[48,16384]{1,0:T(8,128)(2,1)S(1)}, bf16[48,16384]{1,0:T(8,128)(2,1)}, u32[]{:S(2)}) %copy-start) | copy-done | bytes 1572888
  12.1 1.1 copy-done.1
  13.3 0.3 weighted.1
  13.6 1.9 %collective-permute-done.2.args_3_ = bf16[1,2,48,128]{3,2,1,0:T(8,128)(2,1)S(1)} collective-permute-done((bf16[1,2,48,128]{3,2,1,0:T(8,128)(2,1)S(1)}, bf16[1,2,48,128]{3,2,1,0:T(8,128)(2,1)S(1)}, u32[]{:S(2)}, u32[]{:S(2)}) %collective-permute-start.2) | collective-permute-done | bytes 24608 | tf_op jit(solution)/shard_map/ppermute | solution.py:26
  15.5 0.1 hold.1
  15.6 2.5 %collective-permute-start.4 = (bf16[2,4,48,1024]{3,2,1,0:T(8,128)(2,1)S(1)}, bf16[2,4,48,1024]{3,2,1,0:T(8,128)(2,1)S(1)}, u32[]{:S(2)}, u32[]{:S(2)}) collective-permute-start(bf16[2,4,48,1024]{3,2,1,0:T(8,128)(2,1)S(1)} %hold.1), channel_id=1, source_target_pairs={{0,16},{16,0},{1,17},{17,1},{2,18},{18,2},{3,19},{19,3},{4,20},{20... | collective-permute-start | bytes 2359304 | tf_op jit(solution)/shard_map/ppermute | solution.py:484
  18.0 0.8 collective-permute-start.3
  18.8 0.8 copy.19.shifts_ref
  19.6 0.4 collective-permute-done.4.recv_ref.args_10_.args_3_
  19.9 2.8 %rotate.2 = (bf16[2,2,864,1024]{3,2,1,0:T(8,128)(2,1)S(1)}, f32[2,9,1024]{2,1,0:T(8,128)S(1)}, f32[2,9,1024]{2,1,0:T(8,128)S(1)}) custom-call(s32[1]{0:T(128)} %bitcast.core_ref.args_0_, s32[1]{0:T(128)} %bitcast.6.x_ref, s32[1]{0:T(128)} %bitcast.2.part_ref.args_1_.y_lo_ref, s32[9,2]{1,0:T(8,128)S(1)} %copy.19.shifts_ref, ...), custom_call_target="tpu_custom_call" | custom-call | flops 3000000 | bytes 9000000 | tf_op jit(solution)/shard_map/rotate/pallas_call | solution.py:429
  22.8 1.3 %collective-permute-start.5 = (bf16[8,2,48,128]{3,2,1,0:T(8,128)(2,1)S(1)}, bf16[8,2,48,128]{3,2,1,0:T(8,128)(2,1)S(1)}, u32[]{:S(2)}, u32[]{:S(2)}) collective-permute-start(bf16[8,2,48,128]{3,2,1,0:T(8,128)(2,1)S(1)} %stack.15.own_ref), channel_id=1, source_target_pairs={{0,128},{1,129},{16,48},{17,49},{32,160},{33,161},{48,16},{49,17},... | collective-permute-start | bytes 589832 | tf_op jit(solution)/shard_map/ppermute | solution.py:41
  24.1 2.5 %collective-permute-start.6 = (bf16[8,2,48,128]{3,2,1,0:T(8,128)(2,1)S(1)}, bf16[8,2,48,128]{3,2,1,0:T(8,128)(2,1)S(1)}, u32[]{:S(2)}, u32[]{:S(2)}) collective-permute-start(bf16[8,2,48,128]{3,2,1,0:T(8,128)(2,1)S(1)} %stack.15.own_ref), channel_id=1, source_target_pairs={{0,1},{1,0},{16,80},{17,81},{32,33},{33,32},{48,112},{49,113},{64,... | collective-permute-start | bytes 589832 | tf_op jit(solution)/shard_map/ppermute | solution.py:41
  26.6 0.2 collective-permute-start.7
  26.8 2.8 %rotate.3 = (bf16[2,2,864,1024]{3,2,1,0:T(8,128)(2,1)S(1)}, f32[4,9,1024]{2,1,0:T(8,128)S(1)}, f32[4,9,1024]{2,1,0:T(8,128)S(1)}) custom-call(s32[1]{0:T(128)} %bitcast.core_ref.args_0_, s32[1]{0:T(128)} %bitcast.6.x_ref, s32[1]{0:T(128)} %bitcast.2.part_ref.args_1_.y_lo_ref, s32[9,2]{1,0:T(8,128)S(1)} %copy.19.shifts_ref, ...), custom_call_target="tpu_custom_call" | custom-call | flops 3000000 | bytes 9000000 | tf_op jit(solution)/shard_map/rotate/pallas_call | solution.py:429
  29.6 2.4 %collective-permute-done.6.two_ref = bf16[8,2,48,128]{3,2,1,0:T(8,128)(2,1)S(1)} collective-permute-done((bf16[8,2,48,128]{3,2,1,0:T(8,128)(2,1)S(1)}, bf16[8,2,48,128]{3,2,1,0:T(8,128)(2,1)S(1)}, u32[]{:S(2)}, u32[]{:S(2)}) %collective-permute-start.6) | collective-permute-done | bytes 196640 | tf_op jit(solution)/shard_map/ppermute | solution.py:41
  32.0 2.1 %collective-permute-done.7.three_ref = bf16[8,2,48,128]{3,2,1,0:T(8,128)(2,1)S(1)} collective-permute-done((bf16[8,2,48,128]{3,2,1,0:T(8,128)(2,1)S(1)}, bf16[8,2,48,128]{3,2,1,0:T(8,128)(2,1)S(1)}, u32[]{:S(2)}, u32[]{:S(2)}) %collective-permute-start.7) | collective-permute-done | bytes 196640 | tf_op jit(solution)/shard_map/ppermute | solution.py:41
  34.1 0.1 join.1
  34.2 1.1 collective-permute-start.8
  35.3 1.9 %collective-permute-start.11 = (bf16[2,8,2,48,128]{4,3,2,1,0:T(8,128)(2,1)S(1)}, bf16[2,8,2,48,128]{4,3,2,1,0:T(8,128)(2,1)S(1)}, u32[]{:S(2)}, u32[]{:S(2)}) collective-permute-start(bf16[2,8,2,48,128]{4,3,2,1,0:T(8,128)(2,1)S(1)} %get-tuple-element.51.args_2_), channel_id=1, source_target_pairs={{0,96},{1,97},{16,145},{17,144},{32,64},{33,65},{48,177},{49,176},... | collective-permute-start | bytes 1179656 | tf_op jit(solution)/shard_map/ppermute | solution.py:41
  37.2 0.8 collective-permute-start.13
  38.0 3.2 %collective-permute-done.8.args_3_ = bf16[2,8,2,48,128]{4,3,2,1,0:T(8,128)(2,1)S(1)} collective-permute-done((bf16[2,8,2,48,128]{4,3,2,1,0:T(8,128)(2,1)S(1)}, bf16[2,8,2,48,128]{4,3,2,1,0:T(8,128)(2,1)S(1)}, u32[]{:S(2)}, u32[]{:S(2)}) %collective-permute-start.8) | collective-permute-done | bytes 393248 | tf_op jit(solution)/shard_map/ppermute | solution.py:41
  41.2 2.4 %collective-permute-start.10 = (bf16[2,8,2,48,128]{4,3,2,1,0:T(8,128)(2,1)S(1)}, bf16[2,8,2,48,128]{4,3,2,1,0:T(8,128)(2,1)S(1)}, u32[]{:S(2)}, u32[]{:S(2)}) collective-permute-start(bf16[2,8,2,48,128]{4,3,2,1,0:T(8,128)(2,1)S(1)} %collective-permute-done.8.args_3_), channel_id=1, source_target_pairs={{0,96},{1,97},{16,145},{17,144},{32,64},{33,65},{48,177},{49,176},... | collective-permute-start | bytes 1179656 | tf_op jit(solution)/shard_map/ppermute | solution.py:41
  43.6 4.0 %collective-permute-done.13.args_7_ = bf16[2,8,2,48,128]{4,3,2,1,0:T(8,128)(2,1)S(1)} collective-permute-done((bf16[2,8,2,48,128]{4,3,2,1,0:T(8,128)(2,1)S(1)}, bf16[2,8,2,48,128]{4,3,2,1,0:T(8,128)(2,1)S(1)}, u32[]{:S(2)}, u32[]{:S(2)}) %collective-permute-start.13) | collective-permute-done | bytes 393248 | tf_op jit(solution)/shard_map/ppermute | solution.py:41
  47.6 4.2 %collective-permute-done.10.args_5_ = bf16[2,8,2,48,128]{4,3,2,1,0:T(8,128)(2,1)S(1)} collective-permute-done((bf16[2,8,2,48,128]{4,3,2,1,0:T(8,128)(2,1)S(1)}, bf16[2,8,2,48,128]{4,3,2,1,0:T(8,128)(2,1)S(1)}, u32[]{:S(2)}, u32[]{:S(2)}) %collective-permute-start.10) | collective-permute-done | bytes 393248 | tf_op jit(solution)/shard_map/ppermute | solution.py:41
  51.8 4.3 %forward.1.args_4_ = f32[864,256]{1,0:T(8,128)S(1)} custom-call(s32[1]{0:T(128)} %bitcast.core_ref.args_0_, bf16[2,8,2,48,128]{4,3,2,1,0:T(8,128)(2,1)S(1)} %get-tuple-element.50.args_1_, bf16[2,8,2,48,128]{4,3,2,1,0:T(8,128)(2,1)S(1)} %get-tuple-element.51.args_2_, bf16[2,8,2,48,128]{4,3,2,1,0:T(8,128)(2,1)S(1)} %collective-permute-done.8.args_3_, ...), custom_call_target="tpu_custom_call" | custom-call | flops 4000000 | bytes 12000000 | tf_op jit(solution)/shard_map/forward/pallas_call | solution.py:429
  56.1 3.0 %collective-permute-start.14 = (f32[864,256]{1,0:T(8,128)S(1)}, f32[864,256]{1,0:T(8,128)}, u32[]{:S(2)}, u32[]{:S(2)}) collective-permute-start(f32[864,256]{1,0:T(8,128)S(1)} %forward.1.args_4_), channel_id=1, source_target_pairs={{0,16},{16,0},{1,17},{17,1},{2,18},{18,2},{3,19},{19,3},{4,20},{20... | collective-permute-start | bytes 2654216 | tf_op jit(solution)/shard_map/ppermute | solution.py:527
  59.1 0.1 copy.21
  59.2 0.1 fusion
  59.3 0.1 collective-permute-start.15
  59.3 0.1 fusion.1
  59.4 1.8 %collective-permute-done.15 = s32[48,12]{1,0:T(8,128)S(1)} collective-permute-done((s32[48,12]{1,0:T(8,128)S(1)}, s32[48,12]{1,0:T(8,128)S(1)}, u32[]{:S(2)}, u32[]{:S(2)}) %collective-permute-start.15) | collective-permute-done | bytes 2336 | tf_op jit(solution)/shard_map/ppermute | solution.py:487
  61.2 0.1 collective-permute-done.14.args_5_
  61.3 6.2 %first.1 = (f32[4,8,2,48,128]{4,3,2,1,0:T(8,128)S(1)}, bf16[33,48,128]{2,1,0:T(8,128)(2,1)S(1)}, bf16[33,48,128]{2,1,0:T(8,128)(2,1)S(1)}, bf16[192,864]{1,0:T(8...) custom-call(s32[1]{0:T(128)} %bitcast.core_ref.args_0_, s32[1]{0:T(128)} %bitcast.2.part_ref.args_1_.y_lo_ref, ...), custom_call_target="tpu_custom_call" | custom-call | flops 6000000 | bytes 18000000 | tf_op jit(solution)/shard_map/first/pallas_call | solution.py:429
  67.5 0.1 collective-permute-start.16
  67.6 0.5 collective-permute-start.17
  68.2 4.1 %second.1 = (bf16[32,48,128]{2,1,0:T(8,128)(2,1)S(1)}, f32[32,48,128]{2,1,0:T(8,128)S(1)}, f32[32,48,128]{2,1,0:T(8,128)S(1)}, bf16[32,48,128]{2,1,0:T(8,128)(2,1)S(1)}) custom-call(s32[1]{0:T(128)} %bitcast.core_ref.args_0_, s32[1]{0:T(128)} %bitcast.2.part_ref.args_1_.y_lo_ref, bf16[192,864]{1,0:T(8,128)(2,1)S(1)} %get-tuple-element.55.flipped_ref, ...), custom_call_target="tpu_custom_call" | custom-call | flops 4000000 | bytes 12000000 | tf_op jit(solution)/shard_map/second/pallas_call | solution.py:429
  72.3 2.3 %collective-permute-done.16.args_5_ = bf16[33,48,128]{2,1,0:T(8,128)(2,1)S(1)} collective-permute-done((bf16[33,48,128]{2,1,0:T(8,128)(2,1)S(1)}, bf16[33,48,128]{2,1,0:T(8,128)(2,1)S(1)}, u32[]{:S(2)}, u32[]{:S(2)}) %collective-permute-start.16) | collective-permute-done | bytes 405536 | tf_op jit(solution)/shard_map/ppermute | solution.py:41
  74.7 1.3 %collective-permute-done.17.args_6_ = bf16[33,48,128]{2,1,0:T(8,128)(2,1)S(1)} collective-permute-done((bf16[33,48,128]{2,1,0:T(8,128)(2,1)S(1)}, bf16[33,48,128]{2,1,0:T(8,128)(2,1)S(1)}, u32[]{:S(2)}, u32[]{:S(2)}) %collective-permute-start.17) | collective-permute-done | bytes 405536 | tf_op jit(solution)/shard_map/ppermute | solution.py:41
  76.0 0.2 add.12
  76.2 0.2 collective-permute-start.18
  76.5 0.6 collective-permute-start.19
  77.1 11.7 %collective-permute-done.19.three = bf16[64,48,128]{2,1,0:T(8,128)(2,1)S(1)} collective-permute-done((bf16[64,48,128]{2,1,0:T(8,128)(2,1)S(1)}, bf16[64,48,128]{2,1,0:T(8,128)(2,1)S(1)}, u32[]{:S(2)}, u32[]{:S(2)}) %collective-permute-start.19) | collective-permute-done | bytes 786464 | tf_op jit(solution)/shard_map/ppermute | solution.py:41
  88.8 0.3 middle.1
  89.1 0.1 collective-permute-start.20
  89.2 3.0 %collective-permute-start.21 = (bf16[17,48,128]{2,1,0:T(8,128)(2,1)S(1)}, bf16[17,48,128]{2,1,0:T(8,128)(2,1)S(1)}, u32[]{:S(2)}, u32[]{:S(2)}) collective-permute-start(bf16[17,48,128]{2,1,0:T(8,128)(2,1)S(1)} %get-tuple-element.70), channel_id=1, source_target_pairs={{0,1},{1,0},{16,80},{17,81},{32,33},{33,32},{48,112},{49,113},{64,... | collective-permute-start | bytes 626696 | tf_op jit(solution)/shard_map/ppermute | solution.py:41
  92.2 0.9 collective-permute-start.22
  93.0 0.8 collective-permute-done.20.one
  93.8 4.1 %collective-permute-done.21.two = bf16[17,48,128]{2,1,0:T(8,128)(2,1)S(1)} collective-permute-done((bf16[17,48,128]{2,1,0:T(8,128)(2,1)S(1)}, bf16[17,48,128]{2,1,0:T(8,128)(2,1)S(1)}, u32[]{:S(2)}, u32[]{:S(2)}) %collective-permute-start.21) | collective-permute-done | bytes 208928 | tf_op jit(solution)/shard_map/ppermute | solution.py:41
  97.9 2.2 %collective-permute-done.22.three = bf16[17,48,128]{2,1,0:T(8,128)(2,1)S(1)} collective-permute-done((bf16[17,48,128]{2,1,0:T(8,128)(2,1)S(1)}, bf16[17,48,128]{2,1,0:T(8,128)(2,1)S(1)}, u32[]{:S(2)}, u32[]{:S(2)}) %collective-permute-start.22) | collective-permute-done | bytes 208928 | tf_op jit(solution)/shard_map/ppermute | solution.py:41
  100.1 0.1 late.1
  100.2 0.8 collective-permute-start.23
  101.1 2.9 %collective-permute-done.23.came = bf16[9,48,128]{2,1,0:T(8,128)(2,1)S(1)} collective-permute-done((bf16[9,48,128]{2,1,0:T(8,128)(2,1)S(1)}, bf16[9,48,128]{2,1,0:T(8,128)(2,1)S(1)}, u32[]{:S(2)}, u32[]{:S(2)}) %collective-permute-start.23) | collective-permute-done | bytes 110624 | tf_op jit(solution)/shard_map/ppermute | solution.py:26
  103.9 1.3 %collective-permute-start.24 = (bf16[3,48,128]{2,1,0:T(8,128)(2,1)S(1)}, bf16[3,48,128]{2,1,0:T(8,128)(2,1)S(1)}, u32[]{:S(2)}, u32[]{:S(2)}) collective-permute-start(bf16[3,48,128]{2,1,0:T(8,128)(2,1)S(1)} %get-tuple-element.77), channel_id=1, source_target_pairs={{0,4},{2,6},{4,0},{6,2},{8,12},{10,14},{12,8},{14,10},{1,5},{3,7},... | collective-permute-start | bytes 110600 | tf_op jit(solution)/shard_map/ppermute | solution.py:26
  105.2 1.7 %collective-permute-start.25 = (bf16[3,48,128]{2,1,0:T(8,128)(2,1)S(1)}, bf16[3,48,128]{2,1,0:T(8,128)(2,1)S(1)}, u32[]{:S(2)}, u32[]{:S(2)}) collective-permute-start(bf16[3,48,128]{2,1,0:T(8,128)(2,1)S(1)} %get-tuple-element.78), channel_id=1, source_target_pairs={{0,8},{2,10},{4,12},{6,14},{8,0},{10,2},{12,4},{14,6},{1,9},{3,11}... | collective-permute-start | bytes 110600 | tf_op jit(solution)/shard_map/ppermute | solution.py:26
  106.9 2.8 %collective-permute-start.26 = (bf16[3,48,128]{2,1,0:T(8,128)(2,1)S(1)}, bf16[3,48,128]{2,1,0:T(8,128)(2,1)S(1)}, u32[]{:S(2)}, u32[]{:S(2)}) collective-permute-start(bf16[3,48,128]{2,1,0:T(8,128)(2,1)S(1)} %get-tuple-element.79), channel_id=1, source_target_pairs={{0,12},{2,14},{4,8},{6,10},{8,4},{10,6},{12,0},{14,2},{1,13},{3,15... | collective-permute-start | bytes 110600 | tf_op jit(solution)/shard_map/ppermute | solution.py:26
  109.7 3.0 %collective-permute-done.25.four = bf16[3,48,128]{2,1,0:T(8,128)(2,1)S(1)} collective-permute-done((bf16[3,48,128]{2,1,0:T(8,128)(2,1)S(1)}, bf16[3,48,128]{2,1,0:T(8,128)(2,1)S(1)}, u32[]{:S(2)}, u32[]{:S(2)}) %collective-permute-start.25) | collective-permute-done | bytes 36896 | tf_op jit(solution)/shard_map/ppermute | solution.py:26
  112.7 4.5 %collective-permute-start.27 = (f32[2,48,128]{2,1,0:T(8,128)S(1)}, f32[2,48,128]{2,1,0:T(8,128)S(1)}, u32[]{:S(2)}, u32[]{:S(2)}) collective-permute-start(f32[2,48,128]{2,1,0:T(8,128)S(1)} %get-tuple-element.81), channel_id=1, source_target_pairs={{0,16},{16,0},{1,17},{17,1},{2,18},{18,2},{3,19},{19,3},{4,20},{20... | collective-permute-start | bytes 147464 | tf_op jit(solution)/shard_map/ppermute | solution.py:584
  117.2 0.6 reduce
  117.8 0.3 collective-permute-done.27.came_ref
  118.1 0.6 last.1
  118.7 0.5 slice_bitcast_fusion
  (26 shorter events, 0.1 us)
Async XLA Ops:
  0.6 1.0 copy-start.2
  1.7 11.9 %collective-permute-start = (bf16[1,2,48,128]{3,2,1,0:T(8,128)(2,1)S(1)}, bf16[1,2,48,128]{3,2,1,0:T(8,128)(2,1)S(1)}, u32[]{:S(2)}, u32[]{:S(2)}) collective-permute-start(bf16[1,2,48,128]{3,2,1,0:T(8,128)(2,1)S(1)} %pack.1.before_ref.args_0_), channel_id=1, source_target_pairs={{0,4},{2,6},{4,0},{6,2},{8,12},{10,14},{12,8},{14,10},{1,5},{3,7},... | collective-permute-start | bytes 73736 | tf_op jit(solution)/shard_map/ppermute | solution.py:26
  5.6 8.0 %collective-permute-start.1 = (bf16[1,2,48,128]{3,2,1,0:T(8,128)(2,1)S(1)}, bf16[1,2,48,128]{3,2,1,0:T(8,128)(2,1)S(1)}, u32[]{:S(2)}, u32[]{:S(2)}) collective-permute-start(bf16[1,2,48,128]{3,2,1,0:T(8,128)(2,1)S(1)} %pack.1.before_ref.args_0_), channel_id=1, source_target_pairs={{0,8},{2,10},{4,12},{6,14},{8,0},{10,2},{12,4},{14,6},{1,9},{3,11}... | collective-permute-start | bytes 73736 | tf_op jit(solution)/shard_map/ppermute | solution.py:26
  10.7 4.8 %collective-permute-start.2 = (bf16[1,2,48,128]{3,2,1,0:T(8,128)(2,1)S(1)}, bf16[1,2,48,128]{3,2,1,0:T(8,128)(2,1)S(1)}, u32[]{:S(2)}, u32[]{:S(2)}) collective-permute-start(bf16[1,2,48,128]{3,2,1,0:T(8,128)(2,1)S(1)} %pack.1.before_ref.args_0_), channel_id=1, source_target_pairs={{0,12},{2,14},{4,8},{6,10},{8,4},{10,6},{12,0},{14,2},{1,13},{3,15... | collective-permute-start | bytes 73736 | tf_op jit(solution)/shard_map/ppermute | solution.py:26
  10.7 1.4 %copy-start = (bf16[48,16384]{1,0:T(8,128)(2,1)S(1)}, bf16[48,16384]{1,0:T(8,128)(2,1)}, u32[]{:S(2)}) copy-start(bf16[48,16384]{1,0:T(8,128)(2,1)} %images_ref.1) | copy-start | bytes 4718596
  12.1 1.1 copy-start.1
  15.6 4.4 %collective-permute-start.4 = (bf16[2,4,48,1024]{3,2,1,0:T(8,128)(2,1)S(1)}, bf16[2,4,48,1024]{3,2,1,0:T(8,128)(2,1)S(1)}, u32[]{:S(2)}, u32[]{:S(2)}) collective-permute-start(bf16[2,4,48,1024]{3,2,1,0:T(8,128)(2,1)S(1)} %hold.1), channel_id=1, source_target_pairs={{0,16},{16,0},{1,17},{17,1},{2,18},{18,2},{3,19},{19,3},{4,20},{20... | collective-permute-start | bytes 2359304 | tf_op jit(solution)/shard_map/ppermute | solution.py:484
  18.0 4.7 %collective-permute-start.3 = (bf16[4,2,48,128]{3,2,1,0:T(8,128)(2,1)S(1)}, bf16[4,2,48,128]{3,2,1,0:T(8,128)(2,1)S(1)}, u32[]{:S(2)}, u32[]{:S(2)}) collective-permute-start(bf16[4,2,48,128]{3,2,1,0:T(8,128)(2,1)S(1)} %stack.14.args_1_.args_0_), channel_id=1, source_target_pairs={{0,2},{2,0},{4,6},{6,4},{8,10},{10,8},{12,14},{14,12},{1,3},{3,1},... | collective-permute-start | bytes 294920 | tf_op jit(solution)/shard_map/ppermute | solution.py:26
  22.8 6.8 %collective-permute-start.5 = (bf16[8,2,48,128]{3,2,1,0:T(8,128)(2,1)S(1)}, bf16[8,2,48,128]{3,2,1,0:T(8,128)(2,1)S(1)}, u32[]{:S(2)}, u32[]{:S(2)}) collective-permute-start(bf16[8,2,48,128]{3,2,1,0:T(8,128)(2,1)S(1)} %stack.15.own_ref), channel_id=1, source_target_pairs={{0,128},{1,129},{16,48},{17,49},{32,160},{33,161},{48,16},{49,17},... | collective-permute-start | bytes 589832 | tf_op jit(solution)/shard_map/ppermute | solution.py:41
  24.1 7.9 %collective-permute-start.6 = (bf16[8,2,48,128]{3,2,1,0:T(8,128)(2,1)S(1)}, bf16[8,2,48,128]{3,2,1,0:T(8,128)(2,1)S(1)}, u32[]{:S(2)}, u32[]{:S(2)}) collective-permute-start(bf16[8,2,48,128]{3,2,1,0:T(8,128)(2,1)S(1)} %stack.15.own_ref), channel_id=1, source_target_pairs={{0,1},{1,0},{16,80},{17,81},{32,33},{33,32},{48,112},{49,113},{64,... | collective-permute-start | bytes 589832 | tf_op jit(solution)/shard_map/ppermute | solution.py:41
  26.6 7.6 %collective-permute-start.7 = (bf16[8,2,48,128]{3,2,1,0:T(8,128)(2,1)S(1)}, bf16[8,2,48,128]{3,2,1,0:T(8,128)(2,1)S(1)}, u32[]{:S(2)}, u32[]{:S(2)}) collective-permute-start(bf16[8,2,48,128]{3,2,1,0:T(8,128)(2,1)S(1)} %stack.15.own_ref), channel_id=1, source_target_pairs={{0,129},{1,128},{16,112},{17,113},{32,161},{33,160},{48,80},{49,81... | collective-permute-start | bytes 589832 | tf_op jit(solution)/shard_map/ppermute | solution.py:41
  34.2 7.0 %collective-permute-start.8 = (bf16[2,8,2,48,128]{4,3,2,1,0:T(8,128)(2,1)S(1)}, bf16[2,8,2,48,128]{4,3,2,1,0:T(8,128)(2,1)S(1)}, u32[]{:S(2)}, u32[]{:S(2)}) collective-permute-start(bf16[2,8,2,48,128]{4,3,2,1,0:T(8,128)(2,1)S(1)} %get-tuple-element.50.args_1_), channel_id=1, source_target_pairs={{0,32},{1,33},{16,144},{17,145},{32,0},{33,1},{48,176},{49,177},{6... | collective-permute-start | bytes 1179656 | tf_op jit(solution)/shard_map/ppermute | solution.py:41
  35.3 23.8 %copy-start.3 = (s32[48,12]{0,1:T(8,128)S(1)}, s32[48,12]{0,1:T(8,128)}, u32[]{:S(2)}) copy-start(s32[48,12]{0,1:T(8,128)} %param.10) | copy-start | bytes 6916
  35.3 23.9 %copy-start.4 = (s32[48]{0:T(128)S(1)}, s32[48]{0:T(128)}, u32[]{:S(2)}) copy-start(s32[48]{0:T(128)} %param.11) | copy-start | bytes 580
  35.3 8.4 %collective-permute-start.11 = (bf16[2,8,2,48,128]{4,3,2,1,0:T(8,128)(2,1)S(1)}, bf16[2,8,2,48,128]{4,3,2,1,0:T(8,128)(2,1)S(1)}, u32[]{:S(2)}, u32[]{:S(2)}) collective-permute-start(bf16[2,8,2,48,128]{4,3,2,1,0:T(8,128)(2,1)S(1)} %get-tuple-element.51.args_2_), channel_id=1, source_target_pairs={{0,96},{1,97},{16,145},{17,144},{32,64},{33,65},{48,177},{49,176},... | collective-permute-start | bytes 1179656 | tf_op jit(solution)/shard_map/ppermute | solution.py:41
  37.2 10.4 %collective-permute-start.13 = (bf16[2,8,2,48,128]{4,3,2,1,0:T(8,128)(2,1)S(1)}, bf16[2,8,2,48,128]{4,3,2,1,0:T(8,128)(2,1)S(1)}, u32[]{:S(2)}, u32[]{:S(2)}) collective-permute-start(bf16[2,8,2,48,128]{4,3,2,1,0:T(8,128)(2,1)S(1)} %get-tuple-element.50.args_1_), channel_id=1, source_target_pairs={{0,96},{1,97},{16,145},{17,144},{32,64},{33,65},{48,177},{49,176},... | collective-permute-start | bytes 1179656 | tf_op jit(solution)/shard_map/ppermute | solution.py:41
  38.0 9.7 %collective-permute-start.9 = (bf16[2,8,2,48,128]{4,3,2,1,0:T(8,128)(2,1)S(1)}, bf16[2,8,2,48,128]{4,3,2,1,0:T(8,128)(2,1)S(1)}, u32[]{:S(2)}, u32[]{:S(2)}) collective-permute-start(bf16[2,8,2,48,128]{4,3,2,1,0:T(8,128)(2,1)S(1)} %get-tuple-element.51.args_2_), channel_id=1, source_target_pairs={{0,32},{1,33},{16,144},{17,145},{32,0},{33,1},{48,176},{49,177},{6... | collective-permute-start | bytes 1179656 | tf_op jit(solution)/shard_map/ppermute | solution.py:41
  41.2 10.6 %collective-permute-start.10 = (bf16[2,8,2,48,128]{4,3,2,1,0:T(8,128)(2,1)S(1)}, bf16[2,8,2,48,128]{4,3,2,1,0:T(8,128)(2,1)S(1)}, u32[]{:S(2)}, u32[]{:S(2)}) collective-permute-start(bf16[2,8,2,48,128]{4,3,2,1,0:T(8,128)(2,1)S(1)} %collective-permute-done.8.args_3_), channel_id=1, source_target_pairs={{0,96},{1,97},{16,145},{17,144},{32,64},{33,65},{48,177},{49,176},... | collective-permute-start | bytes 1179656 | tf_op jit(solution)/shard_map/ppermute | solution.py:41
  43.6 8.2 %collective-permute-start.12 = (bf16[2,8,2,48,128]{4,3,2,1,0:T(8,128)(2,1)S(1)}, bf16[2,8,2,48,128]{4,3,2,1,0:T(8,128)(2,1)S(1)}, u32[]{:S(2)}, u32[]{:S(2)}) collective-permute-start(bf16[2,8,2,48,128]{4,3,2,1,0:T(8,128)(2,1)S(1)} %collective-permute-done.11.args_8_), channel_id=1, source_target_pairs={{0,32},{1,33},{16,144},{17,145},{32,0},{33,1},{48,176},{49,177},{6... | collective-permute-start | bytes 1179656 | tf_op jit(solution)/shard_map/ppermute | solution.py:41
  56.1 5.2 %collective-permute-start.14 = (f32[864,256]{1,0:T(8,128)S(1)}, f32[864,256]{1,0:T(8,128)}, u32[]{:S(2)}, u32[]{:S(2)}) collective-permute-start(f32[864,256]{1,0:T(8,128)S(1)} %forward.1.args_4_), channel_id=1, source_target_pairs={{0,16},{16,0},{1,17},{17,1},{2,18},{18,2},{3,19},{19,3},{4,20},{20... | collective-permute-start | bytes 2654216 | tf_op jit(solution)/shard_map/ppermute | solution.py:527
  59.3 1.9 %collective-permute-start.15 = (s32[48,12]{1,0:T(8,128)S(1)}, s32[48,12]{1,0:T(8,128)S(1)}, u32[]{:S(2)}, u32[]{:S(2)}) collective-permute-start(s32[48,12]{1,0:T(8,128)S(1)} %fusion), channel_id=1, source_target_pairs={{0,16},{16,0},{1,17},{17,1},{2,18},{18,2},{3,19},{19,3},{4,20},{20... | collective-permute-start | bytes 6920 | tf_op jit(solution)/shard_map/ppermute | solution.py:487
  67.5 7.1 %collective-permute-start.16 = (bf16[33,48,128]{2,1,0:T(8,128)(2,1)S(1)}, bf16[33,48,128]{2,1,0:T(8,128)(2,1)S(1)}, u32[]{:S(2)}, u32[]{:S(2)}) collective-permute-start(bf16[33,48,128]{2,1,0:T(8,128)(2,1)S(1)} %get-tuple-element.60), channel_id=1, source_target_pairs={{0,32},{1,33},{16,144},{17,145},{32,0},{33,1},{48,176},{49,177},{6... | collective-permute-start | bytes 1216520 | tf_op jit(solution)/shard_map/ppermute | solution.py:41
  67.6 8.4 %collective-permute-start.17 = (bf16[33,48,128]{2,1,0:T(8,128)(2,1)S(1)}, bf16[33,48,128]{2,1,0:T(8,128)(2,1)S(1)}, u32[]{:S(2)}, u32[]{:S(2)}) collective-permute-start(bf16[33,48,128]{2,1,0:T(8,128)(2,1)S(1)} %get-tuple-element.61), channel_id=1, source_target_pairs={{0,96},{1,97},{16,145},{17,144},{32,64},{33,65},{48,177},{49,176},... | collective-permute-start | bytes 1216520 | tf_op jit(solution)/shard_map/ppermute | solution.py:41
  76.2 12.6 %collective-permute-start.18 = (bf16[65,48,128]{2,1,0:T(8,128)(2,1)S(1)}, bf16[65,48,128]{2,1,0:T(8,128)(2,1)S(1)}, u32[]{:S(2)}, u32[]{:S(2)}) collective-permute-start(bf16[65,48,128]{2,1,0:T(8,128)(2,1)S(1)} %get-tuple-element.65), channel_id=1, source_target_pairs={{0,32},{1,33},{16,144},{17,145},{32,0},{33,1},{48,176},{49,177},{6... | collective-permute-start | bytes 2396168 | tf_op jit(solution)/shard_map/ppermute | solution.py:41
  76.5 12.3 %collective-permute-start.19 = (bf16[64,48,128]{2,1,0:T(8,128)(2,1)S(1)}, bf16[64,48,128]{2,1,0:T(8,128)(2,1)S(1)}, u32[]{:S(2)}, u32[]{:S(2)}) collective-permute-start(bf16[64,48,128]{2,1,0:T(8,128)(2,1)S(1)} %get-tuple-element.66), channel_id=1, source_target_pairs={{0,96},{1,97},{16,145},{17,144},{32,64},{33,65},{48,177},{49,176},... | collective-permute-start | bytes 2359304 | tf_op jit(solution)/shard_map/ppermute | solution.py:41
  89.1 4.7 %collective-permute-start.20 = (bf16[17,48,128]{2,1,0:T(8,128)(2,1)S(1)}, bf16[17,48,128]{2,1,0:T(8,128)(2,1)S(1)}, u32[]{:S(2)}, u32[]{:S(2)}) collective-permute-start(bf16[17,48,128]{2,1,0:T(8,128)(2,1)S(1)} %get-tuple-element.69), channel_id=1, source_target_pairs={{0,128},{1,129},{16,48},{17,49},{32,160},{33,161},{48,16},{49,17},... | collective-permute-start | bytes 626696 | tf_op jit(solution)/shard_map/ppermute | solution.py:41
  89.2 8.7 %collective-permute-start.21 = (bf16[17,48,128]{2,1,0:T(8,128)(2,1)S(1)}, bf16[17,48,128]{2,1,0:T(8,128)(2,1)S(1)}, u32[]{:S(2)}, u32[]{:S(2)}) collective-permute-start(bf16[17,48,128]{2,1,0:T(8,128)(2,1)S(1)} %get-tuple-element.70), channel_id=1, source_target_pairs={{0,1},{1,0},{16,80},{17,81},{32,33},{33,32},{48,112},{49,113},{64,... | collective-permute-start | bytes 626696 | tf_op jit(solution)/shard_map/ppermute | solution.py:41
  92.2 8.0 %collective-permute-start.22 = (bf16[17,48,128]{2,1,0:T(8,128)(2,1)S(1)}, bf16[17,48,128]{2,1,0:T(8,128)(2,1)S(1)}, u32[]{:S(2)}, u32[]{:S(2)}) collective-permute-start(bf16[17,48,128]{2,1,0:T(8,128)(2,1)S(1)} %get-tuple-element.71), channel_id=1, source_target_pairs={{0,129},{1,128},{16,112},{17,113},{32,161},{33,160},{48,80},{49,81... | collective-permute-start | bytes 626696 | tf_op jit(solution)/shard_map/ppermute | solution.py:41
  100.2 3.7 %collective-permute-start.23 = (bf16[9,48,128]{2,1,0:T(8,128)(2,1)S(1)}, bf16[9,48,128]{2,1,0:T(8,128)(2,1)S(1)}, u32[]{:S(2)}, u32[]{:S(2)}) collective-permute-start(bf16[9,48,128]{2,1,0:T(8,128)(2,1)S(1)} %get-tuple-element.74), channel_id=1, source_target_pairs={{0,2},{2,0},{4,6},{6,4},{8,10},{10,8},{12,14},{14,12},{1,3},{3,1},... | collective-permute-start | bytes 331784 | tf_op jit(solution)/shard_map/ppermute | solution.py:26
  103.9 5.7 %collective-permute-start.24 = (bf16[3,48,128]{2,1,0:T(8,128)(2,1)S(1)}, bf16[3,48,128]{2,1,0:T(8,128)(2,1)S(1)}, u32[]{:S(2)}, u32[]{:S(2)}) collective-permute-start(bf16[3,48,128]{2,1,0:T(8,128)(2,1)S(1)} %get-tuple-element.77), channel_id=1, source_target_pairs={{0,4},{2,6},{4,0},{6,2},{8,12},{10,14},{12,8},{14,10},{1,5},{3,7},... | collective-permute-start | bytes 110600 | tf_op jit(solution)/shard_map/ppermute | solution.py:26
  105.2 7.5 %collective-permute-start.25 = (bf16[3,48,128]{2,1,0:T(8,128)(2,1)S(1)}, bf16[3,48,128]{2,1,0:T(8,128)(2,1)S(1)}, u32[]{:S(2)}, u32[]{:S(2)}) collective-permute-start(bf16[3,48,128]{2,1,0:T(8,128)(2,1)S(1)} %get-tuple-element.78), channel_id=1, source_target_pairs={{0,8},{2,10},{4,12},{6,14},{8,0},{10,2},{12,4},{14,6},{1,9},{3,11}... | collective-permute-start | bytes 110600 | tf_op jit(solution)/shard_map/ppermute | solution.py:26
  106.9 5.8 %collective-permute-start.26 = (bf16[3,48,128]{2,1,0:T(8,128)(2,1)S(1)}, bf16[3,48,128]{2,1,0:T(8,128)(2,1)S(1)}, u32[]{:S(2)}, u32[]{:S(2)}) collective-permute-start(bf16[3,48,128]{2,1,0:T(8,128)(2,1)S(1)} %get-tuple-element.79), channel_id=1, source_target_pairs={{0,12},{2,14},{4,8},{6,10},{8,4},{10,6},{12,0},{14,2},{1,13},{3,15... | collective-permute-start | bytes 110600 | tf_op jit(solution)/shard_map/ppermute | solution.py:26
  112.7 5.4 %collective-permute-start.27 = (f32[2,48,128]{2,1,0:T(8,128)S(1)}, f32[2,48,128]{2,1,0:T(8,128)S(1)}, u32[]{:S(2)}, u32[]{:S(2)}) collective-permute-start(f32[2,48,128]{2,1,0:T(8,128)S(1)} %get-tuple-element.81), channel_id=1, source_target_pairs={{0,16},{16,0},{1,17},{17,1},{2,18},{18,2},{3,19},{19,3},{4,20},{20... | collective-permute-start | bytes 147464 | tf_op jit(solution)/shard_map/ppermute | solution.py:584

commit v5 on v4

--- a/solution.py
+++ b/solution.py
@@ -58,7 +58,7 @@
         row += count
 
 
-def join_kernel(own_ref, one_ref, two_ref, three_ref, rot_ref, low_ref, high_ref):
+def join_kernel(own_ref, one_ref, two_ref, three_ref, rot_ref, lists_ref, low_ref, high_ref):
     low_ref[0] = own_ref[...]
     low_ref[1] = one_ref[...]
     high_ref[0] = two_ref[...]
@@ -415,7 +415,7 @@
     row = jnp.concatenate([total[0:1], total[1:2]], axis=1)
     row = jnp.broadcast_to(row, (8, 2 * LANES))
     row = pltpu.roll(row, (2 * LANES - 12 * ref_ref[0]) % (2 * LANES), 1)
-    totals_ref[...] = row[0:1, :LANES]
+    totals_ref[...] = row[0, : totals_ref.shape[0]]
     for side, block in enumerate((low, high)):
         for g in range(GROUPS):
             start = side * SIDE + g * LANES
@@ -507,7 +507,11 @@
     )
     fours = [blocks] + [over(blocks, m, 1) for m in (1, 2, 3)]
     low, high = call(
-        "join", join_kernel, fours + [rots[1]], [shape(2, 8, 2, HALF, LANES)] * 2, [VMEM] * 4 + [ANY]
+        "join",
+        join_kernel,
+        fours + [rots[1], used_pair],
+        [shape(2, 8, 2, HALF, LANES)] * 2,
+        [VMEM] * 4 + [ANY] * 2,
     )
     one_low, three_high = over(low, 1, 0), over(high, 3, 0)
     one_high, three_low = over(high, 1, 0), over(low, 3, 0)
@@ -586,10 +590,10 @@
         "last",
         last_kernel,
         [core, ref, mine, came],
-        [shape(rdev, BLOCK, dtype=f32), shape(1, LANES, dtype=f32)],
+        [shape(rdev, BLOCK, dtype=f32), shape(rdev, dtype=f32)],
         [SMEM, SMEM, VMEM, VMEM],
     )
-    return (result, totals[0, :rdev], evidence[:, 0])
+    return (result, totals, evidence[:, 0])
 
 
 def solution(mesh):

time: 120 us -> 120 us (level)
    ppermute x1, waiting for transfers between devices: 0.09 us -> 2.18 us  [local(): theirs = lax.ppermute(scores, 'core', swap)]
    ppermute x1, waiting for transfers between devices: 1.8 us -> 0.01 us  [local(): used_pair = jnp.stack([used, lax.ppermute(used, 'core', swap)])]
    unnamed x12 -> x10, local copies, waits for them, and re-layouts: 4.44 us -> 5.12 us
  transfers between devices with their start and end apart: 28 -> 28, of which waited for: 18 -> 17; matrix products, arithmetic and copies ran while one was open for 1% -> 2% of each run, Pallas kernels for 8% -> 8%
where the time goes in v5:
time: 120 us
  waiting for transfers between devices  48.2 us (40%)
  starting transfers between devices  42.3 us (35%)
  Pallas kernels  22.1 us (18%)
  local copies, waits for them, and re-layouts  5.12 us (4%)
  other arithmetic  1.43 us (1%)
    ppermute x16, waiting for transfers between devices, over(): return lax.ppermute(value, ('y_lo', 'x', 'core', 'y_hi'), pairs)  38.1 us
    pallas_call x17, Pallas kernels, call(): pl.pallas_call(kernel, out_shape=outs, in_specs=specs or [VMEM] * len(ins...  22.1 us
    ppermute x8, starting transfers between devices, over_z(): return lax.ppermute(value, 'z', [(i, i ^ bits) for i in range(8)])  16.3 us
    ppermute x16, starting transfers between devices, over(): return lax.ppermute(value, ('y_lo', 'x', 'core', 'y_hi'), pairs)  15.8 us
    ppermute x8, waiting for transfers between devices, over_z(): return lax.ppermute(value, 'z', [(i, i ^ bits) for i in range(8)])  7.69 us
    unnamed x10, local copies, waits for them, and re-layouts  5.12 us
    ppermute x1, starting transfers between devices, local(): came = lax.ppermute(give, 'core', swap)  4.59 us
    ppermute x1, starting transfers between devices, local(): theirs = lax.ppermute(scores, 'core', swap)  2.76 us
  transfers between devices with their start and end apart: 28, of which 17 were waited for; matrix products, arithmetic and copies ran while one was open for 2% of the time, Pallas kernels for 8%

profile of v5, /device:TPU:1, one launch (start us, length us, event | category | flops | bytes accessed | tf_op | source)
XLA Modules:
  0.0 119.9 jit_solution(8366977668624509870)
XLA Ops:
  0.7 1.0 copy-done.2
  1.7 3.9 %collective-permute-start = (bf16[1,2,48,128]{3,2,1,0:T(8,128)(2,1)S(1)}, bf16[1,2,48,128]{3,2,1,0:T(8,128)(2,1)S(1)}, u32[]{:S(2)}, u32[]{:S(2)}) collective-permute-start(bf16[1,2,48,128]{3,2,1,0:T(8,128)(2,1)S(1)} %pack.1.before_ref.args_0_), channel_id=1, source_target_pairs={{0,4},{2,6},{4,0},{6,2},{8,12},{10,14},{12,8},{14,10},{1,5},{3,7},... | collective-permute-start | bytes 73736 | tf_op jit(solution)/shard_map/ppermute | solution.py:26
  5.6 5.1 %collective-permute-start.1 = (bf16[1,2,48,128]{3,2,1,0:T(8,128)(2,1)S(1)}, bf16[1,2,48,128]{3,2,1,0:T(8,128)(2,1)S(1)}, u32[]{:S(2)}, u32[]{:S(2)}) collective-permute-start(bf16[1,2,48,128]{3,2,1,0:T(8,128)(2,1)S(1)} %pack.1.before_ref.args_0_), channel_id=1, source_target_pairs={{0,8},{2,10},{4,12},{6,14},{8,0},{10,2},{12,4},{14,6},{1,9},{3,11}... | collective-permute-start | bytes 73736 | tf_op jit(solution)/shard_map/ppermute | solution.py:26
  10.7 1.4 %copy-done = bf16[48,16384]{1,0:T(8,128)(2,1)S(1)} copy-done((bf16[48,16384]{1,0:T(8,128)(2,1)S(1)}, bf16[48,16384]{1,0:T(8,128)(2,1)}, u32[]{:S(2)}) %copy-start) | copy-done | bytes 1572888
  12.1 1.1 copy-done.1
  13.3 0.3 weighted.1
  13.6 1.9 %collective-permute-done.2.args_3_ = bf16[1,2,48,128]{3,2,1,0:T(8,128)(2,1)S(1)} collective-permute-done((bf16[1,2,48,128]{3,2,1,0:T(8,128)(2,1)S(1)}, bf16[1,2,48,128]{3,2,1,0:T(8,128)(2,1)S(1)}, u32[]{:S(2)}, u32[]{:S(2)}) %collective-permute-start.2) | collective-permute-done | bytes 24608 | tf_op jit(solution)/shard_map/ppermute | solution.py:26
  15.5 0.1 hold.1
  15.6 2.5 %collective-permute-start.4 = (bf16[2,4,48,1024]{3,2,1,0:T(8,128)(2,1)S(1)}, bf16[2,4,48,1024]{3,2,1,0:T(8,128)(2,1)S(1)}, u32[]{:S(2)}, u32[]{:S(2)}) collective-permute-start(bf16[2,4,48,1024]{3,2,1,0:T(8,128)(2,1)S(1)} %hold.1), channel_id=1, source_target_pairs={{0,16},{16,0},{1,17},{17,1},{2,18},{18,2},{3,19},{19,3},{4,20},{20... | collective-permute-start | bytes 2359304 | tf_op jit(solution)/shard_map/ppermute | solution.py:484
  18.0 0.8 copy.22
  18.8 0.7 collective-permute-start.3
  19.6 0.7 fusion
  20.3 0.3 collective-permute-start.8
  20.6 0.8 copy.20.shifts_ref
  21.4 2.8 %rotate.2 = (bf16[2,2,864,1024]{3,2,1,0:T(8,128)(2,1)S(1)}, f32[2,9,1024]{2,1,0:T(8,128)S(1)}, f32[2,9,1024]{2,1,0:T(8,128)S(1)}) custom-call(s32[1]{0:T(128)} %bitcast.core_ref.args_0_, s32[1]{0:T(128)} %bitcast.6.x_ref, s32[1]{0:T(128)} %bitcast.2.part_ref.args_1_.y_lo_ref, s32[9,2]{1,0:T(8,128)S(1)} %copy.20.shifts_ref, ...), custom_call_target="tpu_custom_call" | custom-call | flops 3000000 | bytes 9000000 | tf_op jit(solution)/shard_map/rotate/pallas_call | solution.py:429
  24.2 1.3 %collective-permute-start.5 = (bf16[8,2,48,128]{3,2,1,0:T(8,128)(2,1)S(1)}, bf16[8,2,48,128]{3,2,1,0:T(8,128)(2,1)S(1)}, u32[]{:S(2)}, u32[]{:S(2)}) collective-permute-start(bf16[8,2,48,128]{3,2,1,0:T(8,128)(2,1)S(1)} %stack.15.own_ref), channel_id=1, source_target_pairs={{0,128},{1,129},{16,48},{17,49},{32,160},{33,161},{48,16},{49,17},... | collective-permute-start | bytes 589832 | tf_op jit(solution)/shard_map/ppermute | solution.py:41
  25.5 2.5 %collective-permute-start.6 = (bf16[8,2,48,128]{3,2,1,0:T(8,128)(2,1)S(1)}, bf16[8,2,48,128]{3,2,1,0:T(8,128)(2,1)S(1)}, u32[]{:S(2)}, u32[]{:S(2)}) collective-permute-start(bf16[8,2,48,128]{3,2,1,0:T(8,128)(2,1)S(1)} %stack.15.own_ref), channel_id=1, source_target_pairs={{0,1},{1,0},{16,80},{17,81},{32,33},{33,32},{48,112},{49,113},{64,... | collective-permute-start | bytes 589832 | tf_op jit(solution)/shard_map/ppermute | solution.py:41
  28.0 0.2 collective-permute-start.7
  28.2 0.1 fusion.1
  28.3 2.9 %rotate.3 = (bf16[2,2,864,1024]{3,2,1,0:T(8,128)(2,1)S(1)}, f32[4,9,1024]{2,1,0:T(8,128)S(1)}, f32[4,9,1024]{2,1,0:T(8,128)S(1)}) custom-call(s32[1]{0:T(128)} %bitcast.core_ref.args_0_, s32[1]{0:T(128)} %bitcast.6.x_ref, s32[1]{0:T(128)} %bitcast.2.part_ref.args_1_.y_lo_ref, s32[9,2]{1,0:T(8,128)S(1)} %copy.20.shifts_ref, ...), custom_call_target="tpu_custom_call" | custom-call | flops 3000000 | bytes 9000000 | tf_op jit(solution)/shard_map/rotate/pallas_call | solution.py:429
  31.2 2.3 %collective-permute-done.6.two_ref = bf16[8,2,48,128]{3,2,1,0:T(8,128)(2,1)S(1)} collective-permute-done((bf16[8,2,48,128]{3,2,1,0:T(8,128)(2,1)S(1)}, bf16[8,2,48,128]{3,2,1,0:T(8,128)(2,1)S(1)}, u32[]{:S(2)}, u32[]{:S(2)}) %collective-permute-start.6) | collective-permute-done | bytes 196640 | tf_op jit(solution)/shard_map/ppermute | solution.py:41
  33.5 2.1 %collective-permute-done.7.three_ref = bf16[8,2,48,128]{3,2,1,0:T(8,128)(2,1)S(1)} collective-permute-done((bf16[8,2,48,128]{3,2,1,0:T(8,128)(2,1)S(1)}, bf16[8,2,48,128]{3,2,1,0:T(8,128)(2,1)S(1)}, u32[]{:S(2)}, u32[]{:S(2)}) %collective-permute-start.7) | collective-permute-done | bytes 196640 | tf_op jit(solution)/shard_map/ppermute | solution.py:41
  35.6 0.1 join.1
  35.6 1.1 collective-permute-start.9
  36.7 1.9 %collective-permute-start.12 = (bf16[2,8,2,48,128]{4,3,2,1,0:T(8,128)(2,1)S(1)}, bf16[2,8,2,48,128]{4,3,2,1,0:T(8,128)(2,1)S(1)}, u32[]{:S(2)}, u32[]{:S(2)}) collective-permute-start(bf16[2,8,2,48,128]{4,3,2,1,0:T(8,128)(2,1)S(1)} %get-tuple-element.51.args_2_), channel_id=1, source_target_pairs={{0,96},{1,97},{16,145},{17,144},{32,64},{33,65},{48,177},{49,176},... | collective-permute-start | bytes 1179656 | tf_op jit(solution)/shard_map/ppermute | solution.py:41
  38.6 0.4 collective-permute-start.10
  39.0 0.6 collective-permute-start.14
  39.6 3.0 %collective-permute-done.9.args_3_ = bf16[2,8,2,48,128]{4,3,2,1,0:T(8,128)(2,1)S(1)} collective-permute-done((bf16[2,8,2,48,128]{4,3,2,1,0:T(8,128)(2,1)S(1)}, bf16[2,8,2,48,128]{4,3,2,1,0:T(8,128)(2,1)S(1)}, u32[]{:S(2)}, u32[]{:S(2)}) %collective-permute-start.9) | collective-permute-done | bytes 393248 | tf_op jit(solution)/shard_map/ppermute | solution.py:41
  42.6 2.4 %collective-permute-start.11 = (bf16[2,8,2,48,128]{4,3,2,1,0:T(8,128)(2,1)S(1)}, bf16[2,8,2,48,128]{4,3,2,1,0:T(8,128)(2,1)S(1)}, u32[]{:S(2)}, u32[]{:S(2)}) collective-permute-start(bf16[2,8,2,48,128]{4,3,2,1,0:T(8,128)(2,1)S(1)} %collective-permute-done.9.args_3_), channel_id=1, source_target_pairs={{0,96},{1,97},{16,145},{17,144},{32,64},{33,65},{48,177},{49,176},... | collective-permute-start | bytes 1179656 | tf_op jit(solution)/shard_map/ppermute | solution.py:41
  45.1 0.0 collective-permute-start.13
  45.1 1.8 %collective-permute-done.10.args_4_ = bf16[2,8,2,48,128]{4,3,2,1,0:T(8,128)(2,1)S(1)} collective-permute-done((bf16[2,8,2,48,128]{4,3,2,1,0:T(8,128)(2,1)S(1)}, bf16[2,8,2,48,128]{4,3,2,1,0:T(8,128)(2,1)S(1)}, u32[]{:S(2)}, u32[]{:S(2)}) %collective-permute-start.10) | collective-permute-done | bytes 393248 | tf_op jit(solution)/shard_map/ppermute | solution.py:41
  46.8 2.2 %collective-permute-done.14.args_7_ = bf16[2,8,2,48,128]{4,3,2,1,0:T(8,128)(2,1)S(1)} collective-permute-done((bf16[2,8,2,48,128]{4,3,2,1,0:T(8,128)(2,1)S(1)}, bf16[2,8,2,48,128]{4,3,2,1,0:T(8,128)(2,1)S(1)}, u32[]{:S(2)}, u32[]{:S(2)}) %collective-permute-start.14) | collective-permute-done | bytes 393248 | tf_op jit(solution)/shard_map/ppermute | solution.py:41
  49.1 4.2 %collective-permute-done.11.args_5_ = bf16[2,8,2,48,128]{4,3,2,1,0:T(8,128)(2,1)S(1)} collective-permute-done((bf16[2,8,2,48,128]{4,3,2,1,0:T(8,128)(2,1)S(1)}, bf16[2,8,2,48,128]{4,3,2,1,0:T(8,128)(2,1)S(1)}, u32[]{:S(2)}, u32[]{:S(2)}) %collective-permute-start.11) | collective-permute-done | bytes 393248 | tf_op jit(solution)/shard_map/ppermute | solution.py:41
  53.3 4.3 %forward.1.args_4_ = f32[864,256]{1,0:T(8,128)S(1)} custom-call(s32[1]{0:T(128)} %bitcast.core_ref.args_0_, bf16[2,8,2,48,128]{4,3,2,1,0:T(8,128)(2,1)S(1)} %get-tuple-element.50.args_1_, bf16[2,8,2,48,128]{4,3,2,1,0:T(8,128)(2,1)S(1)} %get-tuple-element.51.args_2_, bf16[2,8,2,48,128]{4,3,2,1,0:T(8,128)(2,1)S(1)} %collective-permute-done.9.args_3_, ...), custom_call_target="tpu_custom_call" | custom-call | flops 4000000 | bytes 12000000 | tf_op jit(solution)/shard_map/forward/pallas_call | solution.py:429
  57.5 2.8 %collective-permute-start.15 = (f32[864,256]{1,0:T(8,128)S(1)}, f32[864,256]{1,0:T(8,128)}, u32[]{:S(2)}, u32[]{:S(2)}) collective-permute-start(f32[864,256]{1,0:T(8,128)S(1)} %forward.1.args_4_), channel_id=1, source_target_pairs={{0,16},{16,0},{1,17},{17,1},{2,18},{18,2},{3,19},{19,3},{4,20},{20... | collective-permute-start | bytes 2654216 | tf_op jit(solution)/shard_map/ppermute | solution.py:531
  60.3 2.2 %collective-permute-done.15.args_5_ = f32[864,256]{1,0:T(8,128)} collective-permute-done((f32[864,256]{1,0:T(8,128)S(1)}, f32[864,256]{1,0:T(8,128)}, u32[]{:S(2)}, u32[]{:S(2)}) %collective-permute-start.15) | collective-permute-done | bytes 884768 | tf_op jit(solution)/shard_map/ppermute | solution.py:531
  62.5 6.2 %first.1 = (f32[4,8,2,48,128]{4,3,2,1,0:T(8,128)S(1)}, bf16[33,48,128]{2,1,0:T(8,128)(2,1)S(1)}, bf16[33,48,128]{2,1,0:T(8,128)(2,1)S(1)}, bf16[192,864]{1,0:T(8...) custom-call(s32[1]{0:T(128)} %bitcast.core_ref.args_0_, s32[1]{0:T(128)} %bitcast.2.part_ref.args_1_.y_lo_ref, ...), custom_call_target="tpu_custom_call" | custom-call | flops 6000000 | bytes 18000000 | tf_op jit(solution)/shard_map/first/pallas_call | solution.py:429
  68.7 0.1 collective-permute-start.16
  68.8 0.5 collective-permute-start.17
  69.4 4.1 %second.1 = (bf16[32,48,128]{2,1,0:T(8,128)(2,1)S(1)}, f32[32,48,128]{2,1,0:T(8,128)S(1)}, f32[32,48,128]{2,1,0:T(8,128)S(1)}, bf16[32,48,128]{2,1,0:T(8,128)(2,1)S(1)}) custom-call(s32[1]{0:T(128)} %bitcast.core_ref.args_0_, s32[1]{0:T(128)} %bitcast.2.part_ref.args_1_.y_lo_ref, bf16[192,864]{1,0:T(8,128)(2,1)S(1)} %get-tuple-element.55.flipped_ref, ...), custom_call_target="tpu_custom_call" | custom-call | flops 4000000 | bytes 12000000 | tf_op jit(solution)/shard_map/second/pallas_call | solution.py:429
  73.5 2.4 %collective-permute-done.16.args_5_ = bf16[33,48,128]{2,1,0:T(8,128)(2,1)S(1)} collective-permute-done((bf16[33,48,128]{2,1,0:T(8,128)(2,1)S(1)}, bf16[33,48,128]{2,1,0:T(8,128)(2,1)S(1)}, u32[]{:S(2)}, u32[]{:S(2)}) %collective-permute-start.16) | collective-permute-done | bytes 405536 | tf_op jit(solution)/shard_map/ppermute | solution.py:41
  75.9 1.3 %collective-permute-done.17.args_6_ = bf16[33,48,128]{2,1,0:T(8,128)(2,1)S(1)} collective-permute-done((bf16[33,48,128]{2,1,0:T(8,128)(2,1)S(1)}, bf16[33,48,128]{2,1,0:T(8,128)(2,1)S(1)}, u32[]{:S(2)}, u32[]{:S(2)}) %collective-permute-start.17) | collective-permute-done | bytes 405536 | tf_op jit(solution)/shard_map/ppermute | solution.py:41
  77.2 0.2 add.12
  77.4 0.2 collective-permute-start.18
  77.6 0.6 collective-permute-start.19
  78.2 11.7 %collective-permute-done.19.three = bf16[64,48,128]{2,1,0:T(8,128)(2,1)S(1)} collective-permute-done((bf16[64,48,128]{2,1,0:T(8,128)(2,1)S(1)}, bf16[64,48,128]{2,1,0:T(8,128)(2,1)S(1)}, u32[]{:S(2)}, u32[]{:S(2)}) %collective-permute-start.19) | collective-permute-done | bytes 786464 | tf_op jit(solution)/shard_map/ppermute | solution.py:41
  90.0 0.3 middle.1
  90.3 0.1 collective-permute-start.20
  90.4 3.0 %collective-permute-start.21 = (bf16[17,48,128]{2,1,0:T(8,128)(2,1)S(1)}, bf16[17,48,128]{2,1,0:T(8,128)(2,1)S(1)}, u32[]{:S(2)}, u32[]{:S(2)}) collective-permute-start(bf16[17,48,128]{2,1,0:T(8,128)(2,1)S(1)} %get-tuple-element.70), channel_id=1, source_target_pairs={{0,1},{1,0},{16,80},{17,81},{32,33},{33,32},{48,112},{49,113},{64,... | collective-permute-start | bytes 626696 | tf_op jit(solution)/shard_map/ppermute | solution.py:41
  93.4 0.9 collective-permute-start.22
  94.2 0.8 collective-permute-done.20.one
  95.0 4.1 %collective-permute-done.21.two = bf16[17,48,128]{2,1,0:T(8,128)(2,1)S(1)} collective-permute-done((bf16[17,48,128]{2,1,0:T(8,128)(2,1)S(1)}, bf16[17,48,128]{2,1,0:T(8,128)(2,1)S(1)}, u32[]{:S(2)}, u32[]{:S(2)}) %collective-permute-start.21) | collective-permute-done | bytes 208928 | tf_op jit(solution)/shard_map/ppermute | solution.py:41
  99.1 2.2 %collective-permute-done.22.three = bf16[17,48,128]{2,1,0:T(8,128)(2,1)S(1)} collective-permute-done((bf16[17,48,128]{2,1,0:T(8,128)(2,1)S(1)}, bf16[17,48,128]{2,1,0:T(8,128)(2,1)S(1)}, u32[]{:S(2)}, u32[]{:S(2)}) %collective-permute-start.22) | collective-permute-done | bytes 208928 | tf_op jit(solution)/shard_map/ppermute | solution.py:41
  101.3 0.1 late.1
  101.4 0.8 collective-permute-start.23
  102.2 2.9 %collective-permute-done.23.came = bf16[9,48,128]{2,1,0:T(8,128)(2,1)S(1)} collective-permute-done((bf16[9,48,128]{2,1,0:T(8,128)(2,1)S(1)}, bf16[9,48,128]{2,1,0:T(8,128)(2,1)S(1)}, u32[]{:S(2)}, u32[]{:S(2)}) %collective-permute-start.23) | collective-permute-done | bytes 110624 | tf_op jit(solution)/shard_map/ppermute | solution.py:26
  105.1 1.3 %collective-permute-start.24 = (bf16[3,48,128]{2,1,0:T(8,128)(2,1)S(1)}, bf16[3,48,128]{2,1,0:T(8,128)(2,1)S(1)}, u32[]{:S(2)}, u32[]{:S(2)}) collective-permute-start(bf16[3,48,128]{2,1,0:T(8,128)(2,1)S(1)} %get-tuple-element.77), channel_id=1, source_target_pairs={{0,4},{2,6},{4,0},{6,2},{8,12},{10,14},{12,8},{14,10},{1,5},{3,7},... | collective-permute-start | bytes 110600 | tf_op jit(solution)/shard_map/ppermute | solution.py:26
  106.4 1.8 %collective-permute-start.25 = (bf16[3,48,128]{2,1,0:T(8,128)(2,1)S(1)}, bf16[3,48,128]{2,1,0:T(8,128)(2,1)S(1)}, u32[]{:S(2)}, u32[]{:S(2)}) collective-permute-start(bf16[3,48,128]{2,1,0:T(8,128)(2,1)S(1)} %get-tuple-element.78), channel_id=1, source_target_pairs={{0,8},{2,10},{4,12},{6,14},{8,0},{10,2},{12,4},{14,6},{1,9},{3,11}... | collective-permute-start | bytes 110600 | tf_op jit(solution)/shard_map/ppermute | solution.py:26
  108.2 2.7 %collective-permute-start.26 = (bf16[3,48,128]{2,1,0:T(8,128)(2,1)S(1)}, bf16[3,48,128]{2,1,0:T(8,128)(2,1)S(1)}, u32[]{:S(2)}, u32[]{:S(2)}) collective-permute-start(bf16[3,48,128]{2,1,0:T(8,128)(2,1)S(1)} %get-tuple-element.79), channel_id=1, source_target_pairs={{0,12},{2,14},{4,8},{6,10},{8,4},{10,6},{12,0},{14,2},{1,13},{3,15... | collective-permute-start | bytes 110600 | tf_op jit(solution)/shard_map/ppermute | solution.py:26
  110.9 2.9 %collective-permute-done.25.four = bf16[3,48,128]{2,1,0:T(8,128)(2,1)S(1)} collective-permute-done((bf16[3,48,128]{2,1,0:T(8,128)(2,1)S(1)}, bf16[3,48,128]{2,1,0:T(8,128)(2,1)S(1)}, u32[]{:S(2)}, u32[]{:S(2)}) %collective-permute-start.25) | collective-permute-done | bytes 36896 | tf_op jit(solution)/shard_map/ppermute | solution.py:26
  113.8 4.6 %collective-permute-start.27 = (f32[2,48,128]{2,1,0:T(8,128)S(1)}, f32[2,48,128]{2,1,0:T(8,128)S(1)}, u32[]{:S(2)}, u32[]{:S(2)}) collective-permute-start(f32[2,48,128]{2,1,0:T(8,128)S(1)} %get-tuple-element.81), channel_id=1, source_target_pairs={{0,16},{16,0},{1,17},{17,1},{2,18},{18,2},{3,19},{19,3},{4,20},{20... | collective-permute-start | bytes 147464 | tf_op jit(solution)/shard_map/ppermute | solution.py:588
  118.4 0.6 reduce
  119.0 0.3 collective-permute-done.27.came_ref
  119.3 0.6 last.1
  (23 shorter events, 0.1 us)
Async XLA Ops:
  0.6 1.0 copy-start.2
  1.7 11.9 %collective-permute-start = (bf16[1,2,48,128]{3,2,1,0:T(8,128)(2,1)S(1)}, bf16[1,2,48,128]{3,2,1,0:T(8,128)(2,1)S(1)}, u32[]{:S(2)}, u32[]{:S(2)}) collective-permute-start(bf16[1,2,48,128]{3,2,1,0:T(8,128)(2,1)S(1)} %pack.1.before_ref.args_0_), channel_id=1, source_target_pairs={{0,4},{2,6},{4,0},{6,2},{8,12},{10,14},{12,8},{14,10},{1,5},{3,7},... | collective-permute-start | bytes 73736 | tf_op jit(solution)/shard_map/ppermute | solution.py:26
  5.6 8.0 %collective-permute-start.1 = (bf16[1,2,48,128]{3,2,1,0:T(8,128)(2,1)S(1)}, bf16[1,2,48,128]{3,2,1,0:T(8,128)(2,1)S(1)}, u32[]{:S(2)}, u32[]{:S(2)}) collective-permute-start(bf16[1,2,48,128]{3,2,1,0:T(8,128)(2,1)S(1)} %pack.1.before_ref.args_0_), channel_id=1, source_target_pairs={{0,8},{2,10},{4,12},{6,14},{8,0},{10,2},{12,4},{14,6},{1,9},{3,11}... | collective-permute-start | bytes 73736 | tf_op jit(solution)/shard_map/ppermute | solution.py:26
  10.7 4.8 %collective-permute-start.2 = (bf16[1,2,48,128]{3,2,1,0:T(8,128)(2,1)S(1)}, bf16[1,2,48,128]{3,2,1,0:T(8,128)(2,1)S(1)}, u32[]{:S(2)}, u32[]{:S(2)}) collective-permute-start(bf16[1,2,48,128]{3,2,1,0:T(8,128)(2,1)S(1)} %pack.1.before_ref.args_0_), channel_id=1, source_target_pairs={{0,12},{2,14},{4,8},{6,10},{8,4},{10,6},{12,0},{14,2},{1,13},{3,15... | collective-permute-start | bytes 73736 | tf_op jit(solution)/shard_map/ppermute | solution.py:26
  10.7 1.4 %copy-start = (bf16[48,16384]{1,0:T(8,128)(2,1)S(1)}, bf16[48,16384]{1,0:T(8,128)(2,1)}, u32[]{:S(2)}) copy-start(bf16[48,16384]{1,0:T(8,128)(2,1)} %images_ref.1) | copy-start | bytes 4718596
  12.1 1.1 copy-start.1
  13.3 14.9 %copy-start.3 = (s32[48]{0:T(128)S(1)}, s32[48]{0:T(128)}, u32[]{:S(2)}) copy-start(s32[48]{0:T(128)} %param.11) | copy-start | bytes 580
  15.6 5.8 %collective-permute-start.4 = (bf16[2,4,48,1024]{3,2,1,0:T(8,128)(2,1)S(1)}, bf16[2,4,48,1024]{3,2,1,0:T(8,128)(2,1)S(1)}, u32[]{:S(2)}, u32[]{:S(2)}) collective-permute-start(bf16[2,4,48,1024]{3,2,1,0:T(8,128)(2,1)S(1)} %hold.1), channel_id=1, source_target_pairs={{0,16},{16,0},{1,17},{17,1},{2,18},{18,2},{3,19},{19,3},{4,20},{20... | collective-permute-start | bytes 2359304 | tf_op jit(solution)/shard_map/ppermute | solution.py:484
  18.8 5.4 %collective-permute-start.3 = (bf16[4,2,48,128]{3,2,1,0:T(8,128)(2,1)S(1)}, bf16[4,2,48,128]{3,2,1,0:T(8,128)(2,1)S(1)}, u32[]{:S(2)}, u32[]{:S(2)}) collective-permute-start(bf16[4,2,48,128]{3,2,1,0:T(8,128)(2,1)S(1)} %stack.14.args_1_.args_0_), channel_id=1, source_target_pairs={{0,2},{2,0},{4,6},{6,4},{8,10},{10,8},{12,14},{14,12},{1,3},{3,1},... | collective-permute-start | bytes 294920 | tf_op jit(solution)/shard_map/ppermute | solution.py:26
  20.3 8.0 %collective-permute-start.8 = (s32[48,12]{1,0:T(8,128)S(1)}, s32[48,12]{1,0:T(8,128)S(1)}, u32[]{:S(2)}, u32[]{:S(2)}) collective-permute-start(s32[48,12]{1,0:T(8,128)S(1)} %fusion), channel_id=1, source_target_pairs={{0,16},{16,0},{1,17},{17,1},{2,18},{18,2},{3,19},{19,3},{4,20},{20... | collective-permute-start | bytes 6920 | tf_op jit(solution)/shard_map/ppermute | solution.py:487
  24.2 6.9 %collective-permute-start.5 = (bf16[8,2,48,128]{3,2,1,0:T(8,128)(2,1)S(1)}, bf16[8,2,48,128]{3,2,1,0:T(8,128)(2,1)S(1)}, u32[]{:S(2)}, u32[]{:S(2)}) collective-permute-start(bf16[8,2,48,128]{3,2,1,0:T(8,128)(2,1)S(1)} %stack.15.own_ref), channel_id=1, source_target_pairs={{0,128},{1,129},{16,48},{17,49},{32,160},{33,161},{48,16},{49,17},... | collective-permute-start | bytes 589832 | tf_op jit(solution)/shard_map/ppermute | solution.py:41
  25.5 7.9 %collective-permute-start.6 = (bf16[8,2,48,128]{3,2,1,0:T(8,128)(2,1)S(1)}, bf16[8,2,48,128]{3,2,1,0:T(8,128)(2,1)S(1)}, u32[]{:S(2)}, u32[]{:S(2)}) collective-permute-start(bf16[8,2,48,128]{3,2,1,0:T(8,128)(2,1)S(1)} %stack.15.own_ref), channel_id=1, source_target_pairs={{0,1},{1,0},{16,80},{17,81},{32,33},{33,32},{48,112},{49,113},{64,... | collective-permute-start | bytes 589832 | tf_op jit(solution)/shard_map/ppermute | solution.py:41
  28.0 7.6 %collective-permute-start.7 = (bf16[8,2,48,128]{3,2,1,0:T(8,128)(2,1)S(1)}, bf16[8,2,48,128]{3,2,1,0:T(8,128)(2,1)S(1)}, u32[]{:S(2)}, u32[]{:S(2)}) collective-permute-start(bf16[8,2,48,128]{3,2,1,0:T(8,128)(2,1)S(1)} %stack.15.own_ref), channel_id=1, source_target_pairs={{0,129},{1,128},{16,112},{17,113},{32,161},{33,160},{48,80},{49,81... | collective-permute-start | bytes 589832 | tf_op jit(solution)/shard_map/ppermute | solution.py:41
  35.6 7.0 %collective-permute-start.9 = (bf16[2,8,2,48,128]{4,3,2,1,0:T(8,128)(2,1)S(1)}, bf16[2,8,2,48,128]{4,3,2,1,0:T(8,128)(2,1)S(1)}, u32[]{:S(2)}, u32[]{:S(2)}) collective-permute-start(bf16[2,8,2,48,128]{4,3,2,1,0:T(8,128)(2,1)S(1)} %get-tuple-element.50.args_1_), channel_id=1, source_target_pairs={{0,32},{1,33},{16,144},{17,145},{32,0},{33,1},{48,176},{49,177},{6... | collective-permute-start | bytes 1179656 | tf_op jit(solution)/shard_map/ppermute | solution.py:41
  36.7 8.4 %collective-permute-start.12 = (bf16[2,8,2,48,128]{4,3,2,1,0:T(8,128)(2,1)S(1)}, bf16[2,8,2,48,128]{4,3,2,1,0:T(8,128)(2,1)S(1)}, u32[]{:S(2)}, u32[]{:S(2)}) collective-permute-start(bf16[2,8,2,48,128]{4,3,2,1,0:T(8,128)(2,1)S(1)} %get-tuple-element.51.args_2_), channel_id=1, source_target_pairs={{0,96},{1,97},{16,145},{17,144},{32,64},{33,65},{48,177},{49,176},... | collective-permute-start | bytes 1179656 | tf_op jit(solution)/shard_map/ppermute | solution.py:41
  38.6 8.2 %collective-permute-start.10 = (bf16[2,8,2,48,128]{4,3,2,1,0:T(8,128)(2,1)S(1)}, bf16[2,8,2,48,128]{4,3,2,1,0:T(8,128)(2,1)S(1)}, u32[]{:S(2)}, u32[]{:S(2)}) collective-permute-start(bf16[2,8,2,48,128]{4,3,2,1,0:T(8,128)(2,1)S(1)} %get-tuple-element.51.args_2_), channel_id=1, source_target_pairs={{0,32},{1,33},{16,144},{17,145},{32,0},{33,1},{48,176},{49,177},{6... | collective-permute-start | bytes 1179656 | tf_op jit(solution)/shard_map/ppermute | solution.py:41
  39.0 10.0 %collective-permute-start.14 = (bf16[2,8,2,48,128]{4,3,2,1,0:T(8,128)(2,1)S(1)}, bf16[2,8,2,48,128]{4,3,2,1,0:T(8,128)(2,1)S(1)}, u32[]{:S(2)}, u32[]{:S(2)}) collective-permute-start(bf16[2,8,2,48,128]{4,3,2,1,0:T(8,128)(2,1)S(1)} %get-tuple-element.50.args_1_), channel_id=1, source_target_pairs={{0,96},{1,97},{16,145},{17,144},{32,64},{33,65},{48,177},{49,176},... | collective-permute-start | bytes 1179656 | tf_op jit(solution)/shard_map/ppermute | solution.py:41
  42.6 10.6 %collective-permute-start.11 = (bf16[2,8,2,48,128]{4,3,2,1,0:T(8,128)(2,1)S(1)}, bf16[2,8,2,48,128]{4,3,2,1,0:T(8,128)(2,1)S(1)}, u32[]{:S(2)}, u32[]{:S(2)}) collective-permute-start(bf16[2,8,2,48,128]{4,3,2,1,0:T(8,128)(2,1)S(1)} %collective-permute-done.9.args_3_), channel_id=1, source_target_pairs={{0,96},{1,97},{16,145},{17,144},{32,64},{33,65},{48,177},{49,176},... | collective-permute-start | bytes 1179656 | tf_op jit(solution)/shard_map/ppermute | solution.py:41
  45.1 8.2 %collective-permute-start.13 = (bf16[2,8,2,48,128]{4,3,2,1,0:T(8,128)(2,1)S(1)}, bf16[2,8,2,48,128]{4,3,2,1,0:T(8,128)(2,1)S(1)}, u32[]{:S(2)}, u32[]{:S(2)}) collective-permute-start(bf16[2,8,2,48,128]{4,3,2,1,0:T(8,128)(2,1)S(1)} %collective-permute-done.12.args_8_), channel_id=1, source_target_pairs={{0,32},{1,33},{16,144},{17,145},{32,0},{33,1},{48,176},{49,177},{6... | collective-permute-start | bytes 1179656 | tf_op jit(solution)/shard_map/ppermute | solution.py:41
  57.5 4.9 %collective-permute-start.15 = (f32[864,256]{1,0:T(8,128)S(1)}, f32[864,256]{1,0:T(8,128)}, u32[]{:S(2)}, u32[]{:S(2)}) collective-permute-start(f32[864,256]{1,0:T(8,128)S(1)} %forward.1.args_4_), channel_id=1, source_target_pairs={{0,16},{16,0},{1,17},{17,1},{2,18},{18,2},{3,19},{19,3},{4,20},{20... | collective-permute-start | bytes 2654216 | tf_op jit(solution)/shard_map/ppermute | solution.py:531
  68.7 7.1 %collective-permute-start.16 = (bf16[33,48,128]{2,1,0:T(8,128)(2,1)S(1)}, bf16[33,48,128]{2,1,0:T(8,128)(2,1)S(1)}, u32[]{:S(2)}, u32[]{:S(2)}) collective-permute-start(bf16[33,48,128]{2,1,0:T(8,128)(2,1)S(1)} %get-tuple-element.60), channel_id=1, source_target_pairs={{0,32},{1,33},{16,144},{17,145},{32,0},{33,1},{48,176},{49,177},{6... | collective-permute-start | bytes 1216520 | tf_op jit(solution)/shard_map/ppermute | solution.py:41
  68.8 8.4 %collective-permute-start.17 = (bf16[33,48,128]{2,1,0:T(8,128)(2,1)S(1)}, bf16[33,48,128]{2,1,0:T(8,128)(2,1)S(1)}, u32[]{:S(2)}, u32[]{:S(2)}) collective-permute-start(bf16[33,48,128]{2,1,0:T(8,128)(2,1)S(1)} %get-tuple-element.61), channel_id=1, source_target_pairs={{0,96},{1,97},{16,145},{17,144},{32,64},{33,65},{48,177},{49,176},... | collective-permute-start | bytes 1216520 | tf_op jit(solution)/shard_map/ppermute | solution.py:41
  77.4 12.6 %collective-permute-start.18 = (bf16[65,48,128]{2,1,0:T(8,128)(2,1)S(1)}, bf16[65,48,128]{2,1,0:T(8,128)(2,1)S(1)}, u32[]{:S(2)}, u32[]{:S(2)}) collective-permute-start(bf16[65,48,128]{2,1,0:T(8,128)(2,1)S(1)} %get-tuple-element.65), channel_id=1, source_target_pairs={{0,32},{1,33},{16,144},{17,145},{32,0},{33,1},{48,176},{49,177},{6... | collective-permute-start | bytes 2396168 | tf_op jit(solution)/shard_map/ppermute | solution.py:41
  77.6 12.3 %collective-permute-start.19 = (bf16[64,48,128]{2,1,0:T(8,128)(2,1)S(1)}, bf16[64,48,128]{2,1,0:T(8,128)(2,1)S(1)}, u32[]{:S(2)}, u32[]{:S(2)}) collective-permute-start(bf16[64,48,128]{2,1,0:T(8,128)(2,1)S(1)} %get-tuple-element.66), channel_id=1, source_target_pairs={{0,96},{1,97},{16,145},{17,144},{32,64},{33,65},{48,177},{49,176},... | collective-permute-start | bytes 2359304 | tf_op jit(solution)/shard_map/ppermute | solution.py:41
  90.3 4.7 %collective-permute-start.20 = (bf16[17,48,128]{2,1,0:T(8,128)(2,1)S(1)}, bf16[17,48,128]{2,1,0:T(8,128)(2,1)S(1)}, u32[]{:S(2)}, u32[]{:S(2)}) collective-permute-start(bf16[17,48,128]{2,1,0:T(8,128)(2,1)S(1)} %get-tuple-element.69), channel_id=1, source_target_pairs={{0,128},{1,129},{16,48},{17,49},{32,160},{33,161},{48,16},{49,17},... | collective-permute-start | bytes 626696 | tf_op jit(solution)/shard_map/ppermute | solution.py:41
  90.4 8.7 %collective-permute-start.21 = (bf16[17,48,128]{2,1,0:T(8,128)(2,1)S(1)}, bf16[17,48,128]{2,1,0:T(8,128)(2,1)S(1)}, u32[]{:S(2)}, u32[]{:S(2)}) collective-permute-start(bf16[17,48,128]{2,1,0:T(8,128)(2,1)S(1)} %get-tuple-element.70), channel_id=1, source_target_pairs={{0,1},{1,0},{16,80},{17,81},{32,33},{33,32},{48,112},{49,113},{64,... | collective-permute-start | bytes 626696 | tf_op jit(solution)/shard_map/ppermute | solution.py:41
  93.4 8.0 %collective-permute-start.22 = (bf16[17,48,128]{2,1,0:T(8,128)(2,1)S(1)}, bf16[17,48,128]{2,1,0:T(8,128)(2,1)S(1)}, u32[]{:S(2)}, u32[]{:S(2)}) collective-permute-start(bf16[17,48,128]{2,1,0:T(8,128)(2,1)S(1)} %get-tuple-element.71), channel_id=1, source_target_pairs={{0,129},{1,128},{16,112},{17,113},{32,161},{33,160},{48,80},{49,81... | collective-permute-start | bytes 626696 | tf_op jit(solution)/shard_map/ppermute | solution.py:41
  101.4 3.7 %collective-permute-start.23 = (bf16[9,48,128]{2,1,0:T(8,128)(2,1)S(1)}, bf16[9,48,128]{2,1,0:T(8,128)(2,1)S(1)}, u32[]{:S(2)}, u32[]{:S(2)}) collective-permute-start(bf16[9,48,128]{2,1,0:T(8,128)(2,1)S(1)} %get-tuple-element.74), channel_id=1, source_target_pairs={{0,2},{2,0},{4,6},{6,4},{8,10},{10,8},{12,14},{14,12},{1,3},{3,1},... | collective-permute-start | bytes 331784 | tf_op jit(solution)/shard_map/ppermute | solution.py:26
  105.1 5.7 %collective-permute-start.24 = (bf16[3,48,128]{2,1,0:T(8,128)(2,1)S(1)}, bf16[3,48,128]{2,1,0:T(8,128)(2,1)S(1)}, u32[]{:S(2)}, u32[]{:S(2)}) collective-permute-start(bf16[3,48,128]{2,1,0:T(8,128)(2,1)S(1)} %get-tuple-element.77), channel_id=1, source_target_pairs={{0,4},{2,6},{4,0},{6,2},{8,12},{10,14},{12,8},{14,10},{1,5},{3,7},... | collective-permute-start | bytes 110600 | tf_op jit(solution)/shard_map/ppermute | solution.py:26
  106.4 7.4 %collective-permute-start.25 = (bf16[3,48,128]{2,1,0:T(8,128)(2,1)S(1)}, bf16[3,48,128]{2,1,0:T(8,128)(2,1)S(1)}, u32[]{:S(2)}, u32[]{:S(2)}) collective-permute-start(bf16[3,48,128]{2,1,0:T(8,128)(2,1)S(1)} %get-tuple-element.78), channel_id=1, source_target_pairs={{0,8},{2,10},{4,12},{6,14},{8,0},{10,2},{12,4},{14,6},{1,9},{3,11}... | collective-permute-start | bytes 110600 | tf_op jit(solution)/shard_map/ppermute | solution.py:26
  108.2 5.6 %collective-permute-start.26 = (bf16[3,48,128]{2,1,0:T(8,128)(2,1)S(1)}, bf16[3,48,128]{2,1,0:T(8,128)(2,1)S(1)}, u32[]{:S(2)}, u32[]{:S(2)}) collective-permute-start(bf16[3,48,128]{2,1,0:T(8,128)(2,1)S(1)} %get-tuple-element.79), channel_id=1, source_target_pairs={{0,12},{2,14},{4,8},{6,10},{8,4},{10,6},{12,0},{14,2},{1,13},{3,15... | collective-permute-start | bytes 110600 | tf_op jit(solution)/shard_map/ppermute | solution.py:26
  113.8 5.5 %collective-permute-start.27 = (f32[2,48,128]{2,1,0:T(8,128)S(1)}, f32[2,48,128]{2,1,0:T(8,128)S(1)}, u32[]{:S(2)}, u32[]{:S(2)}) collective-permute-start(f32[2,48,128]{2,1,0:T(8,128)S(1)} %get-tuple-element.81), channel_id=1, source_target_pairs={{0,16},{16,0},{1,17},{17,1},{2,18},{18,2},{3,19},{19,3},{4,20},{20... | collective-permute-start | bytes 147464 | tf_op jit(solution)/shard_map/ppermute | solution.py:588
